TPU v7x, 128 devices: a whole 4x4x4 slice. The times are simulated.
128 devices in a mesh: section: 2 (over core), ctx: 16 (over z, x), fsdp: 4 (over y).
Axes of the slice: x: 4, y: 4, z: 4, core: 2. Of those that a mesh axis runs over, the one named last changes fastest.
Arguments:
- tokens: bfloat16 [8, 1024, 768], P('fsdp', 'ctx'), may hold values from -6 to 6
- cotangent: float32 [8, 1024, 768], P('fsdp', 'ctx'), may hold values from -6 to 6
- block_order: int32 [32], replicated, may hold values from 0 to 31, as said below
- first_gain: bfloat16 [2, 768], P('section', 'fsdp'), may hold values from 0.5 to 1.5
- first_shift: bfloat16 [2, 768], P('section', 'fsdp'), may hold values from -1.25 to 1.25
- w_query: bfloat16 [2, 768, 768], P('section', 'fsdp'), may hold values from -0.21875 to 0.21875
- b_query: bfloat16 [2, 768], P('section', 'fsdp'), may hold values from -1.25 to 1.25
- w_key: bfloat16 [2, 768, 768], P('section', 'fsdp'), may hold values from -0.21875 to 0.21875
- w_value: bfloat16 [2, 768, 768], P('section', 'fsdp'), may hold values from -0.21875 to 0.21875
- b_value: bfloat16 [2, 768], P('section', 'fsdp'), may hold values from -1.25 to 1.25
- w_out: bfloat16 [2, 768, 768], P('section', 'fsdp'), may hold values from -3.5 to 3.5
- b_out: bfloat16 [2, 768], P('section', 'fsdp'), may hold values from -1.25 to 1.25
- second_gain: bfloat16 [2, 768], P('section', 'fsdp'), may hold values from 0.5 to 1.5
- second_shift: bfloat16 [2, 768], P('section', 'fsdp'), may hold values from -1.25 to 1.25
- w_expand: bfloat16 [2, 768, 3072], P('section', 'fsdp'), may hold values from -0.21875 to 0.21875
- b_expand: bfloat16 [2, 3072], P('section', 'fsdp'), may hold values from -1.25 to 1.25
- w_reduce: bfloat16 [2, 3072, 768], P('section', 'fsdp'), may hold values from -0.21875 to 0.21875
- b_reduce: bfloat16 [2, 768], P('section', 'fsdp'), may hold values from -1.25 to 1.25
Outputs:
- layer_outputs: bfloat16 [2, 8, 1024, 768], P('section', 'fsdp', 'ctx')
- input_grads: float32 [2, 8, 1024, 768], P('section', 'fsdp', 'ctx')
- grad_first_gain: float32 [2, 768], P('section', 'fsdp')
- grad_first_shift: float32 [2, 768], P('section', 'fsdp')
- grad_w_query: float32 [2, 768, 768], P('section', 'fsdp')
- grad_b_query: float32 [2, 768], P('section', 'fsdp')
- grad_w_key: float32 [2, 768, 768], P('section', 'fsdp')
- grad_w_value: float32 [2, 768, 768], P('section', 'fsdp')
- grad_b_value: float32 [2, 768], P('section', 'fsdp')
- grad_w_out: float32 [2, 768, 768], P('section', 'fsdp')
- grad_b_out: float32 [2, 768], P('section', 'fsdp')
- grad_second_gain: float32 [2, 768], P('section', 'fsdp')
- grad_second_shift: float32 [2, 768], P('section', 'fsdp')
- grad_w_expand: float32 [2, 768, 3072], P('section', 'fsdp')
- grad_b_expand: float32 [2, 3072], P('section', 'fsdp')
- grad_w_reduce: float32 [2, 3072, 768], P('section', 'fsdp')
- grad_b_reduce: float32 [2, 768], P('section', 'fsdp')
Inputs may be any that keep to these rules, and one draw needn't show every extreme that they name: `block_order`: a permutation of 0 to 31 in which entries 2c and 2c + 1 are b and 31 - b for some b, for every c.
All inputs are finite; a program needn't handle non-finite values.
Results may differ from a plain program's by a relative error of at most 0.025.
Values may be sent and summed in bfloat16 or wider, within the bound.
A program may use at most 192 MiB of HBM per device.

v0:
```python
import jax
import jax.numpy as jnp
from jax import lax
from jax.sharding import PartitionSpec as P

H = 12
HEAD = 64


EPSILON = 1e-05


def from_behind(block, axis, distance):
    devices = range(lax.axis_size(axis))
    route = [(i - distance, i) for i in devices if i - distance in devices]
    return lax.ppermute(block, axis, route)


def layer_norm(values, gain, shift):
    average = jnp.mean(values, axis=-1, keepdims=True)
    centered = values - average
    variance = jnp.mean(centered * centered, axis=-1, keepdims=True)
    return centered * lax.rsqrt(variance + EPSILON) * gain + shift


def matmul(left, right):
    return jnp.dot(left, right, preferred_element_type=jnp.float32)


def transposed_left(left, right):
    return lax.dot_general(
        left, right, (((0,), (0,)), ((), ())), preferred_element_type=jnp.float32
    )


def transposed_right(left, right):
    return lax.dot_general(
        left, right, (((1,), (1,)), ((), ())), preferred_element_type=jnp.float32
    )


def column_sums(values):
    return jnp.sum(values.astype(jnp.float32), axis=0)


def attention_scores(query, all_keys, query_pos, key_pos):
    rows = query.shape[0]
    length = all_keys.shape[0]
    scores = jnp.einsum(
        "rhd,lhd->hrl",
        query.reshape(rows, H, HEAD),
        all_keys.reshape(length, H, HEAD),
        preferred_element_type=jnp.float32,
    )
    allowed = key_pos[None, None, :] <= query_pos[None, :, None]
    return jnp.where(allowed, scores, -1e30)


def forward(inputs, weights, query_pos, key_pos):
    (
        first_gain,
        first_shift,
        w_query,
        b_query,
        w_key,
        w_value,
        b_value,
        w_out,
        b_out,
        second_gain,
        second_shift,
        w_expand,
        b_expand,
        w_reduce,
        b_reduce,
    ) = weights
    start = inputs.astype(jnp.float32)
    normed = layer_norm(
        start, first_gain.astype(jnp.float32), first_shift.astype(jnp.float32)
    ).astype(jnp.bfloat16)
    query = ((matmul(normed, w_query) + b_query.astype(jnp.float32)) * 0.125).astype(jnp.bfloat16)
    keys = matmul(normed, w_key).astype(jnp.bfloat16)
    values = (matmul(normed, w_value) + b_value.astype(jnp.float32)).astype(jnp.bfloat16)
    all_keys, all_values = (
        lax.all_gather(keys, "ctx", axis=0, tiled=True),
        lax.all_gather(values, "ctx", axis=0, tiled=True),
    )
    scores = attention_scores(query, all_keys, query_pos, key_pos)
    highest = jnp.max(scores, axis=-1, keepdims=True)
    raised = jnp.exp(scores - highest)
    totals = jnp.sum(raised, axis=-1, keepdims=True)
    probs_low = (raised / totals).astype(jnp.bfloat16)
    rows = query.shape[0]
    mixed = jnp.einsum(
        "hrl,lhd->rhd",
        probs_low,
        all_values.reshape(all_values.shape[0], H, HEAD),
        preferred_element_type=jnp.float32,
    )
    mixed = mixed.reshape(rows, -1).astype(jnp.bfloat16)
    hidden = start + (matmul(mixed, w_out) + b_out.astype(jnp.float32))
    normed_two = layer_norm(
        hidden, second_gain.astype(jnp.float32), second_shift.astype(jnp.float32)
    ).astype(jnp.bfloat16)
    before = matmul(normed_two, w_expand) + b_expand.astype(jnp.float32)
    active = jax.nn.gelu(before).astype(jnp.bfloat16)
    result = hidden + (matmul(active, w_reduce) + b_reduce.astype(jnp.float32))
    record = (
        start,
        normed,
        query,
        all_keys,
        all_values,
        highest,
        totals,
        mixed,
        hidden,
        normed_two,
        before,
        active,
    )
    return (record, result)


def backward(record, grad_result, weights, query_pos, key_pos):
    (
        first_gain,
        first_shift,
        w_query,
        b_query,
        w_key,
        w_value,
        b_value,
        w_out,
        b_out,
        second_gain,
        second_shift,
        w_expand,
        b_expand,
        w_reduce,
        b_reduce,
    ) = weights
    (
        start,
        normed,
        query,
        all_keys,
        all_values,
        highest,
        totals,
        mixed,
        hidden,
        normed_two,
        before,
        active,
    ) = record
    grad_branch = grad_result.astype(jnp.bfloat16)
    grad_w_reduce = transposed_left(active, grad_branch)
    grad_b_reduce = column_sums(grad_branch)
    grad_active = transposed_right(grad_branch, w_reduce)
    gelu_back = jax.vjp(jax.nn.gelu, before)[1]
    grad_before = gelu_back(grad_active)[0].astype(jnp.bfloat16)
    grad_w_expand = transposed_left(normed_two, grad_before)
    grad_b_expand = column_sums(grad_before)
    grad_normed_two = transposed_right(grad_before, w_expand)
    second_back = jax.vjp(
        layer_norm, hidden, second_gain.astype(jnp.float32), second_shift.astype(jnp.float32)
    )[1]
    grad_hidden_part, grad_second_gain, grad_second_shift = second_back(grad_normed_two)
    grad_hidden = grad_result + grad_hidden_part
    grad_attn = grad_hidden.astype(jnp.bfloat16)
    grad_w_out = transposed_left(mixed, grad_attn)
    grad_b_out = column_sums(grad_attn)
    grad_mixed = transposed_right(grad_attn, w_out).astype(jnp.bfloat16)
    rows = query.shape[0]
    length = all_keys.shape[0]
    scores = attention_scores(query, all_keys, query_pos, key_pos)
    probs = jnp.exp(scores - highest) / totals
    mixed_heads = grad_mixed.reshape(rows, H, HEAD)
    grad_probs = jnp.einsum(
        "rhd,lhd->hrl",
        mixed_heads,
        all_values.reshape(length, H, HEAD),
        preferred_element_type=jnp.float32,
    )
    inner = jnp.sum(probs * grad_probs, axis=-1, keepdims=True)
    grad_scores = (probs * (grad_probs - inner)).astype(jnp.bfloat16)
    grad_query = (
        jnp.einsum(
            "hrl,lhd->rhd",
            grad_scores,
            all_keys.reshape(length, H, HEAD),
            preferred_element_type=jnp.float32,
        )
        .reshape(rows, -1)
        .astype(jnp.bfloat16)
    )
    grad_query = (grad_query.astype(jnp.float32) * 0.125).astype(jnp.bfloat16)
    key_terms = jnp.einsum(
        "hrl,rhd->lhd",
        grad_scores,
        query.reshape(rows, H, HEAD),
        preferred_element_type=jnp.float32,
    ).reshape(length, -1)
    value_terms = jnp.einsum(
        "hrl,rhd->lhd", probs.astype(jnp.bfloat16), mixed_heads, preferred_element_type=jnp.float32
    ).reshape(length, -1)
    grad_keys, grad_values = (
        lax.psum_scatter(
            key_terms.astype(jnp.bfloat16), "ctx", scatter_dimension=0, tiled=True
        ).astype(jnp.float32),
        lax.psum_scatter(
            value_terms.astype(jnp.bfloat16), "ctx", scatter_dimension=0, tiled=True
        ).astype(jnp.float32),
    )
    grad_keys = grad_keys.astype(jnp.bfloat16)
    grad_values = grad_values.astype(jnp.bfloat16)
    grad_w_query = transposed_left(normed, grad_query)
    grad_b_query = column_sums(grad_query)
    grad_w_key = transposed_left(normed, grad_keys)
    grad_w_value = transposed_left(normed, grad_values)
    grad_b_value = column_sums(grad_values)
    grad_normed = (
        transposed_right(grad_query, w_query)
        + transposed_right(grad_keys, w_key)
        + transposed_right(grad_values, w_value)
    )
    first_back = jax.vjp(
        layer_norm, start, first_gain.astype(jnp.float32), first_shift.astype(jnp.float32)
    )[1]
    grad_start_part, grad_first_gain, grad_first_shift = first_back(grad_normed)
    grad_input = grad_hidden + grad_start_part
    grads = (
        grad_first_gain,
        grad_first_shift,
        grad_w_query,
        grad_b_query,
        grad_w_key,
        grad_w_value,
        grad_b_value,
        grad_w_out,
        grad_b_out,
        grad_second_gain,
        grad_second_shift,
        grad_w_expand,
        grad_b_expand,
        grad_w_reduce,
        grad_b_reduce,
    )
    return (grad_input, grads)


def scatter_tick(grads):
    return (
        lax.psum_scatter(
            grads[0].astype(jnp.bfloat16), "fsdp", scatter_dimension=0, tiled=True
        ).astype(jnp.float32),
        lax.psum_scatter(
            grads[1].astype(jnp.bfloat16), "fsdp", scatter_dimension=0, tiled=True
        ).astype(jnp.float32),
        lax.psum_scatter(
            grads[2].astype(jnp.bfloat16), "fsdp", scatter_dimension=0, tiled=True
        ).astype(jnp.float32),
        lax.psum_scatter(
            grads[3].astype(jnp.bfloat16), "fsdp", scatter_dimension=0, tiled=True
        ).astype(jnp.float32),
        lax.psum_scatter(
            grads[4].astype(jnp.bfloat16), "fsdp", scatter_dimension=0, tiled=True
        ).astype(jnp.float32),
        lax.psum_scatter(
            grads[5].astype(jnp.bfloat16), "fsdp", scatter_dimension=0, tiled=True
        ).astype(jnp.float32),
        lax.psum_scatter(
            grads[6].astype(jnp.bfloat16), "fsdp", scatter_dimension=0, tiled=True
        ).astype(jnp.float32),
        lax.psum_scatter(
            grads[7].astype(jnp.bfloat16), "fsdp", scatter_dimension=0, tiled=True
        ).astype(jnp.float32),
        lax.psum_scatter(
            grads[8].astype(jnp.bfloat16), "fsdp", scatter_dimension=0, tiled=True
        ).astype(jnp.float32),
        lax.psum_scatter(
            grads[9].astype(jnp.bfloat16), "fsdp", scatter_dimension=0, tiled=True
        ).astype(jnp.float32),
        lax.psum_scatter(
            grads[10].astype(jnp.bfloat16), "fsdp", scatter_dimension=0, tiled=True
        ).astype(jnp.float32),
        lax.psum_scatter(
            grads[11].astype(jnp.bfloat16), "fsdp", scatter_dimension=0, tiled=True
        ).astype(jnp.float32),
        lax.psum_scatter(
            grads[12].astype(jnp.bfloat16), "fsdp", scatter_dimension=0, tiled=True
        ).astype(jnp.float32),
        lax.psum_scatter(
            grads[13].astype(jnp.bfloat16), "fsdp", scatter_dimension=0, tiled=True
        ).astype(jnp.float32),
        lax.psum_scatter(
            grads[14].astype(jnp.bfloat16), "fsdp", scatter_dimension=0, tiled=True
        ).astype(jnp.float32),
    )


def shards(
    tokens,
    cotangent,
    block_order,
    first_gain,
    first_shift,
    w_query,
    b_query,
    w_key,
    w_value,
    b_value,
    w_out,
    b_out,
    second_gain,
    second_shift,
    w_expand,
    b_expand,
    w_reduce,
    b_reduce,
):
    section = lax.axis_index("section")
    micro, rows, width = tokens.shape
    ctx_count = lax.axis_size("ctx")
    block = rows // 2
    place = lax.axis_index("ctx")
    local_blocks = lax.dynamic_slice_in_dim(block_order, 2 * place, 2)
    offsets = jnp.arange(rows, dtype=jnp.int32)
    query_pos = (
        jnp.where(offsets < block, local_blocks[0], local_blocks[1]) * block + offsets % block
    )
    key_pos = jnp.repeat(block_order, block) * block + jnp.tile(
        jnp.arange(block, dtype=jnp.int32), 2 * ctx_count
    )
    gathered = (
        lax.all_gather(first_gain, "fsdp", axis=1, tiled=True),
        lax.all_gather(first_shift, "fsdp", axis=1, tiled=True),
        lax.all_gather(w_query, "fsdp", axis=1, tiled=True),
        lax.all_gather(b_query, "fsdp", axis=1, tiled=True),
        lax.all_gather(w_key, "fsdp", axis=1, tiled=True),
        lax.all_gather(w_value, "fsdp", axis=1, tiled=True),
        lax.all_gather(b_value, "fsdp", axis=1, tiled=True),
        lax.all_gather(w_out, "fsdp", axis=1, tiled=True),
        lax.all_gather(b_out, "fsdp", axis=1, tiled=True),
        lax.all_gather(second_gain, "fsdp", axis=1, tiled=True),
        lax.all_gather(second_shift, "fsdp", axis=1, tiled=True),
        lax.all_gather(w_expand, "fsdp", axis=1, tiled=True),
        lax.all_gather(b_expand, "fsdp", axis=1, tiled=True),
        lax.all_gather(w_reduce, "fsdp", axis=1, tiled=True),
        lax.all_gather(b_reduce, "fsdp", axis=1, tiled=True),
    )
    stored = tuple((piece[0] for piece in gathered))

    def fetch_weights():
        return stored

    stash = []
    output_ticks = []
    received = jnp.zeros((rows, width), jnp.bfloat16)
    for tick in range(micro + 1):
        number = jnp.clip(tick - section, 0, micro - 1)
        own_rows = lax.dynamic_index_in_dim(tokens, number, 0, keepdims=False)
        inputs = jnp.where(section == 0, own_rows, received)
        record, result = forward(inputs, fetch_weights(), query_pos, key_pos)
        stash.append(record)
        lowered = result.astype(jnp.bfloat16)
        output_ticks.append(lowered)
        if tick < micro:
            received = from_behind(lowered, "section", 1)
    stacked = jax.tree.map(lambda *parts: jnp.stack(parts), *stash)
    totals_all = None
    grad_ticks = []
    incoming = jnp.zeros((rows, width), jnp.bfloat16)
    for tick in range(micro + 1):
        wanted = tick - (1 - section)
        usable = (wanted >= 0) & (wanted < micro)
        number = jnp.clip(wanted, 0, micro - 1)
        own_grad = lax.dynamic_index_in_dim(cotangent, number, 0, keepdims=False)
        grad_result = jnp.where(section == 1, own_grad, incoming.astype(jnp.float32))
        record = jax.tree.map(
            lambda part: lax.dynamic_index_in_dim(part, number + section, 0, keepdims=False),
            stacked,
        )
        grad_input, grads = backward(record, grad_result, fetch_weights(), query_pos, key_pos)
        grads = tuple((jnp.where(usable, part, 0.0) for part in grads))
        shares = scatter_tick(grads)
        if totals_all is None:
            totals_all = shares
        else:
            totals_all = tuple((earlier + later for earlier, later in zip(totals_all, shares)))
        grad_ticks.append(grad_input)
        if tick < micro:
            incoming = from_behind(grad_input.astype(jnp.bfloat16), "section", -1)
    summed = (
        lax.psum(totals_all[0].astype(jnp.bfloat16), "ctx").astype(jnp.float32),
        lax.psum(totals_all[1].astype(jnp.bfloat16), "ctx").astype(jnp.float32),
        lax.psum(totals_all[2].astype(jnp.bfloat16), "ctx").astype(jnp.float32),
        lax.psum(totals_all[3].astype(jnp.bfloat16), "ctx").astype(jnp.float32),
        lax.psum(totals_all[4].astype(jnp.bfloat16), "ctx").astype(jnp.float32),
        lax.psum(totals_all[5].astype(jnp.bfloat16), "ctx").astype(jnp.float32),
        lax.psum(totals_all[6].astype(jnp.bfloat16), "ctx").astype(jnp.float32),
        lax.psum(totals_all[7].astype(jnp.bfloat16), "ctx").astype(jnp.float32),
        lax.psum(totals_all[8].astype(jnp.bfloat16), "ctx").astype(jnp.float32),
        lax.psum(totals_all[9].astype(jnp.bfloat16), "ctx").astype(jnp.float32),
        lax.psum(totals_all[10].astype(jnp.bfloat16), "ctx").astype(jnp.float32),
        lax.psum(totals_all[11].astype(jnp.bfloat16), "ctx").astype(jnp.float32),
        lax.psum(totals_all[12].astype(jnp.bfloat16), "ctx").astype(jnp.float32),
        lax.psum(totals_all[13].astype(jnp.bfloat16), "ctx").astype(jnp.float32),
        lax.psum(totals_all[14].astype(jnp.bfloat16), "ctx").astype(jnp.float32),
    )
    layer_outputs = lax.dynamic_slice_in_dim(jnp.stack(output_ticks), section, micro, 0)[None]
    input_grads = lax.dynamic_slice_in_dim(jnp.stack(grad_ticks), 1 - section, micro, 0)[None]
    finals = tuple((part[None] for part in summed))
    return (
        layer_outputs,
        input_grads,
        finals[0],
        finals[1],
        finals[2],
        finals[3],
        finals[4],
        finals[5],
        finals[6],
        finals[7],
        finals[8],
        finals[9],
        finals[10],
        finals[11],
        finals[12],
        finals[13],
        finals[14],
    )


def solution(mesh):
    return jax.shard_map(
        shards,
        mesh=mesh,
        in_specs=(
            P("fsdp", "ctx", None),
            P("fsdp", "ctx", None),
            P(),
            P("section", "fsdp"),
            P("section", "fsdp"),
            P("section", "fsdp", None),
            P("section", "fsdp"),
            P("section", "fsdp", None),
            P("section", "fsdp", None),
            P("section", "fsdp"),
            P("section", "fsdp", None),
            P("section", "fsdp"),
            P("section", "fsdp"),
            P("section", "fsdp"),
            P("section", "fsdp", None),
            P("section", "fsdp"),
            P("section", "fsdp", None),
            P("section", "fsdp"),
        ),
        out_specs=(
            P("section", "fsdp", "ctx", None),
            P("section", "fsdp", "ctx", None),
            P("section", "fsdp"),
            P("section", "fsdp"),
            P("section", "fsdp", None),
            P("section", "fsdp"),
            P("section", "fsdp", None),
            P("section", "fsdp", None),
            P("section", "fsdp"),
            P("section", "fsdp", None),
            P("section", "fsdp"),
            P("section", "fsdp"),
            P("section", "fsdp"),
            P("section", "fsdp", None),
            P("section", "fsdp"),
            P("section", "fsdp", None),
            P("section", "fsdp"),
        ),
        check_vma=False,
    )
```

profile of v0, /device:TPU:0, one launch (start us, length us, event | category | flops | bytes accessed | tf_op | source)
XLA Modules:
  0.0 1846.2 jit_solution(4721227482376010817)
XLA Ops:
  41.5 22.0 %all-gather.13.cloned.1.call-done = bf16[1,768,768]{2,1,0:T(8,128)(2,1)} async-done(((bf16[1,192,768]{2,1,0:T(8,128)(2,1)}), bf16[1,768,768]{2,1,0:T(8,128)(2,1)}) %all-gather.13.cloned.1.call-update) | async-done | bytes 1179664 | tf_op jit(solution)/shard_map/all_gather | solution.py:342
  92.1 45.4 %all-gather.21.cloned.1.call-done = bf16[1024,768]{1,0:T(8,128)(2,1)} async-done(((bf16[64,768]{1,0:T(8,128)(2,1)}), bf16[1024,768]{1,0:T(8,128)(2,1)}) %all-gather.21.cloned.1.call-update) | async-done | bytes 1572880 | tf_op jit(solution)/shard_map/all_gather | solution.py:85
  139.2 44.2 %all-gather.15.cloned.1.call-done = bf16[1024,768]{1,0:T(8,128)(2,1)} async-done(((bf16[64,768]{1,0:T(8,128)(2,1)}), bf16[1024,768]{1,0:T(8,128)(2,1)}) %all-gather.15.cloned.1.call-update) | async-done | bytes 1572880 | tf_op jit(solution)/shard_map/all_gather | solution.py:86
  210.6 52.9 %all-gather.25.cloned.1.call-done = bf16[1,768,3072]{2,1,0:T(8,128)(2,1)} async-done(((bf16[1,192,3072]{2,1,0:T(8,128)(2,1)}), bf16[1,768,3072]{2,1,0:T(8,128)(2,1)}) %all-gather.25.cloned.1.call-update) | async-done | bytes 4718608 | tf_op jit(solution)/shard_map/all_gather | solution.py:348
  267.8 50.5 %all-gather.27.cloned.1.call-done = bf16[1,3072,768]{2,1,0:T(8,128)(2,1)} async-done(((bf16[1,768,768]{2,1,0:T(8,128)(2,1)}), bf16[1,3072,768]{2,1,0:T(8,128)(2,1)}) %all-gather.27.cloned.1.call-update) | async-done | bytes 4718608 | tf_op jit(solution)/shard_map/all_gather | solution.py:350
  329.9 41.4 %all-gather.31.cloned.1.call-done = bf16[1024,768]{1,0:T(8,128)(2,1)} async-done(((bf16[64,768]{1,0:T(8,128)(2,1)}), bf16[1024,768]{1,0:T(8,128)(2,1)}) %all-gather.31.cloned.1.call-update) | async-done | bytes 1572880 | tf_op jit(solution)/shard_map/all_gather | solution.py:85
  378.6 38.7 %all-gather.29.cloned.1.call-done = bf16[1024,768]{1,0:T(8,128)(2,1)} async-done(((bf16[64,768]{1,0:T(8,128)(2,1)}), bf16[1024,768]{1,0:T(8,128)(2,1)}) %all-gather.29.cloned.1.call-update) | async-done | bytes 1572880 | tf_op jit(solution)/shard_map/all_gather | solution.py:86
  438.9 38.9 %all-gather.35.cloned.1.call-done = bf16[1024,768]{1,0:T(8,128)(2,1)} async-done(((bf16[64,768]{1,0:T(8,128)(2,1)}), bf16[1024,768]{1,0:T(8,128)(2,1)}) %all-gather.35.cloned.1.call-update) | async-done | bytes 1572880 | tf_op jit(solution)/shard_map/all_gather | solution.py:85
  482.9 40.8 %all-gather.33.cloned.1.call-done = bf16[1024,768]{1,0:T(8,128)(2,1)} async-done(((bf16[64,768]{1,0:T(8,128)(2,1)}), bf16[1024,768]{1,0:T(8,128)(2,1)}) %all-gather.33.cloned.1.call-update) | async-done | bytes 1572880 | tf_op jit(solution)/shard_map/all_gather | solution.py:86
  591.7 56.1 %reduce-scatter.73.cloned.1.call-done = bf16[64,768]{1,0:T(8,128)(2,1)} async-done(((bf16[1024,768]{1,0:T(8,128)(2,1)}), bf16[64,768]{1,0:T(8,128)(2,1)}) %reduce-scatter.73.cloned.1.call-update) | async-done | bytes 98320
  651.7 72.2 %reduce-scatter.75.cloned.1.call-done = bf16[64,768]{1,0:T(8,128)(2,1)} async-done(((bf16[1024,768]{1,0:T(8,128)(2,1)}), bf16[64,768]{1,0:T(8,128)(2,1)}) %reduce-scatter.75.cloned.1.call-update) | async-done | bytes 98320
  771.0 61.3 %reduce-scatter.77.cloned.1.call-done = bf16[64,768]{1,0:T(8,128)(2,1)} async-done(((bf16[1024,768]{1,0:T(8,128)(2,1)}), bf16[64,768]{1,0:T(8,128)(2,1)}) %reduce-scatter.77.cloned.1.call-update) | async-done | bytes 98320
  836.1 72.2 %reduce-scatter.79.cloned.1.call-done = bf16[64,768]{1,0:T(8,128)(2,1)} async-done(((bf16[1024,768]{1,0:T(8,128)(2,1)}), bf16[64,768]{1,0:T(8,128)(2,1)}) %reduce-scatter.79.cloned.1.call-update) | async-done | bytes 98320
  970.7 43.1 %reduce-scatter.83.cloned.1.call-done = bf16[64,768]{1,0:T(8,128)(2,1)} async-done(((bf16[1024,768]{1,0:T(8,128)(2,1)}), bf16[64,768]{1,0:T(8,128)(2,1)}) %reduce-scatter.83.cloned.1.call-update) | async-done | bytes 98320
  1019.6 70.2 %reduce-scatter.81.cloned.1.call-done = bf16[64,768]{1,0:T(8,128)(2,1)} async-done(((bf16[1024,768]{1,0:T(8,128)(2,1)}), bf16[64,768]{1,0:T(8,128)(2,1)}) %reduce-scatter.81.cloned.1.call-update) | async-done | bytes 98320
  1144.4 23.7 %reduce-scatter.59.cloned.1.call-done = bf16[192,768]{1,0:T(8,128)(2,1)} async-done(((bf16[768,768]{1,0:T(8,128)(2,1)}), bf16[192,768]{1,0:T(8,128)(2,1)}) %reduce-scatter.59.cloned.1.call-update) | async-done | bytes 294928 | tf_op jit(solution)/shard_map/reduce_scatter | solution.py:276
  1170.0 24.2 %reduce-scatter.37.cloned.1.call-done = bf16[192,768]{1,0:T(8,128)(2,1)} async-done(((bf16[768,768]{1,0:T(8,128)(2,1)}), bf16[192,768]{1,0:T(8,128)(2,1)}) %reduce-scatter.37.cloned.1.call-update) | async-done | bytes 294928 | tf_op jit(solution)/shard_map/reduce_scatter | solution.py:261
  1194.3 26.3 %reduce-scatter.39.cloned.1.call-done = bf16[192,768]{1,0:T(8,128)(2,1)} async-done(((bf16[768,768]{1,0:T(8,128)(2,1)}), bf16[192,768]{1,0:T(8,128)(2,1)}) %reduce-scatter.39.cloned.1.call-update) | async-done | bytes 294928 | tf_op jit(solution)/shard_map/reduce_scatter | solution.py:261
  1220.6 26.7 %reduce-scatter.41.cloned.1.call-done = bf16[192,768]{1,0:T(8,128)(2,1)} async-done(((bf16[768,768]{1,0:T(8,128)(2,1)}), bf16[192,768]{1,0:T(8,128)(2,1)}) %reduce-scatter.41.cloned.1.call-update) | async-done | bytes 294928 | tf_op jit(solution)/shard_map/reduce_scatter | solution.py:261
  1249.5 24.2 %reduce-scatter.49.cloned.1.call-done = bf16[192,768]{1,0:T(8,128)(2,1)} async-done(((bf16[768,768]{1,0:T(8,128)(2,1)}), bf16[192,768]{1,0:T(8,128)(2,1)}) %reduce-scatter.49.cloned.1.call-update) | async-done | bytes 294928 | tf_op jit(solution)/shard_map/reduce_scatter | solution.py:270
  1273.6 26.2 %reduce-scatter.51.cloned.1.call-done = bf16[192,768]{1,0:T(8,128)(2,1)} async-done(((bf16[768,768]{1,0:T(8,128)(2,1)}), bf16[192,768]{1,0:T(8,128)(2,1)}) %reduce-scatter.51.cloned.1.call-update) | async-done | bytes 294928 | tf_op jit(solution)/shard_map/reduce_scatter | solution.py:270
  1299.8 26.1 %reduce-scatter.53.cloned.1.call-done = bf16[192,768]{1,0:T(8,128)(2,1)} async-done(((bf16[768,768]{1,0:T(8,128)(2,1)}), bf16[192,768]{1,0:T(8,128)(2,1)}) %reduce-scatter.53.cloned.1.call-update) | async-done | bytes 294928 | tf_op jit(solution)/shard_map/reduce_scatter | solution.py:270
  1327.9 24.4 %reduce-scatter.43.cloned.1.call-done = bf16[192,768]{1,0:T(8,128)(2,1)} async-done(((bf16[768,768]{1,0:T(8,128)(2,1)}), bf16[192,768]{1,0:T(8,128)(2,1)}) %reduce-scatter.43.cloned.1.call-update) | async-done | bytes 294928 | tf_op jit(solution)/shard_map/reduce_scatter | solution.py:267
  1352.3 26.4 %reduce-scatter.45.cloned.1.call-done = bf16[192,768]{1,0:T(8,128)(2,1)} async-done(((bf16[768,768]{1,0:T(8,128)(2,1)}), bf16[192,768]{1,0:T(8,128)(2,1)}) %reduce-scatter.45.cloned.1.call-update) | async-done | bytes 294928 | tf_op jit(solution)/shard_map/reduce_scatter | solution.py:267
  1378.6 26.8 %reduce-scatter.47.cloned.1.call-done = bf16[192,768]{1,0:T(8,128)(2,1)} async-done(((bf16[768,768]{1,0:T(8,128)(2,1)}), bf16[192,768]{1,0:T(8,128)(2,1)}) %reduce-scatter.47.cloned.1.call-update) | async-done | bytes 294928 | tf_op jit(solution)/shard_map/reduce_scatter | solution.py:267
  1407.4 51.4 %reduce-scatter.67.cloned.1.call-done = bf16[768,768]{1,0:T(8,128)(2,1)} async-done(((bf16[3072,768]{1,0:T(8,128)(2,1)}), bf16[768,768]{1,0:T(8,128)(2,1)}) %reduce-scatter.67.cloned.1.call-update) | async-done | bytes 1179664 | tf_op jit(solution)/shard_map/reduce_scatter | solution.py:294
  1458.8 53.3 %reduce-scatter.69.cloned.1.call-done = bf16[768,768]{1,0:T(8,128)(2,1)} async-done(((bf16[3072,768]{1,0:T(8,128)(2,1)}), bf16[768,768]{1,0:T(8,128)(2,1)}) %reduce-scatter.69.cloned.1.call-update) | async-done | bytes 1179664 | tf_op jit(solution)/shard_map/reduce_scatter | solution.py:294
  1512.1 53.1 %reduce-scatter.71.cloned.1.call-done = bf16[768,768]{1,0:T(8,128)(2,1)} async-done(((bf16[3072,768]{1,0:T(8,128)(2,1)}), bf16[768,768]{1,0:T(8,128)(2,1)}) %reduce-scatter.71.cloned.1.call-update) | async-done | bytes 1179664 | tf_op jit(solution)/shard_map/reduce_scatter | solution.py:294
  1568.6 49.9 %reduce-scatter.61.cloned.1.call-done = bf16[192,3072]{1,0:T(8,128)(2,1)} async-done(((bf16[768,3072]{1,0:T(8,128)(2,1)}), bf16[192,3072]{1,0:T(8,128)(2,1)}) %reduce-scatter.61.cloned.1.call-update) | async-done | bytes 1179664 | tf_op jit(solution)/shard_map/reduce_scatter | solution.py:288
  1618.5 53.3 %reduce-scatter.63.cloned.1.call-done = bf16[192,3072]{1,0:T(8,128)(2,1)} async-done(((bf16[768,3072]{1,0:T(8,128)(2,1)}), bf16[192,3072]{1,0:T(8,128)(2,1)}) %reduce-scatter.63.cloned.1.call-update) | async-done | bytes 1179664 | tf_op jit(solution)/shard_map/reduce_scatter | solution.py:288
  1671.8 53.1 %reduce-scatter.65.cloned.1.call-done = bf16[192,3072]{1,0:T(8,128)(2,1)} async-done(((bf16[768,3072]{1,0:T(8,128)(2,1)}), bf16[192,3072]{1,0:T(8,128)(2,1)}) %reduce-scatter.65.cloned.1.call-update) | async-done | bytes 1179664 | tf_op jit(solution)/shard_map/reduce_scatter | solution.py:288
  1749.5 75.1 %all-reduce.35 = (bf16[1,192]{1,0:T(2,128)(2,1)S(1)}, bf16[1,192]{1,0:T(2,128)(2,1)S(1)}, bf16[1,192]{1,0:T(2,128)(2,1)S(1)}, bf16[1,192]{1,0:T(2,128)(2,1)S(1)}...) all-reduce(bf16[1,192]{1,0:T(2,128)(2,1)S(1)} %broadcast_in_dim.339, ...), channel_id=1, replica_groups=mesh['section'=2,'ctx'=16,'fsdp'=4] {'ctx'}, use_global_device_ids=true, to_apply=%region_57.58 | all-reduce | flops 2304 | bytes 9216 | tf_op jit(solution)/shard_map/psum | solution.py:396
  (792 shorter events, 432.3 us)
Async XLA Ops:
  9.4 128.1 %all-gather.21.cloned.1.call-start = ((), (), s32[]{:S(2)}) async-start(), calls=%async_computation.28 | async-start | bytes 1671168 | tf_op jit(solution)/shard_map/all_gather | solution.py:85
  41.5 141.9 %all-gather.15.cloned.1.call-start = ((), (), s32[]{:S(2)}) async-start(), calls=%async_computation.25 | async-start | bytes 1671168 | tf_op jit(solution)/shard_map/all_gather | solution.py:86
  65.8 142.8 %all-gather.23.cloned.1.call-start = ((), (), s32[]{:S(2)}) async-start(), calls=%async_computation.29 | async-start | bytes 1474560 | tf_op jit(solution)/shard_map/all_gather | solution.py:344
  66.4 197.1 %all-gather.25.cloned.1.call-start = ((), (), s32[]{:S(2)}) async-start(), calls=%async_computation.30 | async-start | bytes 5898240 | tf_op jit(solution)/shard_map/all_gather | solution.py:348
  67.2 251.1 %all-gather.27.cloned.1.call-start = ((), (), s32[]{:S(2)}) async-start(), calls=%async_computation.31 | async-start | bytes 5898240 | tf_op jit(solution)/shard_map/all_gather | solution.py:350
  67.9 303.5 %all-gather.31.cloned.1.call-start = ((), (), s32[]{:S(2)}) async-start(), calls=%async_computation.33 | async-start | bytes 1671168 | tf_op jit(solution)/shard_map/all_gather | solution.py:85
  327.9 149.9 %all-gather.35.cloned.1.call-start = ((), (), s32[]{:S(2)}) async-start(), calls=%async_computation.35 | async-start | bytes 1671168 | tf_op jit(solution)/shard_map/all_gather | solution.py:85
  435.4 212.5 %reduce-scatter.73.cloned.1.call-start = ((), (), s32[]{:S(2)}) async-start(), calls=%async_computation.54 | async-start | bytes 1671168
  574.7 149.2 %reduce-scatter.75.cloned.1.call-start = ((), (), s32[]{:S(2)}) async-start(), calls=%async_computation.55 | async-start | bytes 1671168
  581.5 250.8 %reduce-scatter.77.cloned.1.call-start = ((), (), s32[]{:S(2)}) async-start(), calls=%async_computation.56 | async-start | bytes 1671168
  758.5 149.8 %reduce-scatter.79.cloned.1.call-start = ((), (), s32[]{:S(2)}) async-start(), calls=%async_computation.57 | async-start | bytes 1671168
  764.9 248.9 %reduce-scatter.83.cloned.1.call-start = ((), (), s32[]{:S(2)}) async-start(), calls=%async_computation.59 | async-start | bytes 1671168
  939.8 149.9 %reduce-scatter.81.cloned.1.call-start = ((), (), s32[]{:S(2)}) async-start(), calls=%async_computation.58 | async-start | bytes 1671168
  948.7 195.7 %reduce-scatter.55.cloned.1.call-start = ((), (), s32[]{:S(2)}) async-start(), calls=%async_computation.45 | async-start | bytes 1474560 | tf_op jit(solution)/shard_map/reduce_scatter | solution.py:276
  952.3 192.1 %reduce-scatter.57.cloned.1.call-start = ((), (), s32[]{:S(2)}) async-start(), calls=%async_computation.46 | async-start | bytes 1474560 | tf_op jit(solution)/shard_map/reduce_scatter | solution.py:276
  954.8 213.3 %reduce-scatter.59.cloned.1.call-start = ((), (), s32[]{:S(2)}) async-start(), calls=%async_computation.47 | async-start | bytes 1474560 | tf_op jit(solution)/shard_map/reduce_scatter | solution.py:276
  957.3 236.9 %reduce-scatter.37.cloned.1.call-start = ((), (), s32[]{:S(2)}) async-start(), calls=%async_computation.36 | async-start | bytes 1474560 | tf_op jit(solution)/shard_map/reduce_scatter | solution.py:261
  959.7 260.9 %reduce-scatter.39.cloned.1.call-start = ((), (), s32[]{:S(2)}) async-start(), calls=%async_computation.37 | async-start | bytes 1474560 | tf_op jit(solution)/shard_map/reduce_scatter | solution.py:261
  962.3 285.1 %reduce-scatter.41.cloned.1.call-start = ((), (), s32[]{:S(2)}) async-start(), calls=%async_computation.38 | async-start | bytes 1474560 | tf_op jit(solution)/shard_map/reduce_scatter | solution.py:261
  967.5 306.2 %reduce-scatter.49.cloned.1.call-start = ((), (), s32[]{:S(2)}) async-start(), calls=%async_computation.42 | async-start | bytes 1474560 | tf_op jit(solution)/shard_map/reduce_scatter | solution.py:270
  969.1 330.7 %reduce-scatter.51.cloned.1.call-start = ((), (), s32[]{:S(2)}) async-start(), calls=%async_computation.43 | async-start | bytes 1474560 | tf_op jit(solution)/shard_map/reduce_scatter | solution.py:270
  970.7 355.3 %reduce-scatter.53.cloned.1.call-start = ((), (), s32[]{:S(2)}) async-start(), calls=%async_computation.44 | async-start | bytes 1474560 | tf_op jit(solution)/shard_map/reduce_scatter | solution.py:270
  1016.2 336.1 %reduce-scatter.43.cloned.1.call-start = ((), (), s32[]{:S(2)}) async-start(), calls=%async_computation.39 | async-start | bytes 1474560 | tf_op jit(solution)/shard_map/reduce_scatter | solution.py:267
  1017.9 360.7 %reduce-scatter.45.cloned.1.call-start = ((), (), s32[]{:S(2)}) async-start(), calls=%async_computation.40 | async-start | bytes 1474560 | tf_op jit(solution)/shard_map/reduce_scatter | solution.py:267
  1019.5 385.9 %reduce-scatter.47.cloned.1.call-start = ((), (), s32[]{:S(2)}) async-start(), calls=%async_computation.41 | async-start | bytes 1474560 | tf_op jit(solution)/shard_map/reduce_scatter | solution.py:267
  1092.2 366.6 %reduce-scatter.67.cloned.1.call-start = ((), (), s32[]{:S(2)}) async-start(), calls=%async_computation.51 | async-start | bytes 5898240 | tf_op jit(solution)/shard_map/reduce_scatter | solution.py:294
  1102.1 409.9 %reduce-scatter.69.cloned.1.call-start = ((), (), s32[]{:S(2)}) async-start(), calls=%async_computation.52 | async-start | bytes 5898240 | tf_op jit(solution)/shard_map/reduce_scatter | solution.py:294
  1107.7 457.5 %reduce-scatter.71.cloned.1.call-start = ((), (), s32[]{:S(2)}) async-start(), calls=%async_computation.53 | async-start | bytes 5898240 | tf_op jit(solution)/shard_map/reduce_scatter | solution.py:294
  1113.1 505.3 %reduce-scatter.61.cloned.1.call-start = ((), (), s32[]{:S(2)}) async-start(), calls=%async_computation.48 | async-start | bytes 5898240 | tf_op jit(solution)/shard_map/reduce_scatter | solution.py:288
  1119.3 552.5 %reduce-scatter.63.cloned.1.call-start = ((), (), s32[]{:S(2)}) async-start(), calls=%async_computation.49 | async-start | bytes 5898240 | tf_op jit(solution)/shard_map/reduce_scatter | solution.py:288
  1124.8 600.1 %reduce-scatter.65.cloned.1.call-start = ((), (), s32[]{:S(2)}) async-start(), calls=%async_computation.50 | async-start | bytes 5898240 | tf_op jit(solution)/shard_map/reduce_scatter | solution.py:288
  1130.2 700.7 %all-reduce.41.cloned.1.call-start = ((), (), s32[]{:S(2)}) async-start(), calls=%async_computation.60 | async-start | bytes 7077888 | tf_op jit(solution)/shard_map/psum | solution.py:398
  (201 other events, 4721.3 us)
Sparse Core Ops, SparseCore 0:
  9.7 26.9 all-gather.18
  38.3 25.1 all-gather.12
  65.2 24.9 all-gather.16
  92.8 44.5 all-gather.20
  140.0 43.3 all-gather.14
  210.3 53.1 all-gather.24
  265.2 53.0 all-gather.26
  326.9 44.4 all-gather.30
  373.9 43.3 all-gather.28
  434.4 43.3 all-gather.34
  480.4 43.3 all-gather.32
  574.9 72.9 reduce-scatter.72
  650.9 72.9 reduce-scatter.74
  758.6 73.5 reduce-scatter.76
  835.3 72.9 reduce-scatter.78
  940.0 73.7 reduce-scatter.82
  1016.9 72.8 reduce-scatter.80
  1117.8 23.9 reduce-scatter.56
  1196.7 23.8 reduce-scatter.38
  1223.5 23.8 reduce-scatter.40
  1249.8 23.8 reduce-scatter.48
  1275.9 23.8 reduce-scatter.50
  1328.4 23.8 reduce-scatter.42
  1354.7 23.8 reduce-scatter.44
  1381.5 23.8 reduce-scatter.46
  1407.8 50.9 reduce-scatter.66
  1461.2 50.8 reduce-scatter.68
  1514.3 50.8 reduce-scatter.70
  1567.6 50.8 reduce-scatter.60
  1620.9 50.8 reduce-scatter.62
  1674.0 50.8 reduce-scatter.64
  1730.1 99.0 all-reduce.40
  (5 shorter events, 118.1 us)
where the time goes:
time: 1860 us; the launch traced here: 1850 us
  waiting for transfers between devices  1350 us (73%)
  matrix products  170 us (9%)
  blocking collectives  120 us (6%)
  local copies, waits for them, and re-layouts  87.4 us (5%)
  other arithmetic  87.3 us (5%)
  between operations  19.7 us (1%)
    unnamed x43, waiting for transfers between devices  380 us
    reduce_scatter x3, waiting for transfers between devices, scatter_tick(): lax.psum_scatter(grads[13].astype(jnp.bfloat16), 'fsdp', scatter_dimensio...  158 us
    reduce_scatter x3, waiting for transfers between devices, scatter_tick(): lax.psum_scatter(grads[11].astype(jnp.bfloat16), 'fsdp', scatter_dimensio...  156 us
    all_gather x3, waiting for transfers between devices, forward(): lax.all_gather(keys, 'ctx', axis=0, tiled=True)  126 us
    all_gather x3, waiting for transfers between devices, forward(): lax.all_gather(values, 'ctx', axis=0, tiled=True)  124 us
    reduce_scatter x3, waiting for transfers between devices, scatter_tick(): lax.psum_scatter(grads[4].astype(jnp.bfloat16), 'fsdp', scatter_dimension...  77.5 us
    reduce_scatter x3, waiting for transfers between devices, scatter_tick(): lax.psum_scatter(grads[2].astype(jnp.bfloat16), 'fsdp', scatter_dimension...  77.3 us
    reduce_scatter x3, waiting for transfers between devices, scatter_tick(): lax.psum_scatter(grads[5].astype(jnp.bfloat16), 'fsdp', scatter_dimension...  76.5 us
  transfers between devices with their start and end apart: 41, of which 35 were waited for; matrix products, arithmetic and copies ran while one was open for 11% of the time, Pallas kernels for 0%

commit v1 on v0

v1 whole, which is shorter than its diff:
```python
import functools

import jax
import jax.numpy as jnp
from jax import lax
from jax.experimental import pallas as pl
from jax.experimental.pallas import tpu as pltpu
from jax.sharding import PartitionSpec as P

HEAD = 64
EPSILON = 1e-05
F32 = jnp.float32
BF16 = jnp.bfloat16
MESH = pl.DeviceIdType.MESH
GELU_SCALE = 0.7978845608028654
GELU_CUBE = 0.044715


def mm(left, right):
    return jnp.dot(left, right, preferred_element_type=F32)


def mm_nt(left, right):
    return lax.dot_general(left, right, (((1,), (1,)), ((), ())), preferred_element_type=F32)


def mm_tn(left, right):
    return lax.dot_general(left, right, (((0,), (0,)), ((), ())), preferred_element_type=F32)


def normalize(values):
    average = jnp.mean(values, axis=-1, keepdims=True)
    centered = values - average
    variance = jnp.mean(centered * centered, axis=-1, keepdims=True)
    factor = lax.rsqrt(variance + EPSILON)
    return centered * factor, factor


def norm_back(grad, normal, factor, gain):
    scaled = grad * gain
    return factor * (
        scaled
        - jnp.mean(scaled, axis=-1, keepdims=True)
        - normal * jnp.mean(scaled * normal, axis=-1, keepdims=True)
    )


def column_sums(values):
    return jnp.sum(values.astype(F32), axis=0, keepdims=True)


def kernel(
    N, S, R, D, F,
    tok, cot, wqkv_in, wout_in, wexp_in, wred_in, vecs_in, biases, qpos, kpos,
    out_y, out_dx, out_wqkv, out_wout, out_wexp, out_wred, out_small,
    u_in, cot_in, gp_in, y_low, dx_buf, dx_low, vecs,
    w3, wexp, n1, n2, g_all, ga_all, gb_all, active, slope,
    q_all, kv, probs, mixed, gm_all, dq_all, dk_all, dv_all, dkv_send, dkv_recv,
    part_send, part_recv, own, hidden, grad,
    ff1s, ff1r, ff2, ff3, aq1s, aq1r, aq2, aq3, ao1s, ao1r, ao2, ao3,
    sm_y, sm_x, sm_z, sm_own,
    ssem, rsem, lsem,
):
    T = S * R
    DH = D // N
    heads = DH // HEAD
    s = lax.axis_index("section")
    c = lax.axis_index("ctx")
    y = lax.axis_index("fsdp")
    x = lax.rem(c, N)
    z = lax.div(c, N)
    straight = y == z
    order = tuple(sorted(range(1, N), key=lambda d: min(d, N - d)))

    def near(v, d):
        return lax.rem(v + d, N)

    counter = [0]

    def block_of(count=N):
        counter[0] += count
        return counter[0] - count

    drains = []

    def start(src, dst, send, recv, device):
        copy = pltpu.make_async_remote_copy(
            src_ref=src, dst_ref=dst, send_sem=ssem.at[send], recv_sem=rsem.at[recv],
            device_id=device, device_id_type=MESH,
        )
        copy.start()
        drains.append((None, copy))

    def start_if(condition, src, dst, send, recv, device):
        copy = pltpu.make_async_remote_copy(
            src_ref=src, dst_ref=dst, send_sem=ssem.at[send], recv_sem=rsem.at[recv],
            device_id=device, device_id_type=MESH,
        )
        pl.when(condition)(lambda: copy.start())
        drains.append((condition, copy))

    def landed(dst, recv):
        pltpu.make_async_remote_copy(
            src_ref=dst, dst_ref=dst, send_sem=ssem.at[0], recv_sem=rsem.at[recv],
            device_id={"section": 1 - s}, device_id_type=MESH,
        ).wait_recv()

    def along(axis, index):
        if axis == "y":
            return {"fsdp": index}
        if axis == "x":
            return {"ctx": z * N + index}
        return {"ctx": index * N + x}

    place = {"x": x, "y": y, "z": z}

    def spread(axis, ref, base):
        me = place[axis]
        for d in order:
            start(ref.at[me], ref.at[me], base + d, base + me, along(axis, near(me, d)))

    def arrived(axis, ref, base, d):
        source = near(place[axis], d)
        landed(ref.at[source], base + source)

    def deal(axis, src, dst, base, d):
        me = place[axis]
        other = near(me, d)
        start(src.at[other], dst.at[me], base + d, base + me, along(axis, other))

    barrier = pltpu.get_barrier_semaphore()
    met = 0
    for dx in range(N):
        for dy in range(N):
            if dx or dy:
                pl.semaphore_signal(
                    barrier, inc=1, device_id={"ctx": z * N + near(x, dx), "fsdp": near(y, dy)},
                    device_id_type=MESH,
                )
                met += 1
    for dz in range(1, N):
        pl.semaphore_signal(
            barrier, inc=1, device_id={"ctx": near(z, dz) * N + x}, device_id_type=MESH
        )
        met += 1
    pl.semaphore_signal(barrier, inc=1, device_id={"section": 1 - s}, device_id_type=MESH)
    met += 1
    partner = {"ctx": y * N + x, "fsdp": z}

    @pl.when(jnp.logical_not(straight))
    def _():
        pl.semaphore_signal(barrier, inc=1, device_id=partner, device_id_type=MESH)
        pl.semaphore_wait(barrier, met + 1)

    @pl.when(straight)
    def _():
        pl.semaphore_wait(barrier, met)

    turned = jnp.logical_not(straight)

    k_u, k_cot, k_gp, k_y, k_dx = (block_of(1) for _ in range(5))
    start_if(jnp.logical_and(s == 0, turned), tok, u_in, k_u, k_u, partner)

    @pl.when(jnp.logical_and(s == 0, straight))
    def _():
        u_in[...] = tok[...]

    k_vecs = block_of()
    vecs[y] = vecs_in[...]
    spread("y", vecs, k_vecs)
    k_w3 = block_of()
    own_w3 = pltpu.make_async_copy(wqkv_in.at[y], w3.at[y], lsem.at[0])
    own_w3.start()
    for d in order:
        deal("y", wqkv_in, w3, k_w3, d)
    k_wexp = block_of()
    own_wexp = pltpu.make_async_copy(
        wexp_in.at[:, pl.ds(pl.multiple_of(y * F, 128), F)], wexp.at[y], lsem.at[1]
    )
    own_wexp.start()
    for d in order:
        other = near(y, d)
        start(
            wexp_in.at[:, pl.ds(pl.multiple_of(other * F, 128), F)], wexp.at[y],
            k_wexp + d, k_wexp + y, along("y", other),
        )
    start_if(jnp.logical_and(s == 1, turned), cot, cot_in, k_cot, k_cot, partner)

    @pl.when(jnp.logical_and(s == 1, straight))
    def _():
        cot_in[...] = cot[...]

    for d in order:
        arrived("y", vecs, k_vecs, d)
    params = vecs[0]
    for other in range(1, N):
        params = params + vecs[other]
    gain1, shift1, gain2, shift2, b_out, b_reduce = (params[i : i + 1] for i in range(6))
    b_query = biases[0:1, 0:DH]
    b_value = biases[1:2, 0:DH]
    b_expand = biases[2:3, 0:F]

    @pl.when(jnp.logical_or(s == 1, turned))
    def _():
        landed(u_in, k_u)

    start_values = u_in[...].reshape(T, D).astype(F32)
    normal, _ = normalize(start_values)
    n1[y] = (normal * gain1 + shift1).astype(BF16)
    k_n1 = block_of()
    spread("y", n1, k_n1)

    own_w3.wait()
    for d in order:
        arrived("y", w3, k_w3, d)
    for d in (0,) + order:
        b = near(y, d)
        if d:
            arrived("y", n1, k_n1, d)
        rows = n1[b]
        kv[x, 0, b] = mm(rows, w3[:, 1].reshape(D, DH)).astype(BF16).reshape(S, R, DH)
        kv[x, 1, b] = (mm(rows, w3[:, 2].reshape(D, DH)) + b_value).astype(BF16).reshape(S, R, DH)
        q_all[b] = (
            ((mm(rows, w3[:, 0].reshape(D, DH)) + b_query) * 0.125).astype(BF16).reshape(S, R, DH)
        )
    k_kv = block_of()
    spread("x", kv, k_kv)

    lanes = lax.broadcasted_iota(jnp.int32, (1, DH), 1)
    in_head = [
        jnp.logical_and(lanes >= h * HEAD, lanes < (h + 1) * HEAD) for h in range(heads)
    ]

    def only(h, values):
        return jnp.where(in_head[h], values.astype(F32), 0.0)

    for d in order:
        arrived("x", kv, k_kv, d)

    @pl.loop(0, S)
    def _(i):
        query = q_all[:, i].reshape(N * R, DH)
        keys = kv[:, 0, :, i].reshape(N * N * R, DH)
        values = kv[:, 1, :, i].reshape(N * N * R, DH)
        allowed = kpos[...] <= qpos[...]
        total = jnp.zeros((N * R, DH), F32)
        for h in range(heads):
            scores = mm_nt(only(h, query).astype(BF16), keys)
            scores = jnp.where(allowed, scores, -1e30)
            raised = jnp.exp(scores - jnp.max(scores, axis=-1, keepdims=True))
            part = raised / jnp.sum(raised, axis=-1, keepdims=True)
            probs[i * heads + h] = part
            total = total + only(h, mm(part.astype(BF16), values))
        mixed[:, i] = total.astype(BF16).reshape(N, R, DH)

    def scatter(number, base, block, dealt):
        for d in dealt:
            b = near(y, d)
            term = block(b, d)
            if d:
                part_send[number, b] = term.astype(BF16)
                deal("y", part_send.at[number], part_recv.at[number], base, d)
            else:
                own[...] = term

    def collected(number, base):
        total = own[...]
        for d in order:
            arrived("y", part_recv.at[number], base, d)
            total = total + part_recv[number, near(y, d)].astype(F32)
        return total

    k_po = block_of()
    scatter(
        0, k_po, lambda b, d: mm(mixed[b].reshape(T, DH), wout_in[...]), order[::-1] + (0,)
    )
    state = start_values + (collected(0, k_po) + b_out)
    hidden[...] = state
    normal, _ = normalize(state)
    n2[y] = (normal * gain2 + shift2).astype(BF16)
    k_n2 = block_of()
    spread("y", n2, k_n2)

    own_wexp.wait()
    for d in order:
        arrived("y", wexp, k_wexp, d)

    def feed(b, d):
        if d:
            arrived("y", n2, k_n2, d)
        before = mm(n2[b], wexp[...].reshape(D, F)) + b_expand
        square = before * before
        bent = jnp.tanh(GELU_SCALE * (before + GELU_CUBE * (square * before)))
        half = 0.5 * (1.0 + bent)
        low = (before * half).astype(BF16)
        active[b] = low
        slope[b] = half + 0.5 * before * (1.0 - bent * bent) * (
            GELU_SCALE * (1.0 + 3.0 * GELU_CUBE * square)
        )
        return mm(low, wred_in[...])

    k_ff = block_of()
    scatter(1, k_ff, feed, (0,) + order)
    result = hidden[...] + (collected(1, k_ff) + b_reduce)
    y_low[...] = result.astype(BF16).reshape(S, R, D)
    start_if(s == 0, y_low, u_in, k_u, k_u, {"section": 1})
    start_if(turned, y_low, out_y, k_y, k_y, partner)
    own_y = pltpu.make_async_copy(y_low, out_y, lsem.at[2])
    pl.when(straight)(lambda: own_y.start())

    @pl.when(jnp.logical_and(s == 1, turned))
    def _():
        landed(cot_in, k_cot)

    @pl.when(s == 1)
    def _():
        grad[...] = cot_in[...].reshape(T, D)

    @pl.when(s == 0)
    def _():
        landed(gp_in, k_gp)
        grad[...] = gp_in[...].astype(F32)

    branch = grad[...].astype(BF16)
    g_all[y] = branch
    k_g = block_of()
    spread("y", g_all, k_g)
    sm_own[...] = jnp.zeros_like(sm_own)
    sm_own[5:6] = column_sums(branch)

    def feed_back(b, d):
        if d:
            arrived("y", g_all, k_g, d)
        low = (mm_nt(g_all[b], wred_in[...]) * slope[b]).astype(BF16)
        gb_all[b] = low
        return mm_nt(low, wexp[...].reshape(D, F))

    k_gf = block_of()
    scatter(2, k_gf, feed_back, (0,) + order)

    g_rows = g_all[...].reshape(N * T, D)
    gb_rows = gb_all[...].reshape(N * T, F)
    sm_own[10:11] = column_sums(gb_rows)
    ff1s[:, 1] = mm_tn(active[...].reshape(N * T, F), g_rows).astype(BF16).reshape(N, F // N, D)
    ff1s[:, 0] = mm_tn(n2[...].reshape(N * T, D), gb_rows).astype(BF16).reshape(N, DH, F)
    k_ff1 = block_of()
    for d in order:
        deal("x", ff1s, ff1r, k_ff1, d)

    grad_two = collected(2, k_gf)
    normal, factor = normalize(hidden[...])
    sm_own[2:3] = column_sums(grad_two * normal)
    sm_own[3:4] = column_sums(grad_two)
    grad_hidden = grad[...] + norm_back(grad_two, normal, factor, gain2)
    grad[...] = grad_hidden
    low = grad_hidden.astype(BF16)
    ga_all[y] = low
    k_ga = block_of()
    spread("y", ga_all, k_ga)
    sm_own[4:5] = column_sums(low)

    for d in (0,) + order:
        if d:
            arrived("y", ga_all, k_ga, d)
        b = near(y, d)
        gm_all[b] = mm_nt(ga_all[b], wout_in[...]).astype(BF16).reshape(S, R, DH)

    @pl.loop(0, S)
    def _(i):
        query = q_all[:, i].reshape(N * R, DH)
        keys = kv[:, 0, :, i].reshape(N * N * R, DH)
        values = kv[:, 1, :, i].reshape(N * N * R, DH)
        grad_mixed = gm_all[:, i].reshape(N * R, DH)
        dq = jnp.zeros((N * R, DH), F32)
        dk = jnp.zeros((N * N * R, DH), F32)
        dv = jnp.zeros((N * N * R, DH), F32)
        for h in range(heads):
            part = probs[i * heads + h]
            mixed_head = only(h, grad_mixed).astype(BF16)
            grad_probs = mm_nt(mixed_head, values)
            inner = jnp.sum(part * grad_probs, axis=-1, keepdims=True)
            grad_scores = (part * (grad_probs - inner)).astype(BF16)
            dq = dq + only(h, mm(grad_scores, keys))
            dk = dk + mm_tn(grad_scores, only(h, query).astype(BF16))
            dv = dv + mm_tn(part.astype(BF16), mixed_head)
        dq_all[:, i] = (dq.astype(BF16).astype(F32) * 0.125).astype(BF16).reshape(N, R, DH)
        dkv_send[:, 0, :, i] = dk.astype(BF16).reshape(N, N, R, DH)
        dkv_send[:, 1, :, i] = dv.astype(BF16).reshape(N, N, R, DH)

    k_dkv = block_of()
    for d in order:
        deal("x", dkv_send, dkv_recv, k_dkv, d)

    def summed(axis, sent, received, base):
        me = place[axis]
        total = sent[me].astype(F32)
        for d in order:
            arrived(axis, received, base, d)
            total = total + received[near(me, d)].astype(F32)
        return total

    def in_order(ref, base):
        for d in order:
            arrived("z", ref, base, d)
        total = ref[0].astype(F32)
        for other in range(1, N):
            total = total + ref[other].astype(F32)
        return total

    ao1s[...] = (
        mm_tn(mixed[...].reshape(N * T, DH), ga_all[...].reshape(N * T, D))
        .astype(BF16)
        .reshape(N, DH // N, D)
    )
    k_ao1 = block_of()
    for d in order:
        deal("x", ao1s, ao1r, k_ao1, d)
    ff2[z] = summed("x", ff1s, ff1r, k_ff1).astype(BF16)
    k_ff2 = block_of()
    spread("z", ff2, k_ff2)

    total = dkv_send[x].astype(F32)
    for d in order:
        arrived("x", dkv_recv, k_dkv, d)
        total = total + dkv_recv[near(x, d)].astype(F32)
    dk_all[...] = total[0].astype(BF16)
    dv_all[...] = total[1].astype(BF16)

    def project_back(b, d):
        return (
            mm_nt(dq_all[b].reshape(T, DH), w3[:, 0].reshape(D, DH))
            + mm_nt(dk_all[b].reshape(T, DH), w3[:, 1].reshape(D, DH))
            + mm_nt(dv_all[b].reshape(T, DH), w3[:, 2].reshape(D, DH))
        )

    k_gn = block_of()
    scatter(3, k_gn, project_back, order[::-1] + (0,))
    n1_rows = n1[...].reshape(N * T, D)
    for j, ref in enumerate((dq_all, dk_all, dv_all)):
        rows = ref[...].reshape(N * T, DH)
        if j == 0:
            sm_own[8:9, 0:DH] = column_sums(rows)
        if j == 2:
            sm_own[9:10, 0:DH] = column_sums(rows)
        aq1s[:, j] = mm_tn(n1_rows, rows).astype(BF16).reshape(N, DH, DH)
    k_aq1 = block_of()
    for d in order:
        deal("x", aq1s, aq1r, k_aq1, d)

    grad_normed = collected(3, k_gn)
    normal, factor = normalize(u_in[...].reshape(T, D).astype(F32))
    sm_own[0:1] = column_sums(grad_normed * normal)
    sm_own[1:2] = column_sums(grad_normed)
    grad_input = grad[...] + norm_back(grad_normed, normal, factor, gain1)
    dx_low[...] = grad_input.astype(BF16)
    start_if(s == 1, dx_low, gp_in, k_gp, k_gp, {"section": 0})
    dx_buf[...] = grad_input.reshape(S, R, D)
    start_if(turned, dx_buf, out_dx, k_dx, k_dx, partner)
    own_dx = pltpu.make_async_copy(dx_buf, out_dx, lsem.at[3])
    pl.when(straight)(lambda: own_dx.start())

    sm_y[y] = sm_own[0:8]
    k_smy = block_of()
    spread("y", sm_y, k_smy)

    k_wexp_out = block_of()
    k_wred_out = block_of()
    k_wqkv_out = block_of()
    k_wout_out = block_of()
    k_sends = [block_of() for _ in range(4)]
    locals_ = []

    def hand_rows(src, dst_of, base, send_base, slot):
        for d in order:
            other = near(x, d)
            start(src, dst_of(x), send_base + d, base + x, along("x", other))
        copy = pltpu.make_async_copy(src, dst_of(x), lsem.at[slot])
        copy.start()
        locals_.append((None, copy))

    def hand_across(src, dst_of, base, send_base, slot):
        home = y == x
        for d in range(N):
            other = near(x, d)
            device = {"ctx": z * N + other, "fsdp": x}
            if d:
                start(src, dst_of(y), send_base + d, base + y, device)
            else:
                start_if(jnp.logical_not(home), src, dst_of(y), send_base + d, base + y, device)
        copy = pltpu.make_async_copy(src, dst_of(y), lsem.at[slot])
        pl.when(home)(lambda: copy.start())
        locals_.append((home, copy))

    def wexp_slot(i):
        return out_wexp.at[:, pl.ds(pl.multiple_of(i * F, 128), F)]

    def wred_slot(i):
        return out_wred.at[i]

    def wqkv_slot(i):
        return out_wqkv.at[i]

    def wout_slot(i):
        return out_wout.at[i]

    ff3[...] = in_order(ff2, k_ff2).astype(BF16)
    hand_across(ff3.at[0], wexp_slot, k_wexp_out, k_sends[0], 4)
    hand_rows(ff3.at[1], wred_slot, k_wred_out, k_sends[1], 5)

    aq2[z] = summed("x", aq1s, aq1r, k_aq1).astype(BF16)
    k_aq2 = block_of()
    spread("z", aq2, k_aq2)
    ao2[z] = summed("x", ao1s, ao1r, k_ao1).astype(BF16)
    k_ao2 = block_of()
    spread("z", ao2, k_ao2)

    for d in order:
        arrived("y", sm_y, k_smy, d)
    rows = sm_y[0]
    for other in range(1, N):
        rows = rows + sm_y[other]
    sm_x[x, 0:8] = rows
    sm_x[x, 8:16] = sm_own[8:16]
    k_smx = block_of()
    spread("x", sm_x, k_smx)

    aq3[...] = in_order(aq2, k_aq2).astype(BF16)
    hand_across(aq3, wqkv_slot, k_wqkv_out, k_sends[2], 6)
    ao3[...] = in_order(ao2, k_ao2).astype(BF16)
    hand_rows(ao3, wout_slot, k_wout_out, k_sends[3], 7)

    for d in order:
        arrived("x", sm_x, k_smx, d)
    rows = sm_x[0]
    for other in range(1, N):
        rows = rows + sm_x[other]
    sm_z[z] = rows
    k_smz = block_of()
    spread("z", sm_z, k_smz)
    for d in order:
        arrived("z", sm_z, k_smz, d)
    rows = sm_z[0]
    for other in range(1, N):
        rows = rows + sm_z[other]
    out_small[...] = rows

    for d in order:
        landed(wred_slot(near(x, d)), k_wred_out + near(x, d))
        landed(wout_slot(near(x, d)), k_wout_out + near(x, d))
    for d in range(N):
        source = near(y, d)
        if d:
            landed(wexp_slot(source), k_wexp_out + source)
            landed(wqkv_slot(source), k_wqkv_out + source)
        else:
            @pl.when(x != y)
            def _():
                landed(wexp_slot(source), k_wexp_out + source)
                landed(wqkv_slot(source), k_wqkv_out + source)

    @pl.when(turned)
    def _():
        landed(out_y, k_y)
        landed(out_dx, k_dx)

    @pl.when(straight)
    def _():
        own_y.wait()
        own_dx.wait()

    for condition, copy in locals_:
        if condition is None:
            copy.wait()
        else:
            pl.when(condition)(functools.partial(copy.wait))
    for condition, copy in drains:
        if condition is None:
            copy.wait_send()
        else:
            pl.when(condition)(functools.partial(copy.wait_send))
    assert counter[0] <= SEMS


SEMS = 128


def shards(
    tokens, cotangent, block_order, first_gain, first_shift, w_query, b_query, w_key, w_value,
    b_value, w_out, b_out, second_gain, second_shift, w_expand, b_expand, w_reduce, b_reduce,
):
    N = lax.axis_size("fsdp")
    S, R, D = tokens.shape
    F = w_reduce.shape[1]
    DH = D // N
    T = S * R
    heads = DH // HEAD
    c = lax.axis_index("ctx")
    y = lax.axis_index("fsdp")
    x = lax.rem(c, N)
    block = R // 2

    places = block_order.reshape(N, N, 2, 1) * block + jnp.arange(block, dtype=jnp.int32)
    places = places.transpose(1, 0, 2, 3).reshape(N, N * R)
    qpos = lax.dynamic_index_in_dim(places, x, 0, keepdims=False).reshape(N * R, 1)
    kpos = places.reshape(1, N * N * R)

    wqkv = jnp.stack([w_query[0], w_key[0], w_value[0]])
    wqkv = wqkv.reshape(3, DH, N, DH).transpose(2, 0, 1, 3)
    six = jnp.concatenate(
        [first_gain, first_shift, second_gain, second_shift, b_out, b_reduce], axis=0
    ).astype(F32)
    vecs = lax.dynamic_update_slice(jnp.zeros((8, D), F32), six, (0, y * DH))
    biases = jnp.zeros((8, max(D, F)), F32)
    biases = biases.at[0:1, 0:DH].set(b_query.astype(F32))
    biases = biases.at[1:2, 0:DH].set(b_value.astype(F32))
    biases = biases.at[2:3, 0:F].set(b_expand.astype(F32))

    def shape(dims, dtype):
        return jax.ShapeDtypeStruct(dims, dtype)

    vmem = pl.BlockSpec(memory_space=pltpu.VMEM)
    hbm = pl.BlockSpec(memory_space=pl.ANY)
    V = pltpu.VMEM
    rows = (N, S, R, DH)
    outs = pl.pallas_call(
        functools.partial(kernel, N, S, R, D, F),
        out_shape=(
            shape((S, R, D), BF16),
            shape((S, R, D), F32),
            shape((N, 3, DH, DH), BF16),
            shape((N, DH // N, D), BF16),
            shape((DH, N * F), BF16),
            shape((N, F // N, D), BF16),
            shape((16, D), F32),
        ),
        in_specs=[vmem, vmem, hbm, vmem, hbm, vmem, vmem, vmem, vmem, vmem],
        out_specs=(hbm, hbm, hbm, hbm, hbm, hbm, vmem),
        scratch_shapes=[
            V((S, R, D), BF16), V((S, R, D), F32), V((T, D), BF16),
            V((S, R, D), BF16), V((S, R, D), F32), V((T, D), BF16), V((N, 8, D), F32),
            V((N, 3, DH, DH), BF16), V((N, DH, F), BF16),
            V((N, T, D), BF16), V((N, T, D), BF16), V((N, T, D), BF16), V((N, T, D), BF16),
            V((N, T, F), BF16), V((N, T, F), BF16), V((N, T, F), F32),
            V(rows, BF16), V((N, 2) + rows, BF16), V((S * heads, N * R, N * N * R), F32),
            V(rows, BF16), V(rows, BF16), V(rows, BF16), V(rows, BF16), V(rows, BF16),
            V((N, 2) + rows, BF16), V((N, 2) + rows, BF16),
            V((4, N, T, D), BF16), V((4, N, T, D), BF16), V((T, D), F32), V((T, D), F32),
            V((T, D), F32),
            V((N, 2, DH, D), BF16), V((N, 2, DH, D), BF16), V((N, 2, DH, D), BF16),
            V((2, DH, D), BF16),
            V((N, 3, DH, DH), BF16), V((N, 3, DH, DH), BF16), V((N, 3, DH, DH), BF16),
            V((3, DH, DH), BF16),
            V((N, DH // N, D), BF16), V((N, DH // N, D), BF16), V((N, DH // N, D), BF16),
            V((DH // N, D), BF16),
            V((N, 8, D), F32), V((N, 16, D), F32), V((N, 16, D), F32), V((16, D), F32),
            pltpu.SemaphoreType.DMA((SEMS,)),
            pltpu.SemaphoreType.DMA((SEMS,)),
            pltpu.SemaphoreType.DMA((8,)),
        ],
        compiler_params=pltpu.CompilerParams(
            collective_id=0, has_side_effects=True, vmem_limit_bytes=60 * 1024 * 1024
        ),
        name="layers",
    )(
        tokens, cotangent, wqkv, w_out[0], w_expand[0], w_reduce[0], vecs, biases, qpos, kpos
    )
    out_y, out_dx, g_qkv, g_out, g_exp, g_red, small = outs
    g_qkv = g_qkv.transpose(1, 2, 0, 3).reshape(3, DH, D).astype(F32)
    mine = lax.dynamic_slice(small, (0, y * DH), (6, DH))
    return (
        out_y[None],
        out_dx[None],
        mine[0:1],
        mine[1:2],
        g_qkv[0:1],
        small[8:9, 0:DH],
        g_qkv[1:2],
        g_qkv[2:3],
        small[9:10, 0:DH],
        g_out.reshape(1, DH, D).astype(F32),
        mine[4:5],
        mine[2:3],
        mine[3:4],
        g_exp.astype(F32)[None],
        small[10:11, 0:F],
        g_red.reshape(1, F, D).astype(F32),
        mine[5:6],
    )


def solution(mesh):
    vector = P("section", "fsdp")
    matrix = P("section", "fsdp", None)
    return jax.shard_map(
        shards,
        mesh=mesh,
        in_specs=(
            P("fsdp", "ctx", None), P("fsdp", "ctx", None), P(),
            vector, vector, matrix, vector, matrix, matrix, vector, matrix, vector, vector, vector,
            matrix, vector, matrix, vector,
        ),
        out_specs=(
            P("section", "fsdp", "ctx", None), P("section", "fsdp", "ctx", None),
            vector, vector, matrix, vector, matrix, matrix, vector, matrix, vector, vector, vector,
            matrix, vector, matrix, vector,
        ),
        check_vma=False,
    )
```

time: 1860 us -> 329 us (0.18)
  waiting for transfers between devices: 1350 us -> 0 us
  Pallas kernels: 0 us -> 299 us
  matrix products: 170 us -> 0 us
  blocking collectives: 120 us -> 0 us
  other arithmetic: 87.3 us -> 7.59 us
  local copies, waits for them, and re-layouts: 87.4 us -> 16.4 us
  between operations: 19.7 us -> 0.86 us
    reduce_scatter x18 -> x0, waiting for transfers between devices: 569 us -> none  [the longest x3 158 us: scatter_tick(): lax.psum_scatter(grads[13].astype(jnp.bfloat16), 'fsdp', scatter_dimensio...]
    all_gather x12 -> x0, waiting for transfers between devices: 402 us -> none  [the longest x3 126 us: forward(): lax.all_gather(keys, 'ctx', axis=0, tiled=True)]
    unnamed x43 -> x0, waiting for transfers between devices: 380 us -> none
    pallas_call x0 -> x1, Pallas kernels: none -> 299 us  [shards(): pl.pallas_call(functools.partial(kernel, N, S, R, D, F), out_shape=(shape...]
    dot_general x75 -> x0, matrix products: 170 us -> none  [the longest x18 49 us: transposed_left(): lax.dot_general(left, right, (((0,), (0,)), ((), ())), preferred_element_...]
    psum x1 -> x0, blocking collectives: 75.1 us -> none  [shards(): lax.psum(totals_all[0].astype(jnp.bfloat16), 'ctx').astype(jnp.float32)]
    unnamed x410 -> x22, local copies, waits for them, and re-layouts: 40.3 us -> 2.16 us
    unnamed x2 -> x0, blocking collectives: 33.3 us -> none
  transfers between devices with their start and end apart: 41 -> 0, of which waited for: 35 -> 0; matrix products, arithmetic and copies ran while one was open for 11% -> 0% of each run, Pallas kernels for 0% -> 0%
where the time goes in v1:
time: 329 us; the launch traced here: 324 us
  Pallas kernels  299 us (91%)
  local copies, waits for them, and re-layouts  16.4 us (5%)
  other arithmetic  7.59 us (2%)
    pallas_call x1, Pallas kernels, shards(): pl.pallas_call(functools.partial(kernel, N, S, R, D, F), out_shape=(shape...  299 us

profile of v1, /device:TPU:0, one launch (start us, length us, event | category | flops | bytes accessed | tf_op | source)
XLA Modules:
  0.0 323.6 jit_solution(7266003416525343193)
XLA Ops:
  0.7 0.7 broadcast_multiply_fusion
  1.3 0.1 mul.21
  1.5 0.1 add.56
  1.6 0.1 add.58
  1.7 0.8 copy.38.qpos
  2.5 0.8 concatenate.9
  3.3 0.5 dynamic_update_slice.3.vecs_in
  3.8 0.1 iota_add_fusion
  3.9 0.7 add.64.kpos
  4.6 1.2 pad_maximum_fusion
  5.8 1.0 reshape.198
  6.9 1.2 copy.43
  8.1 0.3 scatter.19
  8.4 0.1 scatter.20.biases
  8.5 0.6 copy-done.6
  9.1 298.8 %layers.1 = (bf16[2,64,768]{2,1,0:T(8,128)(2,1)}, f32[2,64,768]{2,1,0:T(8,128)}, bf16[4,3,192,192]{3,2,1,0:T(8,128)(2,1)}, bf16[4,48,768]{2,1,0:T(8,128)(2,1)}, ...) custom-call(bf16[2,64,768]{2,1,0:T(8,128)(2,1)} %tok.1, f32[2,64,768]{2,1,0:T(8,128)} %cot.1, ...), custom_call_target="tpu_custom_call" | custom-call | tf_op jit(solution)/shard_map/layers/pallas_call | solution.py:625
  307.9 1.6 fusion.2
  309.5 1.5 convert_bitcast_fusion
  311.0 0.2 fusion.1
  311.2 0.5 copy.39
  311.7 1.3 slice.108
  313.0 0.5 copy.40
  313.5 1.3 slice.111
  314.8 0.5 copy.41
  315.3 1.3 slice.113
  316.7 1.3 slice.118
  318.0 1.6 bitcast_convert_fusion
  319.6 0.1 copy-done
  319.7 1.7 bitcast_convert_fusion.1
  321.3 0.9 bitcast_convert_fusion.2
  322.2 0.7 copy.49
  322.9 0.7 copy.50
  (27 shorter events, 0.2 us)
Async XLA Ops:
  3.8 3.0 copy-start.5
  6.8 1.2 copy-start.8
  6.9 1.2 copy-start.9
  6.9 1.5 copy-start.7
  8.5 0.6 copy-start.6
  314.8 3.1 copy-start.1
  318.0 1.7 copy-start
  319.6 1.7 copy-start.3
  319.7 2.5 copy-start.4
  321.3 1.5 copy-start.2

commit v2 on v1

v2 whole, which is shorter than its diff:
```python
import functools

import jax
import jax.numpy as jnp
from jax import lax
from jax.experimental import pallas as pl
from jax.experimental.pallas import tpu as pltpu
from jax.sharding import PartitionSpec as P

HEAD = 64
EPSILON = 1e-05
F32 = jnp.float32
BF16 = jnp.bfloat16
MESH = pl.DeviceIdType.MESH
GELU_SCALE = 0.7978845608028654
GELU_CUBE = 0.044715
SEMS = 256


def mm(left, right):
    return jnp.dot(left, right, preferred_element_type=F32)


def mm_nt(left, right):
    return lax.dot_general(left, right, (((1,), (1,)), ((), ())), preferred_element_type=F32)


def mm_tn(left, right):
    return lax.dot_general(left, right, (((0,), (0,)), ((), ())), preferred_element_type=F32)


def normalize(values):
    average = jnp.mean(values, axis=-1, keepdims=True)
    centered = values - average
    variance = jnp.mean(centered * centered, axis=-1, keepdims=True)
    factor = lax.rsqrt(variance + EPSILON)
    return centered * factor, factor


def norm_back(grad, normal, factor, gain):
    scaled = grad * gain
    return factor * (
        scaled
        - jnp.mean(scaled, axis=-1, keepdims=True)
        - normal * jnp.mean(scaled * normal, axis=-1, keepdims=True)
    )


def column_sums(values):
    return jnp.sum(values.astype(F32), axis=0, keepdims=True)


def kernel(
    N, S, R, D, F,
    tok, cot, order_in, gain1_in, shift1_in, wq_in, bq_in, wk_in, wv_in, bv_in, wout_in, bout_in,
    gain2_in, shift2_in, wexp_in, bexp_in, wred_in, bred_in,
    out_y, out_dx, out_kv, out_q, out_out, out_wexp, out_wred, out_small,
    u_in, cot_in, gp_in, y_low, dx_buf, dx_low, pack, vecs, kpos, qpos,
    w_send, w_all, wexp, wred, wout, n1, n2, g_all, ga_all, gb_all, active, slope,
    q_all, kv, probs, mixed, gm_all, dq_all, dkv_all, acc_q, acc_kv, dkv_send, dkv_recv,
    part_send, part_recv, hidden, grad,
    ff_s, ff_r, ff_sum, qo_s, qo_r, qo_sum, kv_s, kv_r, kv_sum,
    sm_y, sm_c, sm_own,
    ssem, rsem, lsem, go,
):
    NN = N * N
    M = N * R
    DH = D // N
    W = 2 * DH // 3
    WQ, WKV = 2 * W, 3 * W
    heads = DH // HEAD
    s = lax.axis_index("section")
    c = lax.axis_index("ctx")
    y = lax.axis_index("fsdp")
    x = lax.rem(c, N)
    z = lax.div(c, N)
    straight = y == z
    turned = y != z
    order = tuple(sorted(range(1, N), key=lambda d: min(d, N - d)))
    streams = range(S)
    sibling = {"section": 1 - s}
    partner = {"ctx": y * N + x, "fsdp": z}

    def near(v, d):
        return lax.rem(v + d, N)

    def near_ctx(d):
        return lax.rem(c + d, NN)

    counter = [0]

    def block_of(count=N):
        counter[0] += count
        assert counter[0] <= SEMS
        return counter[0] - count

    drains = []

    def remote(src, dst, send, recv, device):
        return pltpu.make_async_remote_copy(
            src_ref=src, dst_ref=dst, send_sem=ssem.at[send], recv_sem=rsem.at[recv],
            device_id=device, device_id_type=MESH,
        )

    def start(src, dst, send, recv, device):
        copy = remote(src, dst, send, recv, device)
        copy.start()
        drains.append(copy.wait_send)

    def start_if(condition, src, dst, send, recv, device):
        copy = remote(src, dst, send, recv, device)
        pl.when(condition)(lambda: copy.start())
        drains.append(lambda: pl.when(condition)(lambda: copy.wait_send()))

    def start_each(count, make):
        @pl.loop(1, count)
        def _(d):
            make(d).start()

        def drain():
            @pl.loop(1, count)
            def _(d):
                make(d).wait_send()

        drains.append(drain)

    def landed(dst, recv):
        remote(dst, dst, 0, recv, sibling).wait_recv()

    def local_if(condition, src, dst, slot):
        copy = pltpu.make_async_copy(src, dst, lsem.at[slot])
        pl.when(condition)(lambda: copy.start())
        return lambda: pl.when(condition)(lambda: copy.wait())

    def local(src, dst, slot):
        copy = pltpu.make_async_copy(src, dst, lsem.at[slot])
        copy.start()
        return copy.wait

    def along(axis, index):
        if axis == "y":
            return {"fsdp": index}
        return {"ctx": z * N + index}

    place = {"x": x, "y": y}

    def spread(axis, ref, base):
        me = place[axis]
        for d in order:
            start(ref.at[me], ref.at[me], base + d, base + me, along(axis, near(me, d)))

    def arrived(axis, ref, base):
        for d in order:
            source = near(place[axis], d)
            landed(ref.at[source], base + source)

    def deal(axis, src, dst, base):
        me = place[axis]
        for d in order:
            other = near(me, d)
            start(src.at[other], dst.at[me], base + d, base + me, along(axis, other))

    barrier = pltpu.get_barrier_semaphore()

    @pl.loop(1, NN * N)
    def _(d):
        index = lax.rem(c * N + y + d, NN * N)
        pl.semaphore_signal(
            barrier, inc=1, device_id={"ctx": lax.div(index, N), "fsdp": lax.rem(index, N)},
            device_id_type=MESH,
        )

    pl.semaphore_signal(barrier, inc=1, device_id=sibling, device_id_type=MESH)
    wait_wred = local(wred_in, wred, 0)
    wait_wout = local(wout_in, wout.at[pl.ds(WQ - DH, DH)], 1)
    pl.semaphore_wait(barrier, NN * N)

    k_u = block_of(S)
    k_gp = block_of(S)
    k_cot, k_y, k_dx = (block_of(1) for _ in range(3))
    wait_u = []
    for i in streams:
        start_if(
            jnp.logical_and(s == 0, turned), tok.at[i], u_in.at[i], k_u + i, k_u + i, partner
        )
        wait_u.append(
            local_if(jnp.logical_and(s == 0, straight), tok.at[i], u_in.at[i], 2 + i)
        )

    pack[...] = jnp.zeros_like(pack)
    for j, ref in enumerate((gain1_in, shift1_in, gain2_in, shift2_in, bout_in, bred_in)):
        pack[j : j + 1] = ref[...].astype(F32)
    put = (
        lax.broadcasted_iota(jnp.int32, (DH, D), 0) + y * DH
        == lax.broadcasted_iota(jnp.int32, (DH, D), 1)
    )
    vecs[y] = mm(pack[...].astype(BF16), jnp.where(put, 1.0, 0.0).astype(BF16))[0:8]
    k_vecs = block_of()
    spread("y", vecs, k_vecs)

    def picker(width, shift, first):
        row = lax.broadcasted_iota(jnp.int32, (WQ, width), 0)
        col = lax.broadcasted_iota(jnp.int32, (WQ, width), 1)
        inside = jnp.logical_and(col >= first, col < first + DH)
        return jnp.where(
            jnp.logical_and(row - shift == col - first, inside), 1.0, 0.0
        ).astype(BF16)

    for b in range(N):
        lane = b * DH // W * W
        cut = slice(lane, lane + WQ)
        shift = b * DH - lane
        w_send[b, :, 0:WKV] = (
            mm(wk_in[:, cut], picker(WKV, shift, 0)) + mm(wv_in[:, cut], picker(WKV, shift, DH))
        ).astype(BF16)
        w_send[b, :, WKV : WKV + WQ] = mm(wq_in[:, cut], picker(WQ, shift, 0)).astype(BF16)
    w_all[y] = w_send[y]

    @pl.when(s == 1)
    def _():
        pl.semaphore_wait(go, 1)

    k_w = block_of()
    deal("y", w_send, w_all, k_w)

    blocks = 2 * NN
    half = R // 2
    slot = lax.broadcasted_iota(jnp.int32, (1, blocks * half), 1)
    found = jnp.zeros_like(slot)
    for b in range(blocks):
        xb, yb, side = b // (2 * N), b // 2 % N, b % 2
        found = jnp.where(slot >= b * half, order_in[2 * (yb * N + xb) + side] * half - b * half, found)
    kpos[...] = found + slot
    slot = lax.broadcasted_iota(jnp.int32, (M, 1), 0)
    found = jnp.zeros_like(slot)
    for b in range(2 * N):
        found = jnp.where(
            slot >= b * half, order_in[2 * ((b // 2) * N + x) + b % 2] * half - b * half, found
        )
    qpos[...] = found + slot

    arrived("y", vecs, k_vecs)
    params = vecs[0]
    for other in range(1, N):
        params = params + vecs[other]
    gain1, shift1, gain2, shift2, b_out, b_reduce = (params[j : j + 1] for j in range(6))
    lanes = lax.broadcasted_iota(jnp.int32, (1, WQ), 1)

    k_n1 = [block_of() for _ in streams]
    for i in streams:
        @pl.when(jnp.logical_or(s == 1, turned))
        def _():
            landed(u_in.at[i], k_u + i)

        wait_u[i]()
        normal, _ = normalize(u_in[i].astype(F32))
        n1[i, y] = (normal * gain1 + shift1).astype(BF16)
        spread("y", n1.at[i], k_n1[i])

    k_wexp = block_of()

    def wexp_cut(b):
        return wexp_in.at[:, pl.ds(pl.multiple_of(b * F, 128), F)]

    wait_wexp = local(wexp_cut(y), wexp.at[y], 4)
    for d in order:
        other = near(y, d)
        start(wexp_cut(other), wexp.at[y], k_wexp + d, k_wexp + y, along("y", other))
    start_if(jnp.logical_and(s == 1, turned), cot, cot_in, k_cot, k_cot, partner)
    wait_cot = local_if(jnp.logical_and(s == 1, straight), cot, cot_in, 5)

    k_kv = [block_of() for _ in streams]
    arrived("y", w_all, k_w)
    for i in streams:
        arrived("y", n1.at[i], k_n1[i])
        rows = n1[i].reshape(M, D)
        made = mm(rows, w_all[:, :, 0:WKV].reshape(D, WKV))
        made_low = made[:, 0 : 2 * DH]
        kv[i, x] = made_low.astype(BF16)
        kv[i, x, :, W:WKV] = (
            made[:, W:WKV] + bias_at(bv_in, W, WQ, DH)
        ).astype(BF16)
        spread("x", kv.at[i], k_kv[i])
        query = mm(rows, w_all[:, :, WKV : WKV + WQ].reshape(D, WQ)) + bias_at(bq_in, 0, WQ, 0)
        q_all[i] = (query * 0.125).astype(BF16)

    @pl.when(s == 0)
    def _():
        pl.semaphore_signal(go, inc=1, device_id=sibling, device_id_type=MESH)

    def only(h, values, first):
        inside = jnp.logical_and(lanes >= first + h * HEAD, lanes < first + (h + 1) * HEAD)
        return jnp.where(inside, values.astype(F32), 0.0)

    def scatter(number, i, term, base):
        part_send[number, i] = term.astype(BF16).reshape(N, R, D)
        deal("y", part_send.at[number, i], part_recv.at[number, i], base)

    def collected(number, i, base):
        total = part_send[number, i, y].astype(F32)
        arrived("y", part_recv.at[number, i], base)
        for d in order:
            total = total + part_recv[number, i, near(y, d)].astype(F32)
        return total

    wout[0 : WQ - DH] = jnp.zeros((WQ - DH, D), BF16)
    wait_wout()
    k_po = [block_of() for _ in streams]
    for i in streams:
        arrived("x", kv.at[i], k_kv[i])
        allowed = kpos[...] <= qpos[...]
        acc_q[...] = jnp.zeros_like(acc_q)

        @pl.loop(0, heads)
        def _(h):
            keys = kv[i, :, :, 0:WQ].reshape(N * M, WQ)
            values = kv[i, :, :, W:WKV].reshape(N * M, WQ)
            scores = mm_nt(only(h, q_all[i], 0).astype(BF16), keys)
            scores = jnp.where(allowed, scores, -1e30)
            raised = jnp.exp(scores - jnp.max(scores, axis=-1, keepdims=True))
            part = raised / jnp.sum(raised, axis=-1, keepdims=True)
            probs[i * heads + h] = part
            acc_q[...] += only(h, mm(part.astype(BF16), values), WQ - DH)

        low = acc_q[...].astype(BF16)
        mixed[i] = low
        scatter(0, i, mm(low, wout[...]), k_po[i])

    k_n2 = [block_of() for _ in streams]
    for i in streams:
        state = u_in[i].astype(F32) + (collected(0, i, k_po[i]) + b_out)
        hidden[i] = state
        normal, _ = normalize(state)
        n2[i, y] = (normal * gain2 + shift2).astype(BF16)
        spread("y", n2.at[i], k_n2[i])

    wait_wexp()
    wait_wred()
    arrived("y", wexp, k_wexp)
    k_ff = [block_of() for _ in streams]
    for i in streams:
        arrived("y", n2.at[i], k_n2[i])
        before = mm(n2[i].reshape(M, D), wexp[...].reshape(D, F)) + bexp_in[...].astype(F32)
        square = before * before
        bent = jnp.tanh(GELU_SCALE * (before + GELU_CUBE * (square * before)))
        side = 0.5 * (1.0 + bent)
        low = (before * side).astype(BF16)
        active[i] = low
        slope[i] = side + 0.5 * before * (1.0 - bent * bent) * (
            GELU_SCALE * (1.0 + 3.0 * GELU_CUBE * square)
        )
        scatter(1, i, mm(low, wred[...]), k_ff[i])

    for i in streams:
        result = hidden[i] + (collected(1, i, k_ff[i]) + b_reduce)
        y_low[i] = result.astype(BF16)
        start_if(s == 0, y_low.at[i], u_in.at[i], k_u + i, k_u + i, sibling)

    @pl.when(jnp.logical_and(s == 1, turned))
    def _():
        landed(cot_in, k_cot)

    wait_cot()
    sm_own[...] = jnp.zeros_like(sm_own)
    k_g = [block_of() for _ in streams]
    for i in streams:
        @pl.when(s == 1)
        def _():
            grad[i] = cot_in[i]

        @pl.when(s == 0)
        def _():
            landed(gp_in.at[i], k_gp + i)
            grad[i] = gp_in[i].astype(F32)

        low = grad[i].astype(BF16)
        g_all[i, y] = low
        spread("y", g_all.at[i], k_g[i])
        sm_own[5:6] += column_sums(low)

    start_if(turned, y_low, out_y, k_y, k_y, partner)
    wait_y = local_if(straight, y_low, out_y, 6)

    k_gf = [block_of() for _ in streams]
    for i in streams:
        arrived("y", g_all.at[i], k_g[i])
        low = (mm_nt(g_all[i].reshape(M, D), wred[...]) * slope[i]).astype(BF16)
        gb_all[i] = low
        scatter(2, i, mm_nt(low, wexp[...].reshape(D, F)), k_gf[i])

    def turn(index):
        return lax.rem(lax.rem(index, N) + lax.div(index, N), N)

    def piece(index):
        return turn(index) * N + lax.div(index, N)

    mine = piece(c)

    def pool(src, dst, base):
        dst[c] = src[mine]

        def make(d):
            other = near_ctx(d)
            return remote(src.at[piece(other)], dst.at[c], base + d, base + c, {"ctx": other})

        start_each(NN, make)

    def pooled(dst, base):
        @pl.loop(1, NN)
        def _(d):
            landed(dst.at[near_ctx(d)], base + near_ctx(d))

        total = dst[0].astype(F32)
        for other in range(1, NN):
            total = total + dst[other].astype(F32)
        return total

    g_rows = g_all[...].reshape(S * M, D)
    gb_rows = gb_all[...].reshape(S * M, F)
    sm_own[10:11] = column_sums(gb_rows)
    ff_s[:, 1] = mm_tn(active[...].reshape(S * M, F), g_rows).astype(BF16).reshape(NN, F // NN, D)
    ff_s[:, 0] = mm_tn(n2[...].reshape(S * M, D), gb_rows).astype(BF16).reshape(NN, D // NN, F)
    k_ffp = block_of(NN)
    pool(ff_s, ff_r, k_ffp)

    k_ga = [block_of() for _ in streams]
    for i in streams:
        grad_two = collected(2, i, k_gf[i])
        normal, factor = normalize(hidden[i])
        grad_hidden = grad[i] + norm_back(grad_two, normal, factor, gain2)
        grad[i] = grad_hidden
        low = grad_hidden.astype(BF16)
        ga_all[i, y] = low
        spread("y", ga_all.at[i], k_ga[i])
        sm_own[2:3] += column_sums(grad_two * normal)
        sm_own[3:4] += column_sums(grad_two)
        sm_own[4:5] += column_sums(low)

    k_dkv = [block_of() for _ in streams]
    for i in streams:
        arrived("y", ga_all.at[i], k_ga[i])
        gm_all[i] = mm_nt(ga_all[i].reshape(M, D), wout[...]).astype(BF16)
        acc_q[...] = jnp.zeros_like(acc_q)
        acc_kv[...] = jnp.zeros_like(acc_kv)

        @pl.loop(0, heads)
        def _(h):
            keys = kv[i, :, :, 0:WQ].reshape(N * M, WQ)
            values = kv[i, :, :, W:WKV].reshape(N * M, WQ)
            part = probs[i * heads + h]
            mixed_head = only(h, gm_all[i], WQ - DH).astype(BF16)
            grad_probs = mm_nt(mixed_head, values)
            inner = jnp.sum(part * grad_probs, axis=-1, keepdims=True)
            grad_scores = (part * (grad_probs - inner)).astype(BF16)
            acc_q[...] += only(h, mm(grad_scores, keys), 0)
            acc_kv[:, 0:WQ] += mm_tn(grad_scores, only(h, q_all[i], 0).astype(BF16))
            acc_kv[:, W:WKV] += mm_tn(part.astype(BF16), mixed_head)

        dkv_send[i] = acc_kv[...].astype(BF16).reshape(N, M, WKV)
        deal("x", dkv_send.at[i], dkv_recv.at[i], k_dkv[i])
        dq_all[i] = (acc_q[...].astype(BF16).astype(F32) * 0.125).astype(BF16)

    n1_rows = n1[...].reshape(S * M, D)
    dq_rows = dq_all[...].reshape(S * M, WQ)
    sm_own[8:9, 0:DH] = column_sums(dq_rows)[:, 0:DH]
    grad_q = mm_tn(n1_rows, dq_rows)
    grad_o = mm_tn(ga_all[...].reshape(S * M, D), mixed[...].reshape(S * M, WQ))
    qo_s[:, :, 0:W] = grad_q[:, 0:W].astype(BF16).reshape(NN, D // NN, W)
    qo_s[:, :, W:WQ] = (grad_q[:, W:WQ] + grad_o[:, 0:W]).astype(BF16).reshape(NN, D // NN, W)
    qo_s[:, :, WQ:WKV] = grad_o[:, W:WQ].astype(BF16).reshape(NN, D // NN, W)
    k_qop = block_of(NN)
    pool(qo_s, qo_r, k_qop)

    home = turn(c) == y
    finals = []
    late = []

    def hand_rows(src, dst, slot):
        base = block_of(NN)

        def make(d):
            return remote(src, dst(mine), base + d, base + c, {"ctx": near_ctx(d)})

        start_each(NN, make)
        late.append(local(src, dst(mine), slot))

        def finish():
            @pl.loop(1, NN)
            def _(d):
                landed(dst(piece(near_ctx(d))), base + near_ctx(d))

        finals.append(finish)

    def hand_across(src, dst, slot):
        base = block_of(NN)
        owner = turn(c)

        def make(d):
            return remote(
                src, dst(z, y), base + d, base + z * N + y,
                {"ctx": near_ctx(d), "fsdp": owner},
            )

        start_each(NN, make)
        start_if(
            jnp.logical_not(home), src, dst(z, y), base, base + z * N + y,
            {"ctx": c, "fsdp": owner},
        )
        late.append(local_if(home, src, dst(z, y), slot))

        def finish():
            @pl.loop(0, NN)
            def _(index):
                sub = lax.div(index, N)
                source = lax.rem(index, N)
                own = jnp.logical_and(jnp.logical_and(home, sub == z), source == y)

                @pl.when(jnp.logical_not(own))
                def _():
                    landed(dst(sub, source), base + index)

        finals.append(finish)

    def lane_block(ref, width):
        return lambda sub, source: ref.at[
            sub, :, pl.ds(pl.multiple_of(source * width, 128), width)
        ]

    ff_sum[...] = pooled(ff_r, k_ffp).astype(BF16)
    hand_across(ff_sum.at[0], lane_block(out_wexp, F), 7)
    hand_rows(ff_sum.at[1], lambda index: out_wred.at[index], 8)

    k_gn = [block_of() for _ in streams]
    for i in streams:
        total = dkv_send[i, x].astype(F32)
        arrived("x", dkv_recv.at[i], k_dkv[i])
        for d in order:
            total = total + dkv_recv[i, near(x, d)].astype(F32)
        low = total.astype(BF16)
        dkv_all[i] = low
        scatter(
            3, i,
            mm_nt(dq_all[i], w_all[:, :, WKV : WKV + WQ].reshape(D, WQ))
            + mm_nt(low, w_all[:, :, 0:WKV].reshape(D, WKV)),
            k_gn[i],
        )

    dkv_rows = dkv_all[...].reshape(S * M, WKV)
    sm_own[9:10, 0:WKV] = column_sums(dkv_rows)
    kv_s[...] = mm_tn(n1_rows, dkv_rows).astype(BF16).reshape(NN, D // NN, WKV)
    k_kvp = block_of(NN)
    pool(kv_s, kv_r, k_kvp)

    for i in streams:
        grad_normed = collected(3, i, k_gn[i])
        normal, factor = normalize(u_in[i].astype(F32))
        grad_input = grad[i] + norm_back(grad_normed, normal, factor, gain1)
        dx_low[i] = grad_input.astype(BF16)
        start_if(s == 1, dx_low.at[i], gp_in.at[i], k_gp + i, k_gp + i, sibling)
        dx_buf[i] = grad_input
        sm_own[0:1] += column_sums(grad_normed * normal)
        sm_own[1:2] += column_sums(grad_normed)

    sm_y[y] = sm_own[0:8]
    k_smy = block_of()
    spread("y", sm_y, k_smy)
    start_if(turned, dx_buf, out_dx, k_dx, k_dx, partner)
    wait_dx = local_if(straight, dx_buf, out_dx, 9)

    qo_sum[...] = pooled(qo_r, k_qop).astype(BF16)
    hand_across(qo_sum.at[:, 0:WQ], lane_block(out_q, WQ), 10)
    hand_rows(qo_sum.at[:, W:WKV], lambda index: out_out.at[index], 11)

    arrived("y", sm_y, k_smy)
    rows = sm_y[0]
    for other in range(1, N):
        rows = rows + sm_y[other]
    sm_c[c, 0:8] = rows
    sm_c[c, 8:16] = sm_own[8:16]
    k_smc = block_of(NN)
    start_each(
        NN,
        lambda d: remote(sm_c.at[c], sm_c.at[c], k_smc + d, k_smc + c, {"ctx": near_ctx(d)}),
    )

    kv_sum[...] = pooled(kv_r, k_kvp).astype(BF16)
    hand_across(kv_sum, lane_block(out_kv, WKV), 12)

    @pl.loop(1, NN)
    def _(d):
        landed(sm_c.at[near_ctx(d)], k_smc + near_ctx(d))

    rows = sm_c[0]
    for other in range(1, NN):
        rows = rows + sm_c[other]
    out_small[...] = rows

    for finish in finals:
        finish()

    @pl.when(turned)
    def _():
        landed(out_y, k_y)
        landed(out_dx, k_dx)

    for wait in [wait_y, wait_dx] + late:
        wait()
    for drain in drains:
        drain()


def bias_at(ref, lane, width, first):
    size = ref.shape[1]
    row = lax.broadcasted_iota(jnp.int32, (size, width), 0)
    col = lax.broadcasted_iota(jnp.int32, (size, width), 1)
    put = jnp.where(row + first == col + lane, 1.0, 0.0).astype(BF16)
    wide = jnp.broadcast_to(ref[...].astype(F32), (16, size)).astype(BF16)
    return mm(wide, put)[0:1]


def shards(
    tokens, cotangent, block_order, first_gain, first_shift, w_query, b_query, w_key, w_value,
    b_value, w_out, b_out, second_gain, second_shift, w_expand, b_expand, w_reduce, b_reduce,
):
    N = lax.axis_size("fsdp")
    S, R, D = tokens.shape
    F = w_reduce.shape[1]
    DH = D // N
    W = 2 * DH // 3
    WQ, WKV = 2 * W, 3 * W
    NN, M = N * N, N * R
    heads = DH // HEAD
    y = lax.axis_index("fsdp")

    def shape(dims, dtype):
        return jax.ShapeDtypeStruct(dims, dtype)

    vmem = pl.BlockSpec(memory_space=pltpu.VMEM)
    smem = pl.BlockSpec(memory_space=pltpu.SMEM)
    hbm = pl.BlockSpec(memory_space=pl.ANY)
    V = pltpu.VMEM
    slab = V((S, N, R, D), BF16)
    outs = pl.pallas_call(
        functools.partial(kernel, N, S, R, D, F),
        out_shape=(
            shape((S, R, D), BF16),
            shape((S, R, D), F32),
            shape((N, D // NN, N * WKV), BF16),
            shape((N, D // NN, N * WQ), BF16),
            shape((NN, D // NN, WQ), BF16),
            shape((N, D // NN, N * F), BF16),
            shape((NN, F // NN, D), BF16),
            shape((16, D), F32),
        ),
        in_specs=[
            hbm, hbm, smem, vmem, vmem, vmem, vmem, vmem, vmem, vmem, hbm, vmem, vmem, vmem, hbm,
            vmem, hbm, vmem,
        ],
        out_specs=(hbm, hbm, hbm, hbm, hbm, hbm, hbm, vmem),
        scratch_shapes=[
            V((S, R, D), BF16), V((S, R, D), F32), V((S, R, D), BF16), V((S, R, D), BF16),
            V((S, R, D), F32), V((S, R, D), BF16), V((16, DH), F32), V((N, 8, D), F32),
            V((1, N * M), jnp.int32), V((M, 1), jnp.int32),
            V((N, DH, WKV + WQ), BF16), V((N, DH, WKV + WQ), BF16), V((N, DH, F), BF16),
            V((F, D), BF16), V((WQ, D), BF16),
            slab, slab, slab, slab,
            V((S, M, F), BF16), V((S, M, F), BF16), V((S, M, F), F32),
            V((S, M, WQ), BF16), V((S, N, M, WKV), BF16), V((S * heads, M, N * M), F32),
            V((S, M, WQ), BF16), V((S, M, WQ), BF16), V((S, M, WQ), BF16), V((S, M, WKV), BF16),
            V((M, WQ), F32), V((N * M, WKV), F32),
            V((S, N, M, WKV), BF16), V((S, N, M, WKV), BF16),
            V((4, S, N, R, D), BF16), V((4, S, N, R, D), BF16), V((S, R, D), F32),
            V((S, R, D), F32),
            V((NN, 2, D // NN, D), BF16), V((NN, 2, D // NN, D), BF16), V((2, D // NN, D), BF16),
            V((NN, D // NN, WKV), BF16), V((NN, D // NN, WKV), BF16), V((D // NN, WKV), BF16),
            V((NN, D // NN, WKV), BF16), V((NN, D // NN, WKV), BF16), V((D // NN, WKV), BF16),
            V((N, 8, D), F32), V((NN, 16, D), F32), V((16, D), F32),
            pltpu.SemaphoreType.DMA((SEMS,)),
            pltpu.SemaphoreType.DMA((SEMS,)),
            pltpu.SemaphoreType.DMA((16,)),
            pltpu.SemaphoreType.REGULAR,
        ],
        compiler_params=pltpu.CompilerParams(
            collective_id=0, has_side_effects=True, vmem_limit_bytes=60 * 1024 * 1024
        ),
        name="layers",
    )(
        tokens, cotangent, block_order, first_gain, first_shift, w_query[0], b_query, w_key[0],
        w_value[0], b_value, w_out[0], b_out, second_gain, second_shift, w_expand[0], b_expand,
        w_reduce[0], b_reduce,
    )
    out_y, out_dx, g_kv, g_q, g_out, g_exp, g_red, small = outs
    g_kv = g_kv.reshape(DH, N, WKV)
    g_q = g_q.reshape(DH, N, WQ)

    def whole(part):
        return part.astype(F32).reshape(1, DH, D)

    mine = lax.dynamic_slice(small, (0, y * DH), (6, DH))
    return (
        out_y[None],
        out_dx[None],
        mine[0:1],
        mine[1:2],
        whole(g_q[:, :, 0:DH]),
        small[8:9, 0:DH],
        whole(g_kv[:, :, 0:DH]),
        whole(g_kv[:, :, DH:WKV]),
        small[9:10, DH:WKV],
        g_out.reshape(D, WQ)[:, WQ - DH :].T.astype(F32)[None],
        mine[4:5],
        mine[2:3],
        mine[3:4],
        g_exp.reshape(1, DH, N * F).astype(F32),
        small[10:11, 0:F],
        g_red.reshape(1, F, D).astype(F32),
        mine[5:6],
    )


def solution(mesh):
    vector = P("section", "fsdp")
    matrix = P("section", "fsdp", None)
    return jax.shard_map(
        shards,
        mesh=mesh,
        in_specs=(
            P("fsdp", "ctx", None), P("fsdp", "ctx", None), P(),
            vector, vector, matrix, vector, matrix, matrix, vector, matrix, vector, vector, vector,
            matrix, vector, matrix, vector,
        ),
        out_specs=(
            P("section", "fsdp", "ctx", None), P("section", "fsdp", "ctx", None),
            vector, vector, matrix, vector, matrix, matrix, vector, matrix, vector, vector, vector,
            matrix, vector, matrix, vector,
        ),
        check_vma=False,
    )
```

time: 329 us -> 270 us (0.82); the launches traced: 324 us -> 270 us
  Pallas kernels: 299 us -> 254 us
  local copies, waits for them, and re-layouts: 16.4 us -> 10.6 us
    pallas_call x1, Pallas kernels: 299 us -> 254 us  [shards(): pl.pallas_call(functools.partial(kernel, N, S, R, D, F), out_shape=(shape...]
    slice x7 -> x1, local copies, waits for them, and re-layouts: 5.6 us -> 0.18 us  [shards(): g_out.reshape(D, WQ)[:, WQ - DH:].T.astype(F32)[None]]
where the time goes in v2:
time: 270 us
  Pallas kernels  254 us (94%)
  local copies, waits for them, and re-layouts  10.6 us (4%)
  other arithmetic  4.54 us (2%)
    pallas_call x1, Pallas kernels, shards(): pl.pallas_call(functools.partial(kernel, N, S, R, D, F), out_shape=(shape...  254 us

profile of v2, /device:TPU:0, one launch (start us, length us, event | category | flops | bytes accessed | tf_op | source)
XLA Modules:
  0.0 270.1 jit_solution(18308033304941955013)
XLA Ops:
  0.7 254.2 %layers.1 = (bf16[2,64,768]{2,1,0:T(8,128)(2,1)}, f32[2,64,768]{2,1,0:T(8,128)}, bf16[4,48,1536]{2,1,0:T(8,128)(2,1)}, bf16[4,48,1024]{2,1,0:T(8,128)(2,1)}, bf1...) custom-call(bf16[2,64,768]{2,1,0:T(8,128)(2,1)} %tok.1, ...), custom_call_target="tpu_custom_call" | custom-call | tf_op jit(solution)/shard_map/layers/pallas_call | solution.py:643
  254.9 1.6 fusion
  256.5 1.6 reshape.94
  258.1 0.3 slice_convert_fusion
  258.4 0.0 copy-start.1
  258.4 1.3 reshape.103
  259.7 1.3 reshape.105
  261.0 1.3 slice.50
  262.4 0.0 copy-done.1
  262.4 0.0 copy-start
  262.4 1.6 bitcast_convert_fusion
  263.9 0.1 copy-done
  264.0 0.0 copy-start.4
  264.0 1.7 bitcast_convert_fusion.1
  265.7 0.0 copy-done.4
  265.7 0.3 reshape.91
  266.0 0.0 copy-start.3
  266.0 0.1 slice_convert_fusion.2
  266.1 1.3 reshape.101
  267.4 0.0 copy-done.3
  267.4 0.0 copy-start.5
  267.4 0.2 slice.55
  267.6 0.0 copy-start.2
  267.6 0.2 copy.36
  267.8 0.9 convert_bitcast_fusion
  268.6 0.0 copy-done.5
  268.6 0.7 copy.39
  269.3 0.0 copy-done.2
  269.3 0.7 copy.40
Async XLA Ops:
  258.4 3.9 %copy-start.1 = (bf16[16,48,768]{2,1,0:T(8,128)(2,1)S(1)}, bf16[16,48,768]{2,1,0:T(8,128)(2,1)}, u32[]{:S(2)}) copy-start(bf16[16,48,768]{2,1,0:T(8,128)(2,1)} %get-tuple-element.32) | copy-start | bytes 3538948
  262.4 1.7 copy-start
  264.0 1.7 copy-start.4
  266.0 1.4 copy-start.3
  267.4 1.2 copy-start.5
  267.6 1.7 copy-start.2

commit v3 on v2

v3 whole, which is shorter than its diff:
```python
import functools

import jax
import jax.numpy as jnp
from jax import lax
from jax.experimental import pallas as pl
from jax.experimental.pallas import tpu as pltpu
from jax.sharding import PartitionSpec as P

HEAD = 64
EPSILON = 1e-05
F32 = jnp.float32
BF16 = jnp.bfloat16
MESH = pl.DeviceIdType.MESH
GELU_SCALE = 0.7978845608028654
GELU_CUBE = 0.044715
SEMS = 448


def mm(left, right):
    return jnp.dot(left, right, preferred_element_type=F32)


def mm_nt(left, right):
    return lax.dot_general(left, right, (((1,), (1,)), ((), ())), preferred_element_type=F32)


def mm_tn(left, right):
    return lax.dot_general(left, right, (((0,), (0,)), ((), ())), preferred_element_type=F32)


def normalize(values):
    average = jnp.mean(values, axis=-1, keepdims=True)
    centered = values - average
    variance = jnp.mean(centered * centered, axis=-1, keepdims=True)
    factor = lax.rsqrt(variance + EPSILON)
    return centered * factor, factor


def norm_back(grad, normal, factor, gain):
    scaled = grad * gain
    return factor * (
        scaled
        - jnp.mean(scaled, axis=-1, keepdims=True)
        - normal * jnp.mean(scaled * normal, axis=-1, keepdims=True)
    )


def column_sums(values):
    return jnp.sum(values.astype(F32), axis=0, keepdims=True)


def kernel(
    N, J, Q, D, F,
    tok, cot, order_in, rows_in, bexp_in, wq_in, wk_in, wv_in, wout_in, wexp_in, wred_in,
    out_y, out_dx, out_kv, out_q, out_out, out_wexp, out_wred, out_small,
    u_in, cot_in, gp_in, y_low, dx_buf, dx_low, vecs, kpos, qpos,
    wq, wk, wv, w_send, w_all, wexp, wred, wout, n1, n2, g_all, ga_all, gb_all, active, slope,
    q_all, kv, probs, mixed, gm_all, dq_all, dkv_all, dkv_send, dkv_recv,
    part_send, part_recv, hidden, grad,
    ff_s, ff_r, ff_sum, qo_s, qo_r, qo_sum, kv_s, kv_r, kv_sum,
    sm_y, sm_c, sm_own, sm_ly, sm_lc, sm_last,
    ssem, rsem, lsem, go,
):
    NN = N * N
    M = N * Q
    S = J // 2
    DH = D // N
    W = 2 * DH // 3
    WQ, WKV = 2 * W, 3 * W
    heads = DH // HEAD
    s = lax.axis_index("section")
    c = lax.axis_index("ctx")
    y = lax.axis_index("fsdp")
    x = lax.rem(c, N)
    z = lax.div(c, N)
    straight = y == z
    turned = y != z
    order = tuple(sorted(range(1, N), key=lambda d: -min(d, N - d)))
    streams = range(J)
    sibling = {"section": 1 - s}
    partner = {"ctx": y * N + x, "fsdp": z}

    def near(v, d):
        return lax.rem(v + d, N)

    def near_ctx(d):
        return lax.rem(c + d, NN)

    counter = [0]

    def block_of(count=N):
        counter[0] += count
        assert counter[0] <= SEMS
        return counter[0] - count

    drains = []

    def remote(src, dst, send, recv, device):
        return pltpu.make_async_remote_copy(
            src_ref=src, dst_ref=dst, send_sem=ssem.at[send], recv_sem=rsem.at[recv],
            device_id=device, device_id_type=MESH,
        )

    def start(src, dst, send, recv, device):
        copy = remote(src, dst, send, recv, device)
        copy.start()
        drains.append(copy.wait_send)

    def start_if(condition, src, dst, send, recv, device):
        copy = remote(src, dst, send, recv, device)
        pl.when(condition)(lambda: copy.start())
        drains.append(lambda: pl.when(condition)(lambda: copy.wait_send()))

    def start_each(count, make):
        @pl.loop(1, count)
        def _(d):
            make(d).start()

        def drain():
            @pl.loop(1, count)
            def _(d):
                make(d).wait_send()

        drains.append(drain)

    def landed(dst, recv):
        remote(dst, dst, 0, recv, sibling).wait_recv()

    def local_if(condition, src, dst, slot):
        copy = pltpu.make_async_copy(src, dst, lsem.at[slot])
        pl.when(condition)(lambda: copy.start())
        return lambda: pl.when(condition)(lambda: copy.wait())

    def local(src, dst, slot):
        copy = pltpu.make_async_copy(src, dst, lsem.at[slot])
        copy.start()
        return copy.wait

    def along(axis, index):
        if axis == "y":
            return {"fsdp": index}
        return {"ctx": z * N + index}

    place = {"x": x, "y": y}

    def spread(axis, ref, base, *rest):
        me = place[axis]
        for d in order:
            start(
                ref.at[(me,) + rest], ref.at[(me,) + rest], base + d, base + me,
                along(axis, near(me, d)),
            )

    def arrived(axis, ref, base, *rest):
        for d in order:
            source = near(place[axis], d)
            landed(ref.at[(source,) + rest], base + source)

    def deal(axis, src, dst, base):
        me = place[axis]
        for d in order:
            other = near(me, d)
            start(src.at[other], dst.at[me], base + d, base + me, along(axis, other))

    barrier = pltpu.get_barrier_semaphore()

    @pl.loop(1, NN * N)
    def _(d):
        index = lax.rem(c * N + y + d, NN * N)
        pl.semaphore_signal(
            barrier, inc=1, device_id={"ctx": lax.div(index, N), "fsdp": lax.rem(index, N)},
            device_id_type=MESH,
        )

    pl.semaphore_signal(barrier, inc=1, device_id=sibling, device_id_type=MESH)
    wait_cuts = [local(a, b, 13 + j) for j, (a, b) in enumerate(((wq_in, wq), (wk_in, wk), (wv_in, wv)))]
    wait_wred = local(wred_in, wred, 0)
    wait_wout = local(wout_in, wout.at[pl.ds(WQ - DH, DH)], 1)

    put = (
        lax.broadcasted_iota(jnp.int32, (DH, D), 0) + y * DH
        == lax.broadcasted_iota(jnp.int32, (DH, D), 1)
    )
    vecs[y] = mm(rows_in[...].astype(BF16), jnp.where(put, 1.0, 0.0).astype(BF16))[0:8]

    def picker(width, shift, first):
        row = lax.broadcasted_iota(jnp.int32, (WQ, width), 0)
        col = lax.broadcasted_iota(jnp.int32, (WQ, width), 1)
        inside = jnp.logical_and(col >= first, col < first + DH)
        return jnp.where(
            jnp.logical_and(row - shift == col - first, inside), 1.0, 0.0
        ).astype(BF16)

    for wait in wait_cuts:
        wait()
    for b in range(N):
        lane = b * DH // W * W
        cut = slice(lane, lane + WQ)
        shift = b * DH - lane
        w_send[b, :, 0:WKV] = (
            mm(wk[:, cut], picker(WKV, shift, 0)) + mm(wv[:, cut], picker(WKV, shift, DH))
        ).astype(BF16)
        w_send[b, :, WKV : WKV + WQ] = mm(wq[:, cut], picker(WQ, shift, 0)).astype(BF16)
    w_all[y] = w_send[y]
    pl.semaphore_wait(barrier, NN * N)

    k_u = block_of(J)
    k_gp = block_of(J)
    k_cot, k_y, k_dx = (block_of(1) for _ in range(3))
    k_vecs = block_of()
    spread("y", vecs, k_vecs)
    wait_u = []
    for j in streams:
        start_if(
            jnp.logical_and(s == 0, turned), tok.at[j], u_in.at[j], k_u + j, k_u + j, partner
        )
        wait_u.append(
            local_if(jnp.logical_and(s == 0, straight), tok.at[j], u_in.at[j], 16 + j)
        )

    @pl.when(s == 1)
    def _():
        pl.semaphore_wait(go, 1)

    k_w = block_of()
    deal("y", w_send, w_all, k_w)

    slot = lax.broadcasted_iota(jnp.int32, (1, 2 * N * M), 1)
    found = jnp.zeros_like(slot)
    for b in range(2 * NN):
        stored = 2 * (b % N * N + b // (2 * N)) + b // N % 2
        found = jnp.where(slot >= b * Q, order_in[stored] * Q - b * Q, found)
    kpos[...] = found + slot
    slot = lax.broadcasted_iota(jnp.int32, (2 * M, 1), 0)
    found = jnp.zeros_like(slot)
    for b in range(2 * N):
        found = jnp.where(
            slot >= b * Q, order_in[2 * (b % N * N + x) + b // N] * Q - b * Q, found
        )
    qpos[...] = found + slot

    arrived("y", vecs, k_vecs)
    params = vecs[0]
    for other in range(1, N):
        params = params + vecs[other]
    gain1, shift1, gain2, shift2, b_out, b_reduce = (params[r : r + 1] for r in range(6))
    lanes = lax.broadcasted_iota(jnp.int32, (1, WQ), 1)

    k_n1 = [block_of() for _ in streams]
    for j in streams:
        @pl.when(jnp.logical_or(s == 1, turned))
        def _():
            landed(u_in.at[j], k_u + j)

        wait_u[j]()
        normal, _ = normalize(u_in[j].astype(F32))
        n1[j, y] = (normal * gain1 + shift1).astype(BF16)
        spread("y", n1.at[j], k_n1[j])

    k_wexp = block_of()

    def wexp_cut(b):
        return wexp_in.at[:, pl.ds(pl.multiple_of(b * F, 128), F)]

    wait_wexp = local(wexp_cut(y), wexp.at[y], 4)
    for d in order:
        other = near(y, d)
        start(wexp_cut(other), wexp.at[y], k_wexp + d, k_wexp + y, along("y", other))
    start_if(jnp.logical_and(s == 1, turned), cot, cot_in, k_cot, k_cot, partner)
    wait_cot = local_if(jnp.logical_and(s == 1, straight), cot, cot_in, 5)

    k_kv = [block_of() for _ in streams]
    arrived("y", w_all, k_w)
    b_value = bias_at(rows_in[7:8], W, WQ, DH)
    b_query = bias_at(rows_in[6:7], 0, WQ, 0)
    for j in streams:
        arrived("y", n1.at[j], k_n1[j])
        rows = n1[j].reshape(M, D)
        made = mm(rows, w_all[:, :, 0:WKV].reshape(D, WKV))
        kv[j // 2, x, j % 2, :, 0:W] = made[:, 0:W].astype(BF16)
        kv[j // 2, x, j % 2, :, W:WKV] = (made[:, W:WKV] + b_value).astype(BF16)
        spread("x", kv.at[j // 2], k_kv[j], j % 2)
        query = mm(rows, w_all[:, :, WKV : WKV + WQ].reshape(D, WQ)) + b_query
        q_all[j] = (query * 0.125).astype(BF16)

    @pl.when(s == 0)
    def _():
        pl.semaphore_signal(go, inc=1, device_id=sibling, device_id_type=MESH)

    def only(h, values, first):
        inside = jnp.logical_and(lanes >= first + h * HEAD, lanes < first + (h + 1) * HEAD)
        return jnp.where(inside, values.astype(F32), 0.0)

    def scatter(number, j, term, base):
        part_send[number, j] = term.astype(BF16).reshape(N, Q, D)
        deal("y", part_send.at[number, j], part_recv.at[number, j], base)

    def collected(number, j, base):
        total = part_send[number, j, y].astype(F32)
        arrived("y", part_recv.at[number, j], base)
        for d in order:
            total = total + part_recv[number, j, near(y, d)].astype(F32)
        return total

    def pair(ref, i):
        return ref[2 * i : 2 * i + 2].reshape(2 * M, WQ)

    wout[0 : WQ - DH] = jnp.zeros((WQ - DH, D), BF16)
    wait_wout()
    k_po = [block_of() for _ in streams]
    for i in range(S):
        for side in range(2):
            arrived("x", kv.at[i], k_kv[2 * i + side], side)
        allowed = kpos[...] <= qpos[...]
        keys = kv[i, :, :, :, 0:WQ].reshape(2 * N * M, WQ)
        values = kv[i, :, :, :, W:WKV].reshape(2 * N * M, WQ)
        total = jnp.zeros((2 * M, WQ), F32)
        for h in range(heads):
            scores = mm_nt(only(h, pair(q_all, i), 0).astype(BF16), keys)
            scores = jnp.where(allowed, scores, -1e30)
            raised = jnp.exp(scores - jnp.max(scores, axis=-1, keepdims=True))
            part = raised / jnp.sum(raised, axis=-1, keepdims=True)
            probs[i * heads + h] = part
            total = total + only(h, mm(part.astype(BF16), values), WQ - DH)
        low = total.astype(BF16)
        mixed[2 * i : 2 * i + 2] = low.reshape(2, M, WQ)
        term = mm(low, wout[...])
        for side in range(2):
            scatter(0, 2 * i + side, term[side * M : (side + 1) * M], k_po[2 * i + side])

    k_n2 = [block_of() for _ in streams]
    for j in streams:
        state = u_in[j].astype(F32) + (collected(0, j, k_po[j]) + b_out)
        hidden[j] = state
        normal, _ = normalize(state)
        n2[j, y] = (normal * gain2 + shift2).astype(BF16)
        spread("y", n2.at[j], k_n2[j])

    wait_wexp()
    wait_wred()
    arrived("y", wexp, k_wexp)
    k_ff = [block_of() for _ in streams]
    for j in streams:
        arrived("y", n2.at[j], k_n2[j])
        before = mm(n2[j].reshape(M, D), wexp[...].reshape(D, F)) + bexp_in[...].astype(F32)
        square = before * before
        bent = jnp.tanh(GELU_SCALE * (before + GELU_CUBE * (square * before)))
        side = 0.5 * (1.0 + bent)
        low = (before * side).astype(BF16)
        active[j] = low
        slope[j] = side + 0.5 * before * (1.0 - bent * bent) * (
            GELU_SCALE * (1.0 + 3.0 * GELU_CUBE * square)
        )
        scatter(1, j, mm(low, wred[...]), k_ff[j])

    for j in streams:
        result = hidden[j] + (collected(1, j, k_ff[j]) + b_reduce)
        y_low[j] = result.astype(BF16)
        start_if(s == 0, y_low.at[j], u_in.at[j], k_u + j, k_u + j, sibling)

    @pl.when(jnp.logical_and(s == 1, turned))
    def _():
        landed(cot_in, k_cot)

    wait_cot()
    sm_own[...] = jnp.zeros_like(sm_own)
    sm_last[...] = jnp.zeros_like(sm_last)
    k_g = [block_of() for _ in streams]
    for j in streams:
        @pl.when(s == 1)
        def _():
            grad[j] = cot_in[j]

        @pl.when(s == 0)
        def _():
            landed(gp_in.at[j], k_gp + j)
            grad[j] = gp_in[j].astype(F32)

        low = grad[j].astype(BF16)
        g_all[j, y] = low
        spread("y", g_all.at[j], k_g[j])
        sm_own[5:6] += column_sums(low)

    start_if(turned, y_low, out_y, k_y, k_y, partner)
    wait_y = local_if(straight, y_low, out_y, 6)

    k_gf = [block_of() for _ in streams]
    for j in streams:
        arrived("y", g_all.at[j], k_g[j])
        low = (mm_nt(g_all[j].reshape(M, D), wred[...]) * slope[j]).astype(BF16)
        gb_all[j] = low
        scatter(2, j, mm_nt(low, wexp[...].reshape(D, F)), k_gf[j])

    def turn(index):
        return lax.rem(lax.rem(index, N) + lax.div(index, N), N)

    def piece(index):
        return turn(index) * N + lax.div(index, N)

    mine = piece(c)

    def pool(src, dst, base):
        dst[c] = src[mine]

        def make(d):
            other = near_ctx(d)
            return remote(src.at[piece(other)], dst.at[c], base + d, base + c, {"ctx": other})

        start_each(NN, make)

    def pooled(dst, base):
        @pl.loop(1, NN)
        def _(d):
            landed(dst.at[near_ctx(d)], base + near_ctx(d))

        total = dst[0].astype(F32)
        for other in range(1, NN):
            total = total + dst[other].astype(F32)
        return total

    g_rows = g_all[...].reshape(J * M, D)
    gb_rows = gb_all[...].reshape(J * M, F)
    sm_own[10:11] = column_sums(gb_rows)
    ff_s[:, 1] = mm_tn(active[...].reshape(J * M, F), g_rows).astype(BF16).reshape(NN, F // NN, D)
    ff_s[:, 0] = mm_tn(n2[...].reshape(J * M, D), gb_rows).astype(BF16).reshape(NN, D // NN, F)
    k_ffp = block_of(NN)
    pool(ff_s, ff_r, k_ffp)

    k_ga = [block_of() for _ in streams]
    for j in streams:
        grad_two = collected(2, j, k_gf[j])
        normal, factor = normalize(hidden[j])
        grad_hidden = grad[j] + norm_back(grad_two, normal, factor, gain2)
        grad[j] = grad_hidden
        low = grad_hidden.astype(BF16)
        ga_all[j, y] = low
        spread("y", ga_all.at[j], k_ga[j])
        sm_own[2:3] += column_sums(grad_two * normal)
        sm_own[3:4] += column_sums(grad_two)
        sm_own[4:5] += column_sums(low)

    k_dkv = [block_of() for _ in range(S)]
    for i in range(S):
        for j in (2 * i, 2 * i + 1):
            arrived("y", ga_all.at[j], k_ga[j])
            gm_all[j] = mm_nt(ga_all[j].reshape(M, D), wout[...]).astype(BF16)
        keys = kv[i, :, :, :, 0:WQ].reshape(2 * N * M, WQ)
        values = kv[i, :, :, :, W:WKV].reshape(2 * N * M, WQ)
        total = jnp.zeros((2 * M, WQ), F32)
        total_k = jnp.zeros((2 * N * M, WQ), F32)
        total_v = jnp.zeros((2 * N * M, WQ), F32)
        for h in range(heads):
            part = probs[i * heads + h]
            mixed_head = only(h, pair(gm_all, i), WQ - DH).astype(BF16)
            grad_probs = mm_nt(mixed_head, values)
            inner = jnp.sum(part * grad_probs, axis=-1, keepdims=True)
            grad_scores = (part * (grad_probs - inner)).astype(BF16)
            total = total + only(h, mm(grad_scores, keys), 0)
            total_k = total_k + mm_tn(grad_scores, only(h, pair(q_all, i), 0).astype(BF16))
            total_v = total_v + mm_tn(part.astype(BF16), mixed_head)
        shared = total_k[:, W:WQ] + total_v[:, 0:W]
        for lane, terms in ((0, total_k[:, 0:W]), (W, shared), (WQ, total_v[:, W:WQ])):
            dkv_send[i, :, :, :, lane : lane + W] = terms.astype(BF16).reshape(N, 2, M, W)
        deal("x", dkv_send.at[i], dkv_recv.at[i], k_dkv[i])
        low = (total.astype(BF16).astype(F32) * 0.125).astype(BF16)
        dq_all[2 * i : 2 * i + 2] = low.reshape(2, M, WQ)

    n1_rows = n1[...].reshape(J * M, D)
    dq_rows = dq_all[...].reshape(J * M, WQ)
    sm_own[8:9, 0:DH] = column_sums(dq_rows)[:, 0:DH]
    grad_q = mm_tn(n1_rows, dq_rows)
    grad_o = mm_tn(ga_all[...].reshape(J * M, D), mixed[...].reshape(J * M, WQ))
    qo_s[:, :, 0:W] = grad_q[:, 0:W].astype(BF16).reshape(NN, D // NN, W)
    qo_s[:, :, W:WQ] = (grad_q[:, W:WQ] + grad_o[:, 0:W]).astype(BF16).reshape(NN, D // NN, W)
    qo_s[:, :, WQ:WKV] = grad_o[:, W:WQ].astype(BF16).reshape(NN, D // NN, W)
    k_qop = block_of(NN)
    pool(qo_s, qo_r, k_qop)

    home = turn(c) == y
    finals = []
    late = []

    def hand_rows(src, dst, slot):
        base = block_of(NN)

        def make(d):
            return remote(src, dst(mine), base + d, base + c, {"ctx": near_ctx(d)})

        start_each(NN, make)
        late.append(local(src, dst(mine), slot))

        def finish():
            @pl.loop(1, NN)
            def _(d):
                landed(dst(piece(near_ctx(d))), base + near_ctx(d))

        finals.append(finish)

    def hand_across(src, dst, slot):
        base = block_of(NN)
        owner = turn(c)

        def make(d):
            return remote(
                src, dst(z, y), base + d, base + z * N + y,
                {"ctx": near_ctx(d), "fsdp": owner},
            )

        start_each(NN, make)
        start_if(
            jnp.logical_not(home), src, dst(z, y), base, base + z * N + y,
            {"ctx": c, "fsdp": owner},
        )
        late.append(local_if(home, src, dst(z, y), slot))

        def finish():
            @pl.loop(0, NN)
            def _(index):
                sub = lax.div(index, N)
                source = lax.rem(index, N)
                own = jnp.logical_and(jnp.logical_and(home, sub == z), source == y)

                @pl.when(jnp.logical_not(own))
                def _():
                    landed(dst(sub, source), base + index)

        finals.append(finish)

    def lane_block(ref, width):
        return lambda sub, source: ref.at[
            sub, :, pl.ds(pl.multiple_of(source * width, 128), width)
        ]

    k_gn = [block_of() for _ in streams]
    for j in streams:
        i, side = j // 2, j % 2
        if side == 0:
            arrived("x", dkv_recv.at[i], k_dkv[i])
        total = dkv_send[i, x, side].astype(F32)
        for d in order:
            total = total + dkv_recv[i, near(x, d), side].astype(F32)
        low = total.astype(BF16)
        dkv_all[j] = low
        scatter(
            3, j,
            mm_nt(dq_all[j], w_all[:, :, WKV : WKV + WQ].reshape(D, WQ))
            + mm_nt(low, w_all[:, :, 0:WKV].reshape(D, WKV)),
            k_gn[j],
        )

    dkv_rows = dkv_all[...].reshape(J * M, WKV)
    sm_own[9:10, 0:WKV] = column_sums(dkv_rows)
    kv_s[...] = mm_tn(n1_rows, dkv_rows).astype(BF16).reshape(NN, D // NN, WKV)
    k_kvp = block_of(NN)
    pool(kv_s, kv_r, k_kvp)

    sm_y[y] = sm_own[0:8]
    k_smy = block_of()
    spread("y", sm_y, k_smy)
    ff_sum[...] = pooled(ff_r, k_ffp).astype(BF16)
    hand_across(ff_sum.at[0], lane_block(out_wexp, F), 7)
    hand_rows(ff_sum.at[1], lambda index: out_wred.at[index], 8)

    for j in streams:
        grad_normed = collected(3, j, k_gn[j])
        normal, factor = normalize(u_in[j].astype(F32))
        grad_input = grad[j] + norm_back(grad_normed, normal, factor, gain1)
        dx_low[j] = grad_input.astype(BF16)
        start_if(s == 1, dx_low.at[j], gp_in.at[j], k_gp + j, k_gp + j, sibling)
        dx_buf[j] = grad_input
        sm_last[0:1] += column_sums(grad_normed * normal)
        sm_last[1:2] += column_sums(grad_normed)

    sm_ly[y] = sm_last[...]
    k_smly = block_of()
    spread("y", sm_ly, k_smly)
    start_if(turned, dx_buf, out_dx, k_dx, k_dx, partner)
    wait_dx = local_if(straight, dx_buf, out_dx, 9)

    def around(ref, base):
        start_each(
            NN,
            lambda d: remote(ref.at[c], ref.at[c], base + d, base + c, {"ctx": near_ctx(d)}),
        )

    def total_of(ref):
        rows = ref[0]
        for other in range(1, ref.shape[0]):
            rows = rows + ref[other]
        return rows

    kv_sum[...] = pooled(kv_r, k_kvp).astype(BF16)
    hand_across(kv_sum, lane_block(out_kv, WKV), 12)
    arrived("y", sm_ly, k_smly)
    sm_lc[c] = total_of(sm_ly)
    k_smlc = block_of(NN)
    around(sm_lc, k_smlc)
    arrived("y", sm_y, k_smy)
    sm_c[c, 0:8] = total_of(sm_y)
    sm_c[c, 8:16] = sm_own[8:16]
    k_smc = block_of(NN)
    around(sm_c, k_smc)
    qo_sum[...] = pooled(qo_r, k_qop).astype(BF16)
    hand_across(qo_sum.at[:, 0:WQ], lane_block(out_q, WQ), 10)
    hand_rows(qo_sum.at[:, W:WKV], lambda index: out_out.at[index], 11)

    for ref, base in ((sm_lc, k_smlc), (sm_c, k_smc)):
        @pl.loop(1, NN)
        def _(d):
            landed(ref.at[near_ctx(d)], base + near_ctx(d))

    out_small[0:8] = total_of(sm_lc)
    out_small[8:24] = total_of(sm_c)

    for finish in finals:
        finish()

    @pl.when(turned)
    def _():
        landed(out_y, k_y)
        landed(out_dx, k_dx)

    for wait in [wait_y, wait_dx] + late:
        wait()
    for drain in drains:
        drain()


def bias_at(values, lane, width, first):
    size = values.shape[1]
    row = lax.broadcasted_iota(jnp.int32, (size, width), 0)
    col = lax.broadcasted_iota(jnp.int32, (size, width), 1)
    put = jnp.where(row + first == col + lane, 1.0, 0.0).astype(BF16)
    wide = jnp.broadcast_to(values, (16, size)).astype(BF16)
    return mm(wide, put)[0:1]


def shards(
    tokens, cotangent, block_order, first_gain, first_shift, w_query, b_query, w_key, w_value,
    b_value, w_out, b_out, second_gain, second_shift, w_expand, b_expand, w_reduce, b_reduce,
):
    N = lax.axis_size("fsdp")
    S, R, D = tokens.shape
    F = w_reduce.shape[1]
    DH = D // N
    W = 2 * DH // 3
    WQ, WKV = 2 * W, 3 * W
    J, Q = 2 * S, R // 2
    NN, M = N * N, N * Q
    heads = DH // HEAD
    y = lax.axis_index("fsdp")

    rows = jnp.concatenate(
        [first_gain, first_shift, second_gain, second_shift, b_out, b_reduce, b_query, b_value]
    ).astype(F32)
    rows = jnp.pad(rows, ((0, 8), (0, 0)))

    def shape(dims, dtype):
        return jax.ShapeDtypeStruct(dims, dtype)

    vmem = pl.BlockSpec(memory_space=pltpu.VMEM)
    smem = pl.BlockSpec(memory_space=pltpu.SMEM)
    hbm = pl.BlockSpec(memory_space=pl.ANY)
    V = pltpu.VMEM
    slab = V((J, N, Q, D), BF16)
    rows_low, rows_full = V((J, Q, D), BF16), V((J, Q, D), F32)
    outs = pl.pallas_call(
        functools.partial(kernel, N, J, Q, D, F),
        out_shape=(
            shape((J, Q, D), BF16),
            shape((J, Q, D), F32),
            shape((N, D // NN, N * WKV), BF16),
            shape((N, D // NN, N * WQ), BF16),
            shape((NN, D // NN, WQ), BF16),
            shape((N, D // NN, N * F), BF16),
            shape((NN, F // NN, D), BF16),
            shape((24, D), F32),
        ),
        in_specs=[
            hbm, hbm, smem, vmem, vmem, hbm, hbm, hbm, hbm, hbm, hbm,
        ],
        out_specs=(hbm, hbm, hbm, hbm, hbm, hbm, hbm, vmem),
        scratch_shapes=[
            rows_low, rows_full, rows_low, rows_low, rows_full, rows_low, V((N, 8, D), F32),
            V((1, 2 * N * M), jnp.int32), V((2 * M, 1), jnp.int32),
            V((DH, D), BF16), V((DH, D), BF16), V((DH, D), BF16),
            V((N, DH, WKV + WQ), BF16), V((N, DH, WKV + WQ), BF16), V((N, DH, F), BF16),
            V((F, D), BF16), V((WQ, D), BF16),
            slab, slab, slab, slab,
            V((J, M, F), BF16), V((J, M, F), BF16), V((J, M, F), F32),
            V((J, M, WQ), BF16), V((S, N, 2, M, WKV), BF16),
            V((S * heads, 2 * M, 2 * N * M), F32),
            V((J, M, WQ), BF16), V((J, M, WQ), BF16), V((J, M, WQ), BF16), V((J, M, WKV), BF16),
            V((S, N, 2, M, WKV), BF16), V((S, N, 2, M, WKV), BF16),
            V((4, J, N, Q, D), BF16), V((4, J, N, Q, D), BF16), rows_full, rows_full,
            V((NN, 2, D // NN, D), BF16), V((NN, 2, D // NN, D), BF16), V((2, D // NN, D), BF16),
            V((NN, D // NN, WKV), BF16), V((NN, D // NN, WKV), BF16), V((D // NN, WKV), BF16),
            V((NN, D // NN, WKV), BF16), V((NN, D // NN, WKV), BF16), V((D // NN, WKV), BF16),
            V((N, 8, D), F32), V((NN, 16, D), F32), V((16, D), F32),
            V((N, 8, D), F32), V((NN, 8, D), F32), V((8, D), F32),
            pltpu.SemaphoreType.DMA((SEMS,)),
            pltpu.SemaphoreType.DMA((SEMS,)),
            pltpu.SemaphoreType.DMA((24,)),
            pltpu.SemaphoreType.REGULAR,
        ],
        compiler_params=pltpu.CompilerParams(
            collective_id=0, has_side_effects=True, vmem_limit_bytes=60 * 1024 * 1024
        ),
        name="layers",
    )(
        tokens.reshape(J, Q, D), cotangent.reshape(J, Q, D), block_order, rows, b_expand, w_query[0], w_key[0], w_value[0], w_out[0],
        w_expand[0], w_reduce[0],
    )
    out_y, out_dx, g_kv, g_q, g_out, g_exp, g_red, small = outs
    g_kv = g_kv.reshape(DH, N * WKV)
    g_q = g_q.reshape(DH, N * WQ)

    def whole(parts, width, first):
        pieces = [parts[:, b * width + first : b * width + first + DH] for b in range(N)]
        return jnp.concatenate(pieces, axis=1).astype(F32)[None]

    mine = lax.dynamic_slice(small, (0, y * DH), (16, DH))
    return (
        out_y.reshape(1, S, R, D),
        out_dx.reshape(1, S, R, D),
        mine[0:1],
        mine[1:2],
        whole(g_q, WQ, 0),
        small[16:17, 0:DH],
        whole(g_kv, WKV, 0),
        whole(g_kv, WKV, DH),
        small[17:18, DH:WKV],
        g_out.reshape(D, WQ)[:, WQ - DH :].T.astype(F32)[None],
        mine[12:13],
        mine[10:11],
        mine[11:12],
        g_exp.reshape(1, DH, N * F).astype(F32),
        small[18:19, 0:F],
        g_red.reshape(1, F, D).astype(F32),
        mine[13:14],
    )


def solution(mesh):
    vector = P("section", "fsdp")
    matrix = P("section", "fsdp", None)
    return jax.shard_map(
        shards,
        mesh=mesh,
        in_specs=(
            P("fsdp", "ctx", None), P("fsdp", "ctx", None), P(),
            vector, vector, matrix, vector, matrix, matrix, vector, matrix, vector, vector, vector,
            matrix, vector, matrix, vector,
        ),
        out_specs=(
            P("section", "fsdp", "ctx", None), P("section", "fsdp", "ctx", None),
            vector, vector, matrix, vector, matrix, matrix, vector, matrix, vector, vector, vector,
            matrix, vector, matrix, vector,
        ),
        check_vma=False,
    )
```

time: 270 us -> 268 us (level)
  the two profiles are of different devices: /device:TPU:0 before, /device:TPU:100 now
where the time goes in v3:
time: 268 us; the launch traced here: 267 us
  Pallas kernels  253 us (94%)
  local copies, waits for them, and re-layouts  7.02 us (3%)
  other arithmetic  6.88 us (3%)
    pallas_call x1, Pallas kernels, shards(): pl.pallas_call(functools.partial(kernel, N, J, Q, D, F), out_shape=(shape...  253 us

profile of v3, /device:TPU:100, one launch (start us, length us, event | category | flops | bytes accessed | tf_op | source)
XLA Modules:
  0.0 267.2 jit_solution(13743993309976872356)
XLA Ops:
  0.7 0.8 concatenate.57
  1.5 0.6 pad_convert_fusion.rows_in
  2.1 252.6 %layers.1 = (bf16[4,32,768]{2,1,0:T(8,128)(2,1)}, f32[4,32,768]{2,1,0:T(8,128)}, bf16[4,48,1536]{2,1,0:T(8,128)(2,1)}, bf16[4,48,1024]{2,1,0:T(8,128)(2,1)}, bf1...) custom-call(bf16[4,32,768]{2,1,0:T(8,128)(2,1)} %bitcast.62, ...), custom_call_target="tpu_custom_call" | custom-call | tf_op jit(solution)/shard_map/layers/pallas_call | solution.py:668
  254.7 1.5 slice_bitcast_fusion.3
  256.2 0.0 copy-start.4
  256.2 1.2 maximum_convert_fusion.1
  257.4 0.0 copy-start.1
  257.4 0.0 copy-done.4
  257.4 1.0 maximum_convert_fusion
  258.4 1.5 fusion
  259.9 1.3 slice.86
  261.2 0.0 copy-done.1
  261.2 0.0 copy-start
  261.2 1.6 bitcast_convert_fusion
  262.8 0.1 copy-done
  262.9 0.0 copy-start.3
  262.9 1.7 bitcast_convert_fusion.1
  264.6 0.0 copy-done.3
  264.6 0.0 copy-start.5
  264.6 0.2 slice.100
  264.7 0.0 copy-start.2
  264.8 0.2 copy.36
  264.9 0.9 convert_bitcast_fusion
  265.8 0.0 copy-done.5
  265.8 0.7 copy.39
  266.5 0.0 copy-done.2
  266.5 0.7 copy.40
  (1 shorter events, 0.0 us)
Async XLA Ops:
  256.2 1.2 copy-start.4
  257.4 3.8 %copy-start.1 = (bf16[16,48,768]{2,1,0:T(8,128)(2,1)S(1)}, bf16[16,48,768]{2,1,0:T(8,128)(2,1)}, u32[]{:S(2)}) copy-start(bf16[16,48,768]{2,1,0:T(8,128)(2,1)} %get-tuple-element.32) | copy-start | bytes 3538948
  261.2 1.7 copy-start
  262.9 1.7 copy-start.3
  264.6 1.2 copy-start.5
  264.7 1.7 copy-start.2

commit v4 on v3

--- a/solution.py
+++ b/solution.py
@@ -14,7 +14,7 @@
 MESH = pl.DeviceIdType.MESH
 GELU_SCALE = 0.7978845608028654
 GELU_CUBE = 0.044715
-SEMS = 448
+SEMS = 80
 
 
 def mm(left, right):
@@ -58,8 +58,8 @@
     wq, wk, wv, w_send, w_all, wexp, wred, wout, n1, n2, g_all, ga_all, gb_all, active, slope,
     q_all, kv, probs, mixed, gm_all, dq_all, dkv_all, dkv_send, dkv_recv,
     part_send, part_recv, hidden, grad,
-    ff_s, ff_r, ff_sum, qo_s, qo_r, qo_sum, kv_s, kv_r, kv_sum,
-    sm_y, sm_c, sm_own, sm_ly, sm_lc, sm_last,
+    ff_s, ff_in, ff_r, ff_sum, qo_s, qo_r, qo_sum, kv_s, kv_r, kv_sum,
+    sm_y, sm_x, sm_z, sm_own, sm_ly, sm_lx, sm_lz, sm_last,
     ssem, rsem, lsem, go,
 ):
     NN = N * N
@@ -89,10 +89,10 @@
 
     counter = [0]
 
-    def block_of(count=N):
-        counter[0] += count
+    def block_of():
+        counter[0] += 1
         assert counter[0] <= SEMS
-        return counter[0] - count
+        return counter[0] - 1
 
     drains = []
 
@@ -102,27 +102,18 @@
             device_id=device, device_id_type=MESH,
         )
 
-    def start(src, dst, send, recv, device):
-        copy = remote(src, dst, send, recv, device)
+    def start(src, dst, slot, device):
+        copy = remote(src, dst, slot, slot, device)
         copy.start()
         drains.append(copy.wait_send)
 
-    def start_if(condition, src, dst, send, recv, device):
-        copy = remote(src, dst, send, recv, device)
+    def start_if(condition, src, dst, slot, device):
+        copy = remote(src, dst, slot, slot, device)
         pl.when(condition)(lambda: copy.start())
         drains.append(lambda: pl.when(condition)(lambda: copy.wait_send()))
 
-    def start_each(count, make):
-        @pl.loop(1, count)
-        def _(d):
-            make(d).start()
-
-        def drain():
-            @pl.loop(1, count)
-            def _(d):
-                make(d).wait_send()
-
-        drains.append(drain)
+    def sent(ref, slot):
+        remote(ref, ref, slot, 0, sibling).wait_send()
 
     def landed(dst, recv):
         remote(dst, dst, 0, recv, sibling).wait_recv()
@@ -140,40 +131,47 @@
     def along(axis, index):
         if axis == "y":
             return {"fsdp": index}
-        return {"ctx": z * N + index}
-
-    place = {"x": x, "y": y}
-
-    def spread(axis, ref, base, *rest):
+        if axis == "x":
+            return {"ctx": z * N + index}
+        return {"ctx": index * N + x}
+
+    place = {"x": x, "y": y, "z": z}
+    others = pl.ds(0, N - 1)
+    rest_ctx = pl.ds(0, NN - 1)
+
+    def spread(axis, ref, slot, *rest):
         me = place[axis]
         for d in order:
-            start(
-                ref.at[(me,) + rest], ref.at[(me,) + rest], base + d, base + me,
-                along(axis, near(me, d)),
-            )
-
-    def arrived(axis, ref, base, *rest):
-        for d in order:
-            source = near(place[axis], d)
-            landed(ref.at[(source,) + rest], base + source)
-
-    def deal(axis, src, dst, base):
+            at = ref.at[(me,) + rest]
+            remote(at, at, slot, slot, along(axis, near(me, d))).start()
+        drains.append(lambda: sent(ref.at[(others,) + rest], slot))
+
+    def arrived(ref, slot, *rest):
+        landed(ref.at[(others,) + rest], slot)
+
+    def deal(axis, src, dst, slot):
         me = place[axis]
         for d in order:
             other = near(me, d)
-            start(src.at[other], dst.at[me], base + d, base + me, along(axis, other))
+            remote(src.at[other], dst.at[me], slot, slot, along(axis, other)).start()
+        drains.append(lambda: sent(src.at[others], slot))
 
     barrier = pltpu.get_barrier_semaphore()
-
-    @pl.loop(1, NN * N)
+    everyone = 2 * NN * N
+
+    @pl.loop(1, everyone)
     def _(d):
-        index = lax.rem(c * N + y + d, NN * N)
+        index = lax.rem((s * NN + c) * N + y + d, everyone)
         pl.semaphore_signal(
-            barrier, inc=1, device_id={"ctx": lax.div(index, N), "fsdp": lax.rem(index, N)},
+            barrier, inc=1,
+            device_id={
+                "section": lax.div(index, NN * N),
+                "ctx": lax.rem(lax.div(index, N), NN),
+                "fsdp": lax.rem(index, N),
+            },
             device_id_type=MESH,
         )
 
-    pl.semaphore_signal(barrier, inc=1, device_id=sibling, device_id_type=MESH)
     wait_cuts = [local(a, b, 13 + j) for j, (a, b) in enumerate(((wq_in, wq), (wk_in, wk), (wv_in, wv)))]
     wait_wred = local(wred_in, wred, 0)
     wait_wout = local(wout_in, wout.at[pl.ds(WQ - DH, DH)], 1)
@@ -203,17 +201,17 @@
         ).astype(BF16)
         w_send[b, :, WKV : WKV + WQ] = mm(wq[:, cut], picker(WQ, shift, 0)).astype(BF16)
     w_all[y] = w_send[y]
-    pl.semaphore_wait(barrier, NN * N)
-
-    k_u = block_of(J)
-    k_gp = block_of(J)
-    k_cot, k_y, k_dx = (block_of(1) for _ in range(3))
+    pl.semaphore_wait(barrier, everyone - 1)
+
+    k_u = [block_of() for _ in streams]
+    k_gp = [block_of() for _ in streams]
+    k_cot, k_y, k_dx, k_ff_in, k_ff_pool, k_wexp_out, k_wred_out = (block_of() for _ in range(7))
     k_vecs = block_of()
     spread("y", vecs, k_vecs)
     wait_u = []
     for j in streams:
         start_if(
-            jnp.logical_and(s == 0, turned), tok.at[j], u_in.at[j], k_u + j, k_u + j, partner
+            jnp.logical_and(s == 0, turned), tok.at[j], u_in.at[j], k_u[j], partner
         )
         wait_u.append(
             local_if(jnp.logical_and(s == 0, straight), tok.at[j], u_in.at[j], 16 + j)
@@ -240,7 +238,7 @@
         )
     qpos[...] = found + slot
 
-    arrived("y", vecs, k_vecs)
+    arrived(vecs, k_vecs)
     params = vecs[0]
     for other in range(1, N):
         params = params + vecs[other]
@@ -251,31 +249,19 @@
     for j in streams:
         @pl.when(jnp.logical_or(s == 1, turned))
         def _():
-            landed(u_in.at[j], k_u + j)
+            landed(u_in.at[j], k_u[j])
 
         wait_u[j]()
         normal, _ = normalize(u_in[j].astype(F32))
         n1[j, y] = (normal * gain1 + shift1).astype(BF16)
         spread("y", n1.at[j], k_n1[j])
 
-    k_wexp = block_of()
-
-    def wexp_cut(b):
-        return wexp_in.at[:, pl.ds(pl.multiple_of(b * F, 128), F)]
-
-    wait_wexp = local(wexp_cut(y), wexp.at[y], 4)
-    for d in order:
-        other = near(y, d)
-        start(wexp_cut(other), wexp.at[y], k_wexp + d, k_wexp + y, along("y", other))
-    start_if(jnp.logical_and(s == 1, turned), cot, cot_in, k_cot, k_cot, partner)
-    wait_cot = local_if(jnp.logical_and(s == 1, straight), cot, cot_in, 5)
-
     k_kv = [block_of() for _ in streams]
-    arrived("y", w_all, k_w)
+    arrived(w_all, k_w)
     b_value = bias_at(rows_in[7:8], W, WQ, DH)
     b_query = bias_at(rows_in[6:7], 0, WQ, 0)
     for j in streams:
-        arrived("y", n1.at[j], k_n1[j])
+        arrived(n1.at[j], k_n1[j])
         rows = n1[j].reshape(M, D)
         made = mm(rows, w_all[:, :, 0:WKV].reshape(D, WKV))
         kv[j // 2, x, j % 2, :, 0:W] = made[:, 0:W].astype(BF16)
@@ -288,6 +274,19 @@
     def _():
         pl.semaphore_signal(go, inc=1, device_id=sibling, device_id_type=MESH)
 
+    k_wexp = block_of()
+
+    def wexp_cut(b):
+        return wexp_in.at[:, pl.ds(pl.multiple_of(b * F, 128), F)]
+
+    wait_wexp = local(wexp_cut(y), wexp.at[y], 4)
+    for d in order:
+        other = near(y, d)
+        remote(wexp_cut(other), wexp.at[y], k_wexp, k_wexp, along("y", other)).start()
+    drains.append(lambda: sent(wexp.at[others], k_wexp))
+    start_if(jnp.logical_and(s == 1, turned), cot, cot_in, k_cot, partner)
+    wait_cot = local_if(jnp.logical_and(s == 1, straight), cot, cot_in, 5)
+
     def only(h, values, first):
         inside = jnp.logical_and(lanes >= first + h * HEAD, lanes < first + (h + 1) * HEAD)
         return jnp.where(inside, values.astype(F32), 0.0)
@@ -298,7 +297,7 @@
 
     def collected(number, j, base):
         total = part_send[number, j, y].astype(F32)
-        arrived("y", part_recv.at[number, j], base)
+        arrived(part_recv.at[number, j], base)
         for d in order:
             total = total + part_recv[number, j, near(y, d)].astype(F32)
         return total
@@ -311,7 +310,7 @@
     k_po = [block_of() for _ in streams]
     for i in range(S):
         for side in range(2):
-            arrived("x", kv.at[i], k_kv[2 * i + side], side)
+            arrived(kv.at[i], k_kv[2 * i + side], side)
         allowed = kpos[...] <= qpos[...]
         keys = kv[i, :, :, :, 0:WQ].reshape(2 * N * M, WQ)
         values = kv[i, :, :, :, W:WKV].reshape(2 * N * M, WQ)
@@ -339,10 +338,10 @@
 
     wait_wexp()
     wait_wred()
-    arrived("y", wexp, k_wexp)
+    arrived(wexp, k_wexp)
     k_ff = [block_of() for _ in streams]
     for j in streams:
-        arrived("y", n2.at[j], k_n2[j])
+        arrived(n2.at[j], k_n2[j])
         before = mm(n2[j].reshape(M, D), wexp[...].reshape(D, F)) + bexp_in[...].astype(F32)
         square = before * before
         bent = jnp.tanh(GELU_SCALE * (before + GELU_CUBE * (square * before)))
@@ -357,13 +356,94 @@
     for j in streams:
         result = hidden[j] + (collected(1, j, k_ff[j]) + b_reduce)
         y_low[j] = result.astype(BF16)
-        start_if(s == 0, y_low.at[j], u_in.at[j], k_u + j, k_u + j, sibling)
+        start_if(s == 0, y_low.at[j], u_in.at[j], k_u[j], sibling)
+
+    def turn(index):
+        return lax.rem(lax.rem(index, N) + lax.div(index, N), N)
+
+    def piece(index):
+        return turn(index) * N + lax.div(index, N)
+
+    mine = piece(c)
+    owner = turn(c)
+    home = owner == y
+
+    def pool(src, dst, slot):
+        dst[c] = src[mine]
+
+        @pl.loop(1, NN)
+        def _(d):
+            other = near_ctx(d)
+            remote(src.at[piece(other)], dst.at[c], slot, slot, {"ctx": other}).start()
+
+    def pooled(dst, slot):
+        landed(dst.at[rest_ctx], slot)
+        total = dst[0].astype(F32)
+        for other in range(1, NN):
+            total = total + dst[other].astype(F32)
+        return total.astype(BF16)
+
+    def hand_rows(src, out, slot):
+        pltpu.make_async_copy(src, out.at[mine], rsem.at[slot]).start()
+
+        @pl.loop(1, NN)
+        def _(d):
+            remote(src, out.at[mine], slot, slot, {"ctx": near_ctx(d)}).start()
+
+    def across(out, width):
+        return out.at[z, :, pl.ds(pl.multiple_of(y * width, 128), width)]
+
+    def hand_across(src, out, width, slot):
+        dst = across(out, width)
+
+        @pl.when(home)
+        def _():
+            pltpu.make_async_copy(src, dst, rsem.at[slot]).start()
+
+        @pl.when(jnp.logical_not(home))
+        def _():
+            remote(src, dst, slot, slot, {"fsdp": owner}).start()
+
+        @pl.loop(1, NN)
+        def _(d):
+            remote(src, dst, slot, slot, {"ctx": near_ctx(d), "fsdp": owner}).start()
+
+    def handed(out, slot, but_one):
+        @pl.when(home)
+        def _():
+            sent(but_one, slot)
+
+        @pl.when(jnp.logical_not(home))
+        def _():
+            sent(out, slot)
+
+    def reduce_feed():
+        landed(ff_in, k_ff_in)
+        pool(ff_in, ff_r, k_ff_pool)
+        ff_sum[...] = pooled(ff_r, k_ff_pool)
+
+        @pl.loop(0, NN)
+        def _(d):
+            other = near_ctx(d)
+            remote(
+                ff_sum.at[0], across(out_wexp, F), k_wexp_out, k_wexp_out,
+                {"section": 1 - s, "ctx": other, "fsdp": owner},
+            ).start()
+            remote(
+                ff_sum.at[1], out_wred.at[mine], k_wred_out, k_wred_out,
+                {"section": 1 - s, "ctx": other},
+            ).start()
+
+    drains.append(lambda: sent(ff_in.at[rest_ctx], k_ff_pool))
+    drains.append(lambda: sent(out_wexp, k_wexp_out))
+    drains.append(lambda: sent(out_wred, k_wred_out))
 
     @pl.when(jnp.logical_and(s == 1, turned))
     def _():
         landed(cot_in, k_cot)
 
     wait_cot()
+    pl.when(s == 0)(reduce_feed)
     sm_own[...] = jnp.zeros_like(sm_own)
     sm_last[...] = jnp.zeros_like(sm_last)
     k_g = [block_of() for _ in streams]
@@ -374,7 +454,7 @@
 
         @pl.when(s == 0)
         def _():
-            landed(gp_in.at[j], k_gp + j)
+            landed(gp_in.at[j], k_gp[j])
             grad[j] = gp_in[j].astype(F32)
 
         low = grad[j].astype(BF16)
@@ -382,50 +462,22 @@
         spread("y", g_all.at[j], k_g[j])
         sm_own[5:6] += column_sums(low)
 
-    start_if(turned, y_low, out_y, k_y, k_y, partner)
+    start_if(turned, y_low, out_y, k_y, partner)
     wait_y = local_if(straight, y_low, out_y, 6)
 
     k_gf = [block_of() for _ in streams]
     for j in streams:
-        arrived("y", g_all.at[j], k_g[j])
+        arrived(g_all.at[j], k_g[j])
         low = (mm_nt(g_all[j].reshape(M, D), wred[...]) * slope[j]).astype(BF16)
         gb_all[j] = low
         scatter(2, j, mm_nt(low, wexp[...].reshape(D, F)), k_gf[j])
-
-    def turn(index):
-        return lax.rem(lax.rem(index, N) + lax.div(index, N), N)
-
-    def piece(index):
-        return turn(index) * N + lax.div(index, N)
-
-    mine = piece(c)
-
-    def pool(src, dst, base):
-        dst[c] = src[mine]
-
-        def make(d):
-            other = near_ctx(d)
-            return remote(src.at[piece(other)], dst.at[c], base + d, base + c, {"ctx": other})
-
-        start_each(NN, make)
-
-    def pooled(dst, base):
-        @pl.loop(1, NN)
-        def _(d):
-            landed(dst.at[near_ctx(d)], base + near_ctx(d))
-
-        total = dst[0].astype(F32)
-        for other in range(1, NN):
-            total = total + dst[other].astype(F32)
-        return total
 
     g_rows = g_all[...].reshape(J * M, D)
     gb_rows = gb_all[...].reshape(J * M, F)
     sm_own[10:11] = column_sums(gb_rows)
     ff_s[:, 1] = mm_tn(active[...].reshape(J * M, F), g_rows).astype(BF16).reshape(NN, F // NN, D)
     ff_s[:, 0] = mm_tn(n2[...].reshape(J * M, D), gb_rows).astype(BF16).reshape(NN, D // NN, F)
-    k_ffp = block_of(NN)
-    pool(ff_s, ff_r, k_ffp)
+    start(ff_s, ff_in, k_ff_in, sibling)
 
     k_ga = [block_of() for _ in streams]
     for j in streams:
@@ -443,7 +495,7 @@
     k_dkv = [block_of() for _ in range(S)]
     for i in range(S):
         for j in (2 * i, 2 * i + 1):
-            arrived("y", ga_all.at[j], k_ga[j])
+            arrived(ga_all.at[j], k_ga[j])
             gm_all[j] = mm_nt(ga_all[j].reshape(M, D), wout[...]).astype(BF16)
         keys = kv[i, :, :, :, 0:WQ].reshape(2 * N * M, WQ)
         values = kv[i, :, :, :, W:WKV].reshape(2 * N * M, WQ)
@@ -474,69 +526,20 @@
     qo_s[:, :, 0:W] = grad_q[:, 0:W].astype(BF16).reshape(NN, D // NN, W)
     qo_s[:, :, W:WQ] = (grad_q[:, W:WQ] + grad_o[:, 0:W]).astype(BF16).reshape(NN, D // NN, W)
     qo_s[:, :, WQ:WKV] = grad_o[:, W:WQ].astype(BF16).reshape(NN, D // NN, W)
-    k_qop = block_of(NN)
-    pool(qo_s, qo_r, k_qop)
-
-    home = turn(c) == y
-    finals = []
-    late = []
-
-    def hand_rows(src, dst, slot):
-        base = block_of(NN)
-
-        def make(d):
-            return remote(src, dst(mine), base + d, base + c, {"ctx": near_ctx(d)})
-
-        start_each(NN, make)
-        late.append(local(src, dst(mine), slot))
-
-        def finish():
-            @pl.loop(1, NN)
-            def _(d):
-                landed(dst(piece(near_ctx(d))), base + near_ctx(d))
-
-        finals.append(finish)
-
-    def hand_across(src, dst, slot):
-        base = block_of(NN)
-        owner = turn(c)
-
-        def make(d):
-            return remote(
-                src, dst(z, y), base + d, base + z * N + y,
-                {"ctx": near_ctx(d), "fsdp": owner},
-            )
-
-        start_each(NN, make)
-        start_if(
-            jnp.logical_not(home), src, dst(z, y), base, base + z * N + y,
-            {"ctx": c, "fsdp": owner},
-        )
-        late.append(local_if(home, src, dst(z, y), slot))
-
-        def finish():
-            @pl.loop(0, NN)
-            def _(index):
-                sub = lax.div(index, N)
-                source = lax.rem(index, N)
-                own = jnp.logical_and(jnp.logical_and(home, sub == z), source == y)
-
-                @pl.when(jnp.logical_not(own))
-                def _():
-                    landed(dst(sub, source), base + index)
-
-        finals.append(finish)
-
-    def lane_block(ref, width):
-        return lambda sub, source: ref.at[
-            sub, :, pl.ds(pl.multiple_of(source * width, 128), width)
-        ]
+    k_qo, k_kv_pool, k_q_out, k_o_out, k_kv_out = (block_of() for _ in range(5))
+    pl.when(s == 0)(lambda: pool(qo_s, qo_r, k_qo))
+
+    def reduce_qo():
+        qo_sum[...] = pooled(qo_r, k_qo)
+        hand_across(qo_sum.at[:, 0:WQ], out_q, WQ, k_q_out)
+        hand_rows(qo_sum.at[:, W:WKV], out_out, k_o_out)
+
 
     k_gn = [block_of() for _ in streams]
     for j in streams:
         i, side = j // 2, j % 2
         if side == 0:
-            arrived("x", dkv_recv.at[i], k_dkv[i])
+            arrived(dkv_recv.at[i], k_dkv[i])
         total = dkv_send[i, x, side].astype(F32)
         for d in order:
             total = total + dkv_recv[i, near(x, d), side].astype(F32)
@@ -552,22 +555,22 @@
     dkv_rows = dkv_all[...].reshape(J * M, WKV)
     sm_own[9:10, 0:WKV] = column_sums(dkv_rows)
     kv_s[...] = mm_tn(n1_rows, dkv_rows).astype(BF16).reshape(NN, D // NN, WKV)
-    k_kvp = block_of(NN)
-    pool(kv_s, kv_r, k_kvp)
+
+    @pl.when(s == 0)
+    def _():
+        pool(kv_s, kv_r, k_kv_pool)
+        reduce_qo()
 
     sm_y[y] = sm_own[0:8]
     k_smy = block_of()
     spread("y", sm_y, k_smy)
-    ff_sum[...] = pooled(ff_r, k_ffp).astype(BF16)
-    hand_across(ff_sum.at[0], lane_block(out_wexp, F), 7)
-    hand_rows(ff_sum.at[1], lambda index: out_wred.at[index], 8)
 
     for j in streams:
         grad_normed = collected(3, j, k_gn[j])
         normal, factor = normalize(u_in[j].astype(F32))
         grad_input = grad[j] + norm_back(grad_normed, normal, factor, gain1)
         dx_low[j] = grad_input.astype(BF16)
-        start_if(s == 1, dx_low.at[j], gp_in.at[j], k_gp + j, k_gp + j, sibling)
+        start_if(s == 1, dx_low.at[j], gp_in.at[j], k_gp[j], sibling)
         dx_buf[j] = grad_input
         sm_last[0:1] += column_sums(grad_normed * normal)
         sm_last[1:2] += column_sums(grad_normed)
@@ -575,53 +578,67 @@
     sm_ly[y] = sm_last[...]
     k_smly = block_of()
     spread("y", sm_ly, k_smly)
-    start_if(turned, dx_buf, out_dx, k_dx, k_dx, partner)
-    wait_dx = local_if(straight, dx_buf, out_dx, 9)
-
-    def around(ref, base):
-        start_each(
-            NN,
-            lambda d: remote(ref.at[c], ref.at[c], base + d, base + c, {"ctx": near_ctx(d)}),
-        )
+
+    @pl.when(s == 1)
+    def _():
+        pool(kv_s, kv_r, k_kv_pool)
+        pool(qo_s, qo_r, k_qo)
 
     def total_of(ref):
         rows = ref[0]
-        for other in range(1, ref.shape[0]):
+        for other in range(1, N):
             rows = rows + ref[other]
         return rows
 
-    kv_sum[...] = pooled(kv_r, k_kvp).astype(BF16)
-    hand_across(kv_sum, lane_block(out_kv, WKV), 12)
-    arrived("y", sm_ly, k_smly)
-    sm_lc[c] = total_of(sm_ly)
-    k_smlc = block_of(NN)
-    around(sm_lc, k_smlc)
-    arrived("y", sm_y, k_smy)
-    sm_c[c, 0:8] = total_of(sm_y)
-    sm_c[c, 8:16] = sm_own[8:16]
-    k_smc = block_of(NN)
-    around(sm_c, k_smc)
-    qo_sum[...] = pooled(qo_r, k_qop).astype(BF16)
-    hand_across(qo_sum.at[:, 0:WQ], lane_block(out_q, WQ), 10)
-    hand_rows(qo_sum.at[:, W:WKV], lambda index: out_out.at[index], 11)
-
-    for ref, base in ((sm_lc, k_smlc), (sm_c, k_smc)):
-        @pl.loop(1, NN)
-        def _(d):
-            landed(ref.at[near_ctx(d)], base + near_ctx(d))
-
-    out_small[0:8] = total_of(sm_lc)
-    out_small[8:24] = total_of(sm_c)
-
-    for finish in finals:
-        finish()
+    arrived(sm_y, k_smy)
+    sm_x[x, 0:8] = total_of(sm_y)
+    sm_x[x, 8:16] = sm_own[8:16]
+    k_smx = block_of()
+    spread("x", sm_x, k_smx)
+    arrived(sm_ly, k_smly)
+    sm_lx[x] = total_of(sm_ly)
+    k_smlx = block_of()
+    spread("x", sm_lx, k_smlx)
+    start_if(turned, dx_buf, out_dx, k_dx, partner)
+    wait_dx = local_if(straight, dx_buf, out_dx, 9)
+    kv_sum[...] = pooled(kv_r, k_kv_pool)
+    hand_across(kv_sum, out_kv, WKV, k_kv_out)
+    arrived(sm_x, k_smx)
+    sm_z[z] = total_of(sm_x)
+    k_smz = block_of()
+    spread("z", sm_z, k_smz)
+    arrived(sm_lx, k_smlx)
+    sm_lz[z] = total_of(sm_lx)
+    k_smlz = block_of()
+    spread("z", sm_lz, k_smlz)
+
+    @pl.when(s == 1)
+    def _():
+        reduce_qo()
+        reduce_feed()
+
+    arrived(sm_z, k_smz)
+    arrived(sm_lz, k_smlz)
+    out_small[0:8] = total_of(sm_lz)
+    out_small[8:24] = total_of(sm_z)
+    drains.append(lambda: sent(qo_s.at[rest_ctx], k_qo))
+    drains.append(lambda: sent(kv_s.at[rest_ctx], k_kv_pool))
+    drains.append(lambda: handed(out_kv, k_kv_out, kv_r.at[rest_ctx]))
+    drains.append(lambda: handed(out_q, k_q_out, qo_r.at[rest_ctx, :, pl.ds(0, WQ)]))
+    drains.append(lambda: sent(out_out.at[rest_ctx], k_o_out))
+
+    for ref, slot in (
+        (out_kv, k_kv_out), (out_q, k_q_out), (out_out, k_o_out), (out_wexp, k_wexp_out),
+        (out_wred, k_wred_out),
+    ):
+        landed(ref, slot)
 
     @pl.when(turned)
     def _():
         landed(out_y, k_y)
         landed(out_dx, k_dx)
 
-    for wait in [wait_y, wait_dx] + late:
+    for wait in (wait_y, wait_dx):
         wait()
     for drain in drains:
         drain()
@@ -694,11 +711,12 @@
             V((J, M, WQ), BF16), V((J, M, WQ), BF16), V((J, M, WQ), BF16), V((J, M, WKV), BF16),
             V((S, N, 2, M, WKV), BF16), V((S, N, 2, M, WKV), BF16),
             V((4, J, N, Q, D), BF16), V((4, J, N, Q, D), BF16), rows_full, rows_full,
-            V((NN, 2, D // NN, D), BF16), V((NN, 2, D // NN, D), BF16), V((2, D // NN, D), BF16),
+            V((NN, 2, D // NN, D), BF16), V((NN, 2, D // NN, D), BF16),
+            V((NN, 2, D // NN, D), BF16), V((2, D // NN, D), BF16),
             V((NN, D // NN, WKV), BF16), V((NN, D // NN, WKV), BF16), V((D // NN, WKV), BF16),
             V((NN, D // NN, WKV), BF16), V((NN, D // NN, WKV), BF16), V((D // NN, WKV), BF16),
-            V((N, 8, D), F32), V((NN, 16, D), F32), V((16, D), F32),
-            V((N, 8, D), F32), V((NN, 8, D), F32), V((8, D), F32),
+            V((N, 8, D), F32), V((N, 16, D), F32), V((N, 16, D), F32), V((16, D), F32),
+            V((N, 8, D), F32), V((N, 8, D), F32), V((N, 8, D), F32), V((8, D), F32),
             pltpu.SemaphoreType.DMA((SEMS,)),
             pltpu.SemaphoreType.DMA((SEMS,)),
             pltpu.SemaphoreType.DMA((24,)),

time: 268 us -> 259 us (0.966)
  the two profiles are of different devices: /device:TPU:100 before, /device:TPU:0 now
where the time goes in v4:
time: 259 us; the launch traced here: 256 us
  Pallas kernels  241 us (93%)
  local copies, waits for them, and re-layouts  7.02 us (3%)
  other arithmetic  6.88 us (3%)
    pallas_call x1, Pallas kernels, shards(): pl.pallas_call(functools.partial(kernel, N, J, Q, D, F), out_shape=(shape...  241 us

profile of v4, /device:TPU:0, one launch (start us, length us, event | category | flops | bytes accessed | tf_op | source)
XLA Modules:
  0.0 255.7 jit_solution(7873197797889206886)
XLA Ops:
  0.7 0.8 concatenate.57
  1.5 0.6 pad_convert_fusion.rows_in
  2.1 241.1 %layers.1 = (bf16[4,32,768]{2,1,0:T(8,128)(2,1)}, f32[4,32,768]{2,1,0:T(8,128)}, bf16[4,48,1536]{2,1,0:T(8,128)(2,1)}, bf16[4,48,1024]{2,1,0:T(8,128)(2,1)}, bf1...) custom-call(bf16[4,32,768]{2,1,0:T(8,128)(2,1)} %bitcast.62, ...), custom_call_target="tpu_custom_call" | custom-call | tf_op jit(solution)/shard_map/layers/pallas_call | solution.py:685
  243.2 1.5 slice_bitcast_fusion.3
  244.7 0.0 copy-start.4
  244.7 1.2 maximum_convert_fusion.1
  245.9 0.0 copy-start.1
  245.9 0.0 copy-done.4
  246.0 1.0 maximum_convert_fusion
  246.9 1.5 fusion
  248.4 1.3 slice.86
  249.8 0.0 copy-done.1
  249.8 0.0 copy-start
  249.8 1.6 bitcast_convert_fusion
  251.3 0.1 copy-done
  251.4 0.0 copy-start.3
  251.4 1.7 bitcast_convert_fusion.1
  253.1 0.0 copy-done.3
  253.1 0.0 copy-start.5
  253.1 0.2 slice.100
  253.3 0.0 copy-start.2
  253.3 0.2 copy.36
  253.5 0.9 convert_bitcast_fusion
  254.3 0.0 copy-done.5
  254.3 0.7 copy.39
  255.0 0.0 copy-done.2
  255.0 0.7 copy.40
  (1 shorter events, 0.0 us)
Async XLA Ops:
  244.7 1.2 copy-start.4
  245.9 3.8 %copy-start.1 = (bf16[16,48,768]{2,1,0:T(8,128)(2,1)S(1)}, bf16[16,48,768]{2,1,0:T(8,128)(2,1)}, u32[]{:S(2)}) copy-start(bf16[16,48,768]{2,1,0:T(8,128)(2,1)} %get-tuple-element.32) | copy-start | bytes 3538948
  249.8 1.7 copy-start
  251.4 1.7 copy-start.3
  253.1 1.2 copy-start.5
  253.3 1.7 copy-start.2

commit v5 on v4

--- a/solution.py
+++ b/solution.py
@@ -58,7 +58,7 @@
     wq, wk, wv, w_send, w_all, wexp, wred, wout, n1, n2, g_all, ga_all, gb_all, active, slope,
     q_all, kv, probs, mixed, gm_all, dq_all, dkv_all, dkv_send, dkv_recv,
     part_send, part_recv, hidden, grad,
-    ff_s, ff_in, ff_r, ff_sum, qo_s, qo_r, qo_sum, kv_s, kv_r, kv_sum,
+    ff_s, ff_in, ff_r, ff_one, ff_two, ff_sum, qo_s, qo_r, qo_sum, kv_s, kv_r, kv_sum,
     sm_y, sm_x, sm_z, sm_own, sm_ly, sm_lx, sm_lz, sm_last,
     ssem, rsem, lsem, go,
 ):
@@ -139,21 +139,27 @@
     others = pl.ds(0, N - 1)
     rest_ctx = pl.ds(0, NN - 1)
 
-    def spread(axis, ref, slot, *rest):
+    def send_spread(axis, ref, slot, *rest):
         me = place[axis]
         for d in order:
             at = ref.at[(me,) + rest]
             remote(at, at, slot, slot, along(axis, near(me, d))).start()
+
+    def spread(axis, ref, slot, *rest):
+        send_spread(axis, ref, slot, *rest)
         drains.append(lambda: sent(ref.at[(others,) + rest], slot))
 
     def arrived(ref, slot, *rest):
         landed(ref.at[(others,) + rest], slot)
 
-    def deal(axis, src, dst, slot):
+    def send_deal(axis, src, dst, slot):
         me = place[axis]
         for d in order:
             other = near(me, d)
             remote(src.at[other], dst.at[me], slot, slot, along(axis, other)).start()
+
+    def deal(axis, src, dst, slot):
+        send_deal(axis, src, dst, slot)
         drains.append(lambda: sent(src.at[others], slot))
 
     barrier = pltpu.get_barrier_semaphore()
@@ -205,7 +211,8 @@
 
     k_u = [block_of() for _ in streams]
     k_gp = [block_of() for _ in streams]
-    k_cot, k_y, k_dx, k_ff_in, k_ff_pool, k_wexp_out, k_wred_out = (block_of() for _ in range(7))
+    k_cot, k_y, k_dx, k_ff_in, k_wexp_out, k_wred_out = (block_of() for _ in range(6))
+    k_first, k_second, k_third = ([block_of(), block_of()] for _ in range(3))
     k_vecs = block_of()
     spread("y", vecs, k_vecs)
     wait_u = []
@@ -417,24 +424,48 @@
         def _():
             sent(out, slot)
 
+    axes = (("x", "z"), ("z", "x"))
+
+    def total_at(axis, own, received):
+        total = own.astype(F32)
+        for d in order:
+            total = total + received[near(place[axis], d)].astype(F32)
+        return total.astype(BF16)
+
     def reduce_feed():
         landed(ff_in, k_ff_in)
-        pool(ff_in, ff_r, k_ff_pool)
-        ff_sum[...] = pooled(ff_r, k_ff_pool)
-
-        @pl.loop(0, NN)
-        def _(d):
-            other = near_ctx(d)
+        for k in range(2):
+            send_deal(axes[k][0], ff_in.at[k], ff_r.at[k], k_first[k])
+        for k in range(2):
+            first, second = axes[k]
+            arrived(ff_r.at[k], k_first[k])
+            ff_one[k] = total_at(first, ff_in[k, place[first]], ff_r.at[k])
+            send_deal(second, ff_one.at[k], ff_two.at[k], k_second[k])
+        for k in range(2):
+            second = axes[k][1]
+            arrived(ff_two.at[k], k_second[k])
+            ff_sum[k, place[second]] = total_at(
+                second, ff_one[k, place[second]], ff_two.at[k]
+            )
+            send_spread(second, ff_sum.at[k], k_third[k])
+        arrived(ff_sum.at[0], k_third[0])
+        wide = out_wexp.at[:, :, pl.ds(pl.multiple_of(y * F, 128), F)]
+        for d in range(N):
             remote(
-                ff_sum.at[0], across(out_wexp, F), k_wexp_out, k_wexp_out,
-                {"section": 1 - s, "ctx": other, "fsdp": owner},
+                ff_sum.at[0], wide, k_wexp_out, k_wexp_out,
+                {"section": 1 - s, "ctx": z * N + near(x, d), "fsdp": x},
             ).start()
+        arrived(ff_sum.at[1], k_third[1])
+        for d in range(N):
             remote(
-                ff_sum.at[1], out_wred.at[mine], k_wred_out, k_wred_out,
-                {"section": 1 - s, "ctx": other},
+                ff_sum.at[1], out_wred.at[z], k_wred_out, k_wred_out,
+                {"section": 1 - s, "ctx": near(z, d) * N + x},
             ).start()
 
-    drains.append(lambda: sent(ff_in.at[rest_ctx], k_ff_pool))
+    for k in range(2):
+        drains.append(lambda k=k: sent(ff_in.at[k, others], k_first[k]))
+        drains.append(lambda k=k: sent(ff_one.at[k, others], k_second[k]))
+        drains.append(lambda k=k: sent(ff_sum.at[k, others], k_third[k]))
     drains.append(lambda: sent(out_wexp, k_wexp_out))
     drains.append(lambda: sent(out_wred, k_wred_out))
 
@@ -475,8 +506,10 @@
     g_rows = g_all[...].reshape(J * M, D)
     gb_rows = gb_all[...].reshape(J * M, F)
     sm_own[10:11] = column_sums(gb_rows)
-    ff_s[:, 1] = mm_tn(active[...].reshape(J * M, F), g_rows).astype(BF16).reshape(NN, F // NN, D)
-    ff_s[:, 0] = mm_tn(n2[...].reshape(J * M, D), gb_rows).astype(BF16).reshape(NN, D // NN, F)
+    ff_s[1] = (
+        mm_tn(active[...].reshape(J * M, F), g_rows).astype(BF16).reshape(N, N, F // NN, D)
+    )
+    ff_s[0] = mm_tn(n2[...].reshape(J * M, D), gb_rows).astype(BF16).reshape(N, N, D // NN, F)
     start(ff_s, ff_in, k_ff_in, sibling)
 
     k_ga = [block_of() for _ in streams]
@@ -681,6 +714,7 @@
     hbm = pl.BlockSpec(memory_space=pl.ANY)
     V = pltpu.VMEM
     slab = V((J, N, Q, D), BF16)
+    whole_sum, part_sum = V((2, N, N, D // NN, D), BF16), V((2, N, D // NN, D), BF16)
     rows_low, rows_full = V((J, Q, D), BF16), V((J, Q, D), F32)
     outs = pl.pallas_call(
         functools.partial(kernel, N, J, Q, D, F),
@@ -691,7 +725,7 @@
             shape((N, D // NN, N * WQ), BF16),
             shape((NN, D // NN, WQ), BF16),
             shape((N, D // NN, N * F), BF16),
-            shape((NN, F // NN, D), BF16),
+            shape((N, N, F // NN, D), BF16),
             shape((24, D), F32),
         ),
         in_specs=[
@@ -711,8 +745,7 @@
             V((J, M, WQ), BF16), V((J, M, WQ), BF16), V((J, M, WQ), BF16), V((J, M, WKV), BF16),
             V((S, N, 2, M, WKV), BF16), V((S, N, 2, M, WKV), BF16),
             V((4, J, N, Q, D), BF16), V((4, J, N, Q, D), BF16), rows_full, rows_full,
-            V((NN, 2, D // NN, D), BF16), V((NN, 2, D // NN, D), BF16),
-            V((NN, 2, D // NN, D), BF16), V((2, D // NN, D), BF16),
+            whole_sum, whole_sum, whole_sum, part_sum, part_sum, part_sum,
             V((NN, D // NN, WKV), BF16), V((NN, D // NN, WKV), BF16), V((D // NN, WKV), BF16),
             V((NN, D // NN, WKV), BF16), V((NN, D // NN, WKV), BF16), V((D // NN, WKV), BF16),
             V((N, 8, D), F32), V((N, 16, D), F32), V((N, 16, D), F32), V((16, D), F32),

time: 259 us -> 244 us (0.942)
  the two profiles are of different devices: /device:TPU:0 before, /device:TPU:24 now
where the time goes in v5:
time: 244 us
  Pallas kernels  229 us (94%)
  local copies, waits for them, and re-layouts  6.92 us (3%)
  other arithmetic  6.88 us (3%)
    pallas_call x1, Pallas kernels, shards(): pl.pallas_call(functools.partial(kernel, N, J, Q, D, F), out_shape=(shape...  229 us

profile of v5, /device:TPU:24, one launch (start us, length us, event | category | flops | bytes accessed | tf_op | source)
XLA Modules:
  0.0 243.6 jit_solution(2261922567823718408)
XLA Ops:
  0.7 0.8 concatenate.57
  1.5 0.6 pad_convert_fusion.rows_in
  2.1 229.1 %layers.1 = (bf16[4,32,768]{2,1,0:T(8,128)(2,1)}, f32[4,32,768]{2,1,0:T(8,128)}, bf16[4,48,1536]{2,1,0:T(8,128)(2,1)}, bf16[4,48,1024]{2,1,0:T(8,128)(2,1)}, bf1...) custom-call(bf16[4,32,768]{2,1,0:T(8,128)(2,1)} %bitcast.60, ...), custom_call_target="tpu_custom_call" | custom-call | tf_op jit(solution)/shard_map/layers/pallas_call | solution.py:719
  231.2 1.5 slice_bitcast_fusion.3
  232.7 0.0 copy-start.4
  232.7 1.2 maximum_convert_fusion.1
  233.9 0.0 copy-start.1
  233.9 0.0 copy-done.4
  233.9 1.0 maximum_convert_fusion
  234.9 1.5 fusion
  236.4 1.3 slice.86
  237.7 0.0 copy-done.1
  237.7 0.0 copy-start
  237.7 1.7 bitcast_convert_fusion
  239.4 0.0 copy-done
  239.4 0.0 copy-start.3
  239.4 1.6 convert.7
  241.0 0.0 copy-done.3
  241.0 0.0 copy-start.5
  241.0 0.2 slice.100
  241.2 0.0 copy-start.2
  241.2 0.2 copy.36
  241.3 0.9 convert_bitcast_fusion
  242.2 0.0 copy-done.5
  242.2 0.7 copy.39
  242.9 0.0 copy-done.2
  242.9 0.7 copy.40
  (1 shorter events, 0.0 us)
Async XLA Ops:
  232.7 1.2 copy-start.4
  233.9 3.8 %copy-start.1 = (bf16[4,48,3072]{2,1,0:T(8,128)(2,1)S(1)}, bf16[4,48,3072]{2,1,0:T(8,128)(2,1)}, u32[]{:S(2)}) copy-start(bf16[4,48,3072]{2,1,0:T(8,128)(2,1)} %get-tuple-element.31) | copy-start | bytes 3538948
  237.7 1.7 copy-start
  239.4 1.6 copy-start.3
  241.0 1.2 copy-start.5
  241.2 1.7 copy-start.2

commit v6 on v5

--- a/solution.py
+++ b/solution.py
@@ -163,21 +163,24 @@
         drains.append(lambda: sent(src.at[others], slot))
 
     barrier = pltpu.get_barrier_semaphore()
-    everyone = 2 * NN * N
-
-    @pl.loop(1, everyone)
+
+    def greet(device):
+        pl.semaphore_signal(barrier, inc=1, device_id=device, device_id_type=MESH)
+
+    @pl.loop(1, NN * N)
     def _(d):
-        index = lax.rem((s * NN + c) * N + y + d, everyone)
-        pl.semaphore_signal(
-            barrier, inc=1,
-            device_id={
-                "section": lax.div(index, NN * N),
-                "ctx": lax.rem(lax.div(index, N), NN),
-                "fsdp": lax.rem(index, N),
-            },
-            device_id_type=MESH,
-        )
-
+        index = lax.rem(c * N + y + d, NN * N)
+        greet({"ctx": lax.div(index, N), "fsdp": lax.rem(index, N)})
+
+    @pl.loop(0, NN)
+    def _(d):
+        greet({"section": 1 - s, "ctx": z * N + lax.rem(d, N), "fsdp": lax.div(d, N)})
+
+    @pl.loop(1, N)
+    def _(d):
+        greet({"section": 1 - s, "ctx": near(z, d) * N + x})
+
+    greeted = NN * N - 1 + NN + N - 1
     wait_cuts = [local(a, b, 13 + j) for j, (a, b) in enumerate(((wq_in, wq), (wk_in, wk), (wv_in, wv)))]
     wait_wred = local(wred_in, wred, 0)
     wait_wout = local(wout_in, wout.at[pl.ds(WQ - DH, DH)], 1)
@@ -207,12 +210,12 @@
         ).astype(BF16)
         w_send[b, :, WKV : WKV + WQ] = mm(wq[:, cut], picker(WQ, shift, 0)).astype(BF16)
     w_all[y] = w_send[y]
-    pl.semaphore_wait(barrier, everyone - 1)
+    pl.semaphore_wait(barrier, greeted)
 
     k_u = [block_of() for _ in streams]
     k_gp = [block_of() for _ in streams]
-    k_cot, k_y, k_dx, k_ff_in, k_wexp_out, k_wred_out = (block_of() for _ in range(6))
-    k_first, k_second, k_third = ([block_of(), block_of()] for _ in range(3))
+    k_cot, k_y, k_dx, k_wexp_out, k_wred_out = (block_of() for _ in range(5))
+    k_ff_in, k_first, k_second, k_third = ([block_of(), block_of()] for _ in range(4))
     k_vecs = block_of()
     spread("y", vecs, k_vecs)
     wait_u = []
@@ -326,7 +329,7 @@
             scores = mm_nt(only(h, pair(q_all, i), 0).astype(BF16), keys)
             scores = jnp.where(allowed, scores, -1e30)
             raised = jnp.exp(scores - jnp.max(scores, axis=-1, keepdims=True))
-            part = raised / jnp.sum(raised, axis=-1, keepdims=True)
+            part = raised * (1.0 / jnp.sum(raised, axis=-1, keepdims=True))
             probs[i * heads + h] = part
             total = total + only(h, mm(part.astype(BF16), values), WQ - DH)
         low = total.astype(BF16)
@@ -433,21 +436,27 @@
         return total.astype(BF16)
 
     def reduce_feed():
-        landed(ff_in, k_ff_in)
-        for k in range(2):
+        for k in (1, 0):
+            landed(ff_in.at[k], k_ff_in[k])
             send_deal(axes[k][0], ff_in.at[k], ff_r.at[k], k_first[k])
-        for k in range(2):
+        for k in (1, 0):
             first, second = axes[k]
             arrived(ff_r.at[k], k_first[k])
             ff_one[k] = total_at(first, ff_in[k, place[first]], ff_r.at[k])
             send_deal(second, ff_one.at[k], ff_two.at[k], k_second[k])
-        for k in range(2):
+        for k in (1, 0):
             second = axes[k][1]
             arrived(ff_two.at[k], k_second[k])
             ff_sum[k, place[second]] = total_at(
                 second, ff_one[k, place[second]], ff_two.at[k]
             )
             send_spread(second, ff_sum.at[k], k_third[k])
+        arrived(ff_sum.at[1], k_third[1])
+        for d in range(N):
+            remote(
+                ff_sum.at[1], out_wred.at[z], k_wred_out, k_wred_out,
+                {"section": 1 - s, "ctx": near(z, d) * N + x},
+            ).start()
         arrived(ff_sum.at[0], k_third[0])
         wide = out_wexp.at[:, :, pl.ds(pl.multiple_of(y * F, 128), F)]
         for d in range(N):
@@ -455,12 +464,6 @@
                 ff_sum.at[0], wide, k_wexp_out, k_wexp_out,
                 {"section": 1 - s, "ctx": z * N + near(x, d), "fsdp": x},
             ).start()
-        arrived(ff_sum.at[1], k_third[1])
-        for d in range(N):
-            remote(
-                ff_sum.at[1], out_wred.at[z], k_wred_out, k_wred_out,
-                {"section": 1 - s, "ctx": near(z, d) * N + x},
-            ).start()
 
     for k in range(2):
         drains.append(lambda k=k: sent(ff_in.at[k, others], k_first[k]))
@@ -505,12 +508,13 @@
 
     g_rows = g_all[...].reshape(J * M, D)
     gb_rows = gb_all[...].reshape(J * M, F)
-    sm_own[10:11] = column_sums(gb_rows)
     ff_s[1] = (
         mm_tn(active[...].reshape(J * M, F), g_rows).astype(BF16).reshape(N, N, F // NN, D)
     )
+    start(ff_s.at[1], ff_in.at[1], k_ff_in[1], sibling)
     ff_s[0] = mm_tn(n2[...].reshape(J * M, D), gb_rows).astype(BF16).reshape(N, N, D // NN, F)
-    start(ff_s, ff_in, k_ff_in, sibling)
+    start(ff_s.at[0], ff_in.at[0], k_ff_in[0], sibling)
+    sm_own[10:11] = column_sums(gb_rows)
 
     k_ga = [block_of() for _ in streams]
     for j in streams:
@@ -628,14 +632,14 @@
     sm_x[x, 8:16] = sm_own[8:16]
     k_smx = block_of()
     spread("x", sm_x, k_smx)
+    kv_sum[...] = pooled(kv_r, k_kv_pool)
+    hand_across(kv_sum, out_kv, WKV, k_kv_out)
     arrived(sm_ly, k_smly)
     sm_lx[x] = total_of(sm_ly)
     k_smlx = block_of()
     spread("x", sm_lx, k_smlx)
     start_if(turned, dx_buf, out_dx, k_dx, partner)
     wait_dx = local_if(straight, dx_buf, out_dx, 9)
-    kv_sum[...] = pooled(kv_r, k_kv_pool)
-    hand_across(kv_sum, out_kv, WKV, k_kv_out)
     arrived(sm_x, k_smx)
     sm_z[z] = total_of(sm_x)
     k_smz = block_of()

time: 244 us -> 235 us (0.963)
  the two profiles are of different devices: /device:TPU:24 before, /device:TPU:0 now
where the time goes in v6:
time: 235 us; the launch traced here: 232 us
  Pallas kernels  217 us (92%)
  local copies, waits for them, and re-layouts  6.93 us (3%)
  other arithmetic  6.88 us (3%)
    pallas_call x1, Pallas kernels, shards(): pl.pallas_call(functools.partial(kernel, N, J, Q, D, F), out_shape=(shape...  217 us

profile of v6, /device:TPU:0, one launch (start us, length us, event | category | flops | bytes accessed | tf_op | source)
XLA Modules:
  0.0 231.6 jit_solution(11045177769181962231)
XLA Ops:
  0.7 0.8 concatenate.57
  1.5 0.6 pad_convert_fusion.rows_in
  2.1 217.0 %layers.1 = (bf16[4,32,768]{2,1,0:T(8,128)(2,1)}, f32[4,32,768]{2,1,0:T(8,128)}, bf16[4,48,1536]{2,1,0:T(8,128)(2,1)}, bf16[4,48,1024]{2,1,0:T(8,128)(2,1)}, bf1...) custom-call(bf16[4,32,768]{2,1,0:T(8,128)(2,1)} %bitcast.60, ...), custom_call_target="tpu_custom_call" | custom-call | tf_op jit(solution)/shard_map/layers/pallas_call | solution.py:723
  219.1 1.5 slice_bitcast_fusion.3
  220.6 0.0 copy-start.4
  220.6 1.2 maximum_convert_fusion.1
  221.8 0.0 copy-start.1
  221.8 0.0 copy-done.4
  221.9 1.0 maximum_convert_fusion
  222.8 1.5 fusion
  224.3 1.3 slice.86
  225.7 0.0 copy-done.1
  225.7 0.0 copy-start
  225.7 1.7 bitcast_convert_fusion
  227.3 0.0 copy-done
  227.3 0.0 copy-start.3
  227.3 1.6 convert.7
  228.9 0.0 copy-done.3
  228.9 0.0 copy-start.5
  228.9 0.2 slice.100
  229.1 0.0 copy-start.2
  229.1 0.2 copy.36
  229.3 0.9 convert_bitcast_fusion
  230.1 0.0 copy-done.5
  230.1 0.7 copy.39
  230.8 0.0 copy-done.2
  230.8 0.7 copy.40
  (1 shorter events, 0.0 us)
Async XLA Ops:
  220.6 1.2 copy-start.4
  221.8 3.8 %copy-start.1 = (bf16[4,48,3072]{2,1,0:T(8,128)(2,1)S(1)}, bf16[4,48,3072]{2,1,0:T(8,128)(2,1)}, u32[]{:S(2)}) copy-start(bf16[4,48,3072]{2,1,0:T(8,128)(2,1)} %get-tuple-element.31) | copy-start | bytes 3538948
  225.7 1.7 copy-start
  227.3 1.6 copy-start.3
  228.9 1.2 copy-start.5
  229.1 1.7 copy-start.2

commit v7 on v6

--- a/solution.py
+++ b/solution.py
@@ -280,10 +280,6 @@
         query = mm(rows, w_all[:, :, WKV : WKV + WQ].reshape(D, WQ)) + b_query
         q_all[j] = (query * 0.125).astype(BF16)
 
-    @pl.when(s == 0)
-    def _():
-        pl.semaphore_signal(go, inc=1, device_id=sibling, device_id_type=MESH)
-
     k_wexp = block_of()
 
     def wexp_cut(b):
@@ -337,6 +333,10 @@
         term = mm(low, wout[...])
         for side in range(2):
             scatter(0, 2 * i + side, term[side * M : (side + 1) * M], k_po[2 * i + side])
+
+    @pl.when(s == 0)
+    def _():
+        pl.semaphore_signal(go, inc=1, device_id=sibling, device_id_type=MESH)
 
     k_n2 = [block_of() for _ in streams]
     for j in streams:
@@ -596,7 +596,6 @@
     @pl.when(s == 0)
     def _():
         pool(kv_s, kv_r, k_kv_pool)
-        reduce_qo()
 
     sm_y[y] = sm_own[0:8]
     k_smy = block_of()
@@ -649,10 +648,8 @@
     k_smlz = block_of()
     spread("z", sm_lz, k_smlz)
 
-    @pl.when(s == 1)
-    def _():
-        reduce_qo()
-        reduce_feed()
+    reduce_qo()
+    pl.when(s == 1)(reduce_feed)
 
     arrived(sm_z, k_smz)
     arrived(sm_lz, k_smlz)

time: 235 us -> 241 us (1.026)
  Pallas kernels: 217 us -> 223 us
    pallas_call x1, Pallas kernels: 217 us -> 223 us  [shards(): pl.pallas_call(functools.partial(kernel, N, J, Q, D, F), out_shape=(shape...]
where the time goes in v7:
time: 241 us; the launch traced here: 238 us
  Pallas kernels  223 us (93%)
  local copies, waits for them, and re-layouts  6.93 us (3%)
  other arithmetic  6.88 us (3%)
    pallas_call x1, Pallas kernels, shards(): pl.pallas_call(functools.partial(kernel, N, J, Q, D, F), out_shape=(shape...  223 us

profile of v7, /device:TPU:0, one launch (start us, length us, event | category | flops | bytes accessed | tf_op | source)
XLA Modules:
  0.0 237.5 jit_solution(3008861903129954688)
XLA Ops:
  0.7 0.8 concatenate.57
  1.5 0.6 pad_convert_fusion.rows_in
  2.1 223.0 %layers.1 = (bf16[4,32,768]{2,1,0:T(8,128)(2,1)}, f32[4,32,768]{2,1,0:T(8,128)}, bf16[4,48,1536]{2,1,0:T(8,128)(2,1)}, bf16[4,48,1024]{2,1,0:T(8,128)(2,1)}, bf1...) custom-call(bf16[4,32,768]{2,1,0:T(8,128)(2,1)} %bitcast.60, ...), custom_call_target="tpu_custom_call" | custom-call | tf_op jit(solution)/shard_map/layers/pallas_call | solution.py:720
  225.1 1.5 slice_bitcast_fusion.3
  226.5 0.0 copy-start.4
  226.6 1.2 maximum_convert_fusion.1
  227.8 0.0 copy-start.1
  227.8 0.0 copy-done.4
  227.8 1.0 maximum_convert_fusion
  228.8 1.5 fusion
  230.3 1.3 slice.86
  231.6 0.0 copy-done.1
  231.6 0.0 copy-start
  231.6 1.7 bitcast_convert_fusion
  233.3 0.0 copy-done
  233.3 0.0 copy-start.3
  233.3 1.6 convert.7
  234.9 0.0 copy-done.3
  234.9 0.0 copy-start.5
  234.9 0.2 slice.100
  235.1 0.0 copy-start.2
  235.1 0.2 copy.36
  235.2 0.9 convert_bitcast_fusion
  236.1 0.0 copy-done.5
  236.1 0.7 copy.39
  236.8 0.0 copy-done.2
  236.8 0.7 copy.40
  (1 shorter events, 0.0 us)
Async XLA Ops:
  226.5 1.2 copy-start.4
  227.8 3.8 %copy-start.1 = (bf16[4,48,3072]{2,1,0:T(8,128)(2,1)S(1)}, bf16[4,48,3072]{2,1,0:T(8,128)(2,1)}, u32[]{:S(2)}) copy-start(bf16[4,48,3072]{2,1,0:T(8,128)(2,1)} %get-tuple-element.31) | copy-start | bytes 3538948
  231.6 1.7 copy-start
  233.3 1.6 copy-start.3
  234.9 1.2 copy-start.5
  235.1 1.7 copy-start.2
